TPU v7x, 32 devices: a whole 2x2x4 slice. The times are simulated.
32 devices in a mesh: tgt: 8 (over z, y), mem: 4 (over x, core).
Axes of the slice: x: 2, y: 2, z: 4, core: 2. Of those that a mesh axis runs over, the one named last changes fastest.
Arguments:
- target: bfloat16 [64, 189, 1472], P(('tgt', 'mem')), may hold values from -6 to 6
- memory: bfloat16 [64, 1024, 1472], P('tgt', 'mem'), may hold values from -6 to 6
- lengths: int32 [64], P('tgt'), may hold values from 200 to 1024, as said below
- gate_bias: float32 [64, 1024], P('tgt', 'mem'), may hold values from -3 to 0
- out_grad: bfloat16 [64, 189, 1472], P(('tgt', 'mem')), may hold values from -6 to 6
- gain_self: bfloat16 [1472], replicated, may hold values from 0.5 to 1.5
- gain_cross: bfloat16 [1472], replicated, may hold values from 0.5 to 1.5
- gain_ffn: bfloat16 [1472], replicated, may hold values from 0.5 to 1.5
- rel_table: float32 [32, 6], replicated, may hold values from -4 to 4
- self_q: bfloat16 [1472, 384], P('tgt'), may hold values from -0.0390625 to 0.0390625
- self_k: bfloat16 [1472, 384], P('tgt'), may hold values from -0.15625 to 0.15625
- self_v: bfloat16 [1472, 384], P('tgt'), may hold values from -0.15625 to 0.15625
- self_o: bfloat16 [384, 1472], P('tgt'), may hold values from -1.75 to 1.75
- cross_q: bfloat16 [1472, 384], P('tgt'), may hold values from -0.0390625 to 0.0390625
- cross_k: bfloat16 [1472, 384], P('tgt'), may hold values from -0.15625 to 0.15625
- cross_v: bfloat16 [1472, 384], P('tgt'), may hold values from -0.15625 to 0.15625
- cross_o: bfloat16 [384, 1472], P('tgt'), may hold values from -3.5 to 3.5
- ffn_gate: bfloat16 [1472, 3584], P('tgt'), may hold values from -0.15625 to 0.15625
- ffn_up: bfloat16 [1472, 3584], P('tgt'), may hold values from -0.15625 to 0.15625
- ffn_down: bfloat16 [3584, 1472], P('tgt'), may hold values from -0.09375 to 0.09375
Outputs:
- layer_out: bfloat16 [64, 189, 1472], P(('tgt', 'mem'))
- target_grad: bfloat16 [64, 189, 1472], P(('tgt', 'mem'))
- memory_grad: bfloat16 [64, 1024, 1472], P('tgt', 'mem')
- gain_self_grad: float32 [1472], replicated
- gain_cross_grad: float32 [1472], replicated
- gain_ffn_grad: float32 [1472], replicated
- rel_table_grad: float32 [32, 6], replicated
- self_q_grad: float32 [1472, 384], P('tgt')
- self_k_grad: float32 [1472, 384], P('tgt')
- self_v_grad: float32 [1472, 384], P('tgt')
- self_o_grad: float32 [384, 1472], P('tgt')
- cross_q_grad: float32 [1472, 384], P('tgt')
- cross_k_grad: float32 [1472, 384], P('tgt')
- cross_v_grad: float32 [1472, 384], P('tgt')
- cross_o_grad: float32 [384, 1472], P('tgt')
- ffn_gate_grad: float32 [1472, 3584], P('tgt')
- ffn_up_grad: float32 [1472, 3584], P('tgt')
- ffn_down_grad: float32 [3584, 1472], P('tgt')
Inputs may be any that keep to these rules, and one draw needn't show every extreme that they name: `lengths`: each item's true encoder length; some item has exactly 1024.
All inputs are finite; a program needn't handle non-finite values.
Results may differ from a plain program's by a relative error of at most 0.025.
The roundings to bfloat16 on the way count: a program that leaves them out, or rounds other values in their place, can miss the bound.
Values may be sent and summed in bfloat16 or wider, within the bound.
A program may use at most 448 MiB of HBM per device.

v0:
```python
import jax
import jax.numpy as jnp
import numpy as np
from jax import lax
from jax.sharding import PartitionSpec as P

HEADS = 6
HEAD = 64
BUCKETS = 32
MAX_DIST = 128
TGT_LEN = 189
MICRO = 2


EPS = 1e-06
NEG = -1e30
HIGH = lax.Precision.HIGHEST


def joined(value, axis, join):
    pieces = jax.tree.map(lambda part: lax.all_gather(part, axis), value)
    head = jax.tree.map(lambda part: part[0], pieces)
    tail = jax.tree.map(lambda part: part[1:], pieces)
    so_far, _ = lax.scan(lambda so_far, section: (join(so_far, section), None), head, tail)
    return so_far


def bucket_onehot():
    places = np.arange(TGT_LEN)
    distance = np.maximum(places[:, None] - places[None, :], 0)
    exact_max = BUCKETS // 2
    scaled = (
        np.log(np.maximum(distance, 1) / exact_max)
        / np.log(MAX_DIST / exact_max)
        * (BUCKETS - exact_max)
    )
    far_bucket = np.minimum(
        exact_max + np.floor(np.maximum(scaled, 0.0)).astype(np.int64), BUCKETS - 1
    )
    bucket = np.where(distance < exact_max, distance, far_bucket)
    return (bucket.reshape(-1)[:, None] == np.arange(BUCKETS)[None, :]).astype(np.float32)


def rms_norm(inputs, gain_vec):
    scaled = lax.rsqrt(jnp.mean(inputs * inputs, axis=-1, keepdims=True) + EPS)
    return inputs * scaled * gain_vec


def norm_back(inputs, gain_vec, upstream):
    normed_out, pullback = jax.vjp(rms_norm, inputs, gain_vec)
    return pullback(upstream)


def matmul(left, right):
    return jnp.dot(left, right, preferred_element_type=jnp.float32)


def weight_grad(left, right):
    return lax.dot_general(
        left.reshape(-1, left.shape[-1]),
        right.reshape(-1, right.shape[-1]),
        (((0,), (0,)), ((), ())),
        preferred_element_type=jnp.float32,
    )


def input_grad(upstream, weight):
    return lax.dot_general(
        upstream,
        weight,
        (((upstream.ndim - 1,), (1,)), ((), ())),
        preferred_element_type=jnp.float32,
    )


def softmax_merge(earlier, later):
    highest = jnp.maximum(earlier[0], later[0])
    return (
        highest,
        earlier[1] * jnp.exp(earlier[0] - highest) + later[1] * jnp.exp(later[0] - highest),
    )


def reduce_grads(grads):
    shard_sums = (
        lax.psum_scatter(grads[0], "tgt", scatter_dimension=0, tiled=True),
        lax.psum_scatter(grads[1], "tgt", scatter_dimension=0, tiled=True),
        lax.psum_scatter(grads[2], "tgt", scatter_dimension=0, tiled=True),
        lax.psum_scatter(grads[3], "tgt", scatter_dimension=0, tiled=True),
        lax.psum_scatter(grads[4], "tgt", scatter_dimension=0, tiled=True),
        lax.psum_scatter(grads[5], "tgt", scatter_dimension=0, tiled=True),
        lax.psum_scatter(grads[6], "tgt", scatter_dimension=0, tiled=True),
        lax.psum_scatter(grads[7], "tgt", scatter_dimension=0, tiled=True),
        lax.psum_scatter(grads[8], "tgt", scatter_dimension=0, tiled=True),
        lax.psum_scatter(grads[9], "tgt", scatter_dimension=0, tiled=True),
        lax.psum_scatter(grads[10], "tgt", scatter_dimension=0, tiled=True),
    )
    column_sums = (
        lax.psum_scatter(
            shard_sums[0].astype(jnp.bfloat16), "mem", scatter_dimension=1, tiled=True
        ).astype(jnp.float32),
        lax.psum_scatter(
            shard_sums[1].astype(jnp.bfloat16), "mem", scatter_dimension=1, tiled=True
        ).astype(jnp.float32),
        lax.psum_scatter(
            shard_sums[2].astype(jnp.bfloat16), "mem", scatter_dimension=1, tiled=True
        ).astype(jnp.float32),
        lax.psum_scatter(
            shard_sums[3].astype(jnp.bfloat16), "mem", scatter_dimension=1, tiled=True
        ).astype(jnp.float32),
        lax.psum_scatter(
            shard_sums[4].astype(jnp.bfloat16), "mem", scatter_dimension=1, tiled=True
        ).astype(jnp.float32),
        lax.psum_scatter(
            shard_sums[5].astype(jnp.bfloat16), "mem", scatter_dimension=1, tiled=True
        ).astype(jnp.float32),
        lax.psum_scatter(
            shard_sums[6].astype(jnp.bfloat16), "mem", scatter_dimension=1, tiled=True
        ).astype(jnp.float32),
        lax.psum_scatter(
            shard_sums[7].astype(jnp.bfloat16), "mem", scatter_dimension=1, tiled=True
        ).astype(jnp.float32),
        lax.psum_scatter(
            shard_sums[8].astype(jnp.bfloat16), "mem", scatter_dimension=1, tiled=True
        ).astype(jnp.float32),
        lax.psum_scatter(
            shard_sums[9].astype(jnp.bfloat16), "mem", scatter_dimension=1, tiled=True
        ).astype(jnp.float32),
        lax.psum_scatter(
            shard_sums[10].astype(jnp.bfloat16), "mem", scatter_dimension=1, tiled=True
        ).astype(jnp.float32),
    )
    return (
        lax.all_gather(column_sums[0].astype(jnp.bfloat16), "mem", axis=1, tiled=True).astype(
            jnp.float32
        ),
        lax.all_gather(column_sums[1].astype(jnp.bfloat16), "mem", axis=1, tiled=True).astype(
            jnp.float32
        ),
        lax.all_gather(column_sums[2].astype(jnp.bfloat16), "mem", axis=1, tiled=True).astype(
            jnp.float32
        ),
        lax.all_gather(column_sums[3].astype(jnp.bfloat16), "mem", axis=1, tiled=True).astype(
            jnp.float32
        ),
        lax.all_gather(column_sums[4].astype(jnp.bfloat16), "mem", axis=1, tiled=True).astype(
            jnp.float32
        ),
        lax.all_gather(column_sums[5].astype(jnp.bfloat16), "mem", axis=1, tiled=True).astype(
            jnp.float32
        ),
        lax.all_gather(column_sums[6].astype(jnp.bfloat16), "mem", axis=1, tiled=True).astype(
            jnp.float32
        ),
        lax.all_gather(column_sums[7].astype(jnp.bfloat16), "mem", axis=1, tiled=True).astype(
            jnp.float32
        ),
        lax.all_gather(column_sums[8].astype(jnp.bfloat16), "mem", axis=1, tiled=True).astype(
            jnp.float32
        ),
        lax.all_gather(column_sums[9].astype(jnp.bfloat16), "mem", axis=1, tiled=True).astype(
            jnp.float32
        ),
        lax.all_gather(column_sums[10].astype(jnp.bfloat16), "mem", axis=1, tiled=True).astype(
            jnp.float32
        ),
    )


def add_trees(first_tree, second_tree):
    if first_tree is None:
        return second_tree
    return jax.tree.map(jnp.add, first_tree, second_tree)


def on_device(
    target,
    memory,
    lengths,
    gate_bias,
    out_grad,
    gain_self,
    gain_cross,
    gain_ffn,
    rel_table,
    self_q,
    self_k,
    self_v,
    self_o,
    cross_q,
    cross_k,
    cross_v,
    cross_o,
    ffn_gate,
    ffn_up,
    ffn_down,
):
    groups_mem = lax.axis_size("mem")
    mem_index = lax.axis_index("mem")
    items_dev = target.shape[0]
    seq_len = target.shape[1]
    model_dim = target.shape[2]
    mem_dev = memory.shape[1]
    per_section = items_dev // MICRO
    inner_dim = HEADS * HEAD
    rows_cross = groups_mem * per_section
    norm_self = gain_self.astype(jnp.float32)
    norm_cross = gain_cross.astype(jnp.float32)
    norm_ffn = gain_ffn.astype(jnp.float32)
    onehot = jnp.asarray(bucket_onehot())
    rel_bias = (
        jnp.dot(onehot, rel_table, precision=HIGH)
        .reshape(seq_len, seq_len, HEADS)
        .transpose(2, 0, 1)
    )
    causal = jnp.arange(seq_len)[:, None] >= jnp.arange(seq_len)[None, :]
    positions = mem_index * mem_dev + jnp.arange(mem_dev)
    memory_view = memory.reshape(groups_mem, items_dev, mem_dev, model_dim)
    bias_view = gate_bias.reshape(groups_mem, items_dev, mem_dev)
    length_view = lengths.reshape(groups_mem, items_dev)
    outputs_list = []
    target_grads = []
    memory_grads = []
    summed = None
    small_sum = None
    for micro_step in range(MICRO):
        start_row = micro_step * per_section
        stop_row = start_row + per_section
        inputs = target[start_row:stop_row].astype(jnp.float32)
        mem_now = memory_view[:, start_row:stop_row].reshape(rows_cross, mem_dev, model_dim)
        bias_now = bias_view[:, start_row:stop_row].reshape(rows_cross, mem_dev)
        len_now = length_view[:, start_row:stop_row].reshape(rows_cross)
        gathered = (
            lax.all_gather(self_q, "tgt", axis=0, tiled=True),
            lax.all_gather(self_k, "tgt", axis=0, tiled=True),
            lax.all_gather(self_v, "tgt", axis=0, tiled=True),
            lax.all_gather(self_o, "tgt", axis=0, tiled=True),
            lax.all_gather(cross_q, "tgt", axis=0, tiled=True),
            lax.all_gather(cross_k, "tgt", axis=0, tiled=True),
            lax.all_gather(cross_v, "tgt", axis=0, tiled=True),
            lax.all_gather(cross_o, "tgt", axis=0, tiled=True),
            lax.all_gather(ffn_gate, "tgt", axis=0, tiled=True),
            lax.all_gather(ffn_up, "tgt", axis=0, tiled=True),
            lax.all_gather(ffn_down, "tgt", axis=0, tiled=True),
        )
        (
            self_q_all,
            self_k_all,
            self_v_all,
            self_o_all,
            cross_q_all,
            cross_k_all,
            cross_v_all,
            cross_o_all,
            gate_all,
            up_all,
            down_all,
        ) = gathered
        normed = rms_norm(inputs, norm_self).astype(jnp.bfloat16)
        query_heads = (
            matmul(normed, self_q_all)
            .astype(jnp.bfloat16)
            .reshape(per_section, seq_len, HEADS, HEAD)
        )
        key_heads = (
            matmul(normed, self_k_all)
            .astype(jnp.bfloat16)
            .reshape(per_section, seq_len, HEADS, HEAD)
        )
        value_heads = (
            matmul(normed, self_v_all)
            .astype(jnp.bfloat16)
            .reshape(per_section, seq_len, HEADS, HEAD)
        )
        self_scores = (
            jnp.einsum(
                "nihc,njhc->nhij", query_heads, key_heads, preferred_element_type=jnp.float32
            )
            + rel_bias[None]
        )
        self_scores = jnp.where(causal[None, None], self_scores, NEG)
        self_probs = jax.nn.softmax(self_scores, axis=-1)
        self_low = self_probs.astype(jnp.bfloat16)
        attended = (
            jnp.einsum("nhij,njhc->nihc", self_low, value_heads, preferred_element_type=jnp.float32)
            .reshape(per_section, seq_len, inner_dim)
            .astype(jnp.bfloat16)
        )
        after_self = inputs + matmul(attended, self_o_all)
        normed_cross = rms_norm(after_self, norm_cross).astype(jnp.bfloat16)
        own_queries = matmul(normed_cross, cross_q_all).astype(jnp.bfloat16)
        all_queries = lax.all_gather(own_queries, "mem", axis=0, tiled=True)
        query_rows = all_queries.reshape(rows_cross, seq_len, HEADS, HEAD)
        mem_keys = matmul(mem_now, cross_k_all).astype(jnp.bfloat16)
        mem_values = matmul(mem_now, cross_v_all).astype(jnp.bfloat16)
        key_rows = mem_keys.reshape(rows_cross, mem_dev, HEADS, HEAD)
        value_rows = mem_values.reshape(rows_cross, mem_dev, HEADS, HEAD)
        mem_mask = (positions[None, :] < len_now[:, None])[:, None, None, :]
        cross_scores = (
            jnp.einsum("nihc,njhc->nhij", query_rows, key_rows, preferred_element_type=jnp.float32)
            + bias_now[:, None, None, :]
        )
        cross_scores = jnp.where(mem_mask, cross_scores, NEG)
        local_max = jnp.max(cross_scores, axis=-1)
        local_sum = jnp.sum(
            jnp.where(mem_mask, jnp.exp(cross_scores - local_max[..., None]), 0.0), axis=-1
        )
        row_max, row_sum = joined((local_max, local_sum), "mem", softmax_merge)
        cross_probs = (
            jnp.where(mem_mask, jnp.exp(cross_scores - row_max[..., None]), 0.0)
            / row_sum[..., None]
        )
        cross_low = cross_probs.astype(jnp.bfloat16)
        partial_out = jnp.einsum(
            "nhij,njhc->nihc", cross_low, value_rows, preferred_element_type=jnp.float32
        ).reshape(rows_cross, seq_len, inner_dim)
        cross_att = lax.psum_scatter(partial_out, "mem", scatter_dimension=0, tiled=True).astype(
            jnp.bfloat16
        )
        after_cross = after_self + matmul(cross_att, cross_o_all)
        normed_ffn = rms_norm(after_cross, norm_ffn).astype(jnp.bfloat16)
        gate_pre = matmul(normed_ffn, gate_all)
        up_pre = matmul(normed_ffn, up_all)
        hidden = (jax.nn.gelu(gate_pre, approximate=True) * up_pre).astype(jnp.bfloat16)
        layer_out = after_cross + matmul(hidden, down_all)
        outputs_list.append(layer_out.astype(jnp.bfloat16))
        gathered = (
            lax.all_gather(self_q, "tgt", axis=0, tiled=True),
            lax.all_gather(self_k, "tgt", axis=0, tiled=True),
            lax.all_gather(self_v, "tgt", axis=0, tiled=True),
            lax.all_gather(self_o, "tgt", axis=0, tiled=True),
            lax.all_gather(cross_q, "tgt", axis=0, tiled=True),
            lax.all_gather(cross_k, "tgt", axis=0, tiled=True),
            lax.all_gather(cross_v, "tgt", axis=0, tiled=True),
            lax.all_gather(cross_o, "tgt", axis=0, tiled=True),
            lax.all_gather(ffn_gate, "tgt", axis=0, tiled=True),
            lax.all_gather(ffn_up, "tgt", axis=0, tiled=True),
            lax.all_gather(ffn_down, "tgt", axis=0, tiled=True),
        )
        (
            self_q_all,
            self_k_all,
            self_v_all,
            self_o_all,
            cross_q_all,
            cross_k_all,
            cross_v_all,
            cross_o_all,
            gate_all,
            up_all,
            down_all,
        ) = gathered
        down_in = out_grad[start_row:stop_row]
        upstream = down_in.astype(jnp.float32)
        grad_down = weight_grad(hidden, down_in)
        hidden_back = input_grad(down_in, down_all).astype(jnp.bfloat16)

        def gated(gate_in, up_in):
            return jax.nn.gelu(gate_in, approximate=True) * up_in

        gated_out, gate_pull = jax.vjp(gated, gate_pre, up_pre)
        gate_back, up_back = gate_pull(hidden_back.astype(jnp.float32))
        gate_back = gate_back.astype(jnp.bfloat16)
        up_back = up_back.astype(jnp.bfloat16)
        grad_gate = weight_grad(normed_ffn, gate_back)
        grad_up = weight_grad(normed_ffn, up_back)
        ffn_in_back = input_grad(gate_back, gate_all) + input_grad(up_back, up_all)
        cross_res_back, grad_norm_ffn = norm_back(after_cross, norm_ffn, ffn_in_back)
        after_cross_back = upstream + cross_res_back
        cross_branch = after_cross_back.astype(jnp.bfloat16)
        grad_cross_o = weight_grad(cross_att, cross_branch)
        att_back = input_grad(cross_branch, cross_o_all).astype(jnp.bfloat16)
        all_att_back = lax.all_gather(att_back, "mem", axis=0, tiled=True)
        back_rows = all_att_back.reshape(rows_cross, seq_len, HEADS, HEAD)
        cross_dprob = jnp.einsum(
            "nihc,njhc->nhij", back_rows, value_rows, preferred_element_type=jnp.float32
        )
        partial_delta = jnp.sum(cross_probs * cross_dprob, axis=-1)
        row_delta = lax.psum(partial_delta, "mem")
        cross_dscore = (cross_probs * (cross_dprob - row_delta[..., None])).astype(jnp.bfloat16)
        values_back = (
            jnp.einsum("nhij,nihc->njhc", cross_low, back_rows, preferred_element_type=jnp.float32)
            .reshape(rows_cross, mem_dev, inner_dim)
            .astype(jnp.bfloat16)
        )
        keys_back = (
            jnp.einsum(
                "nhij,nihc->njhc", cross_dscore, query_rows, preferred_element_type=jnp.float32
            )
            .reshape(rows_cross, mem_dev, inner_dim)
            .astype(jnp.bfloat16)
        )
        query_part = jnp.einsum(
            "nhij,njhc->nihc", cross_dscore, key_rows, preferred_element_type=jnp.float32
        ).reshape(rows_cross, seq_len, inner_dim)
        query_back = lax.psum_scatter(query_part, "mem", scatter_dimension=0, tiled=True).astype(
            jnp.bfloat16
        )
        grad_cross_k = weight_grad(mem_now, keys_back)
        grad_cross_v = weight_grad(mem_now, values_back)
        memory_back = input_grad(keys_back, cross_k_all) + input_grad(values_back, cross_v_all)
        memory_grads.append(
            memory_back.astype(jnp.bfloat16).reshape(groups_mem, per_section, mem_dev, model_dim)
        )
        grad_cross_q = weight_grad(normed_cross, query_back)
        normed_cross_back = input_grad(query_back, cross_q_all)
        self_res_back, grad_norm_cross = norm_back(after_self, norm_cross, normed_cross_back)
        after_self_back = after_cross_back + self_res_back
        self_branch = after_self_back.astype(jnp.bfloat16)
        grad_self_o = weight_grad(attended, self_branch)
        self_att_back = (
            input_grad(self_branch, self_o_all)
            .astype(jnp.bfloat16)
            .reshape(per_section, seq_len, HEADS, HEAD)
        )
        self_dprob = jnp.einsum(
            "nihc,njhc->nhij", self_att_back, value_heads, preferred_element_type=jnp.float32
        )
        self_delta = jnp.sum(self_probs * self_dprob, axis=-1, keepdims=True)
        self_dscore = self_probs * (self_dprob - self_delta)
        table_part = jnp.dot(
            onehot.T,
            jnp.sum(self_dscore, axis=0).transpose(1, 2, 0).reshape(seq_len * seq_len, HEADS),
            precision=HIGH,
        )
        dscore_low = self_dscore.astype(jnp.bfloat16)
        q_back = (
            jnp.einsum("nhij,njhc->nihc", dscore_low, key_heads, preferred_element_type=jnp.float32)
            .reshape(per_section, seq_len, inner_dim)
            .astype(jnp.bfloat16)
        )
        k_back = (
            jnp.einsum(
                "nhij,nihc->njhc", dscore_low, query_heads, preferred_element_type=jnp.float32
            )
            .reshape(per_section, seq_len, inner_dim)
            .astype(jnp.bfloat16)
        )
        v_back = (
            jnp.einsum(
                "nhij,nihc->njhc", self_low, self_att_back, preferred_element_type=jnp.float32
            )
            .reshape(per_section, seq_len, inner_dim)
            .astype(jnp.bfloat16)
        )
        grad_self_q = weight_grad(normed, q_back)
        grad_self_k = weight_grad(normed, k_back)
        grad_self_v = weight_grad(normed, v_back)
        normed_back = (
            input_grad(q_back, self_q_all)
            + input_grad(k_back, self_k_all)
            + input_grad(v_back, self_v_all)
        )
        input_back, grad_norm_self = norm_back(inputs, norm_self, normed_back)
        target_grads.append((after_self_back + input_back).astype(jnp.bfloat16))
        section_grads = (
            grad_self_q,
            grad_self_k,
            grad_self_v,
            grad_self_o,
            grad_cross_q,
            grad_cross_k,
            grad_cross_v,
            grad_cross_o,
            grad_gate,
            grad_up,
            grad_down,
        )
        small_sum = add_trees(
            small_sum, (grad_norm_self, grad_norm_cross, grad_norm_ffn, table_part)
        )
        summed = add_trees(summed, reduce_grads(section_grads))
    small_total = lax.psum((small_sum[0], small_sum[1], small_sum[2], small_sum[3]), ("tgt", "mem"))
    layer_all = jnp.concatenate(outputs_list, axis=0)
    target_all = jnp.concatenate(target_grads, axis=0)
    memory_all = jnp.concatenate(memory_grads, axis=1).reshape(
        groups_mem * items_dev, mem_dev, model_dim
    )
    return (
        layer_all,
        target_all,
        memory_all,
        small_total[0],
        small_total[1],
        small_total[2],
        small_total[3],
        summed[0],
        summed[1],
        summed[2],
        summed[3],
        summed[4],
        summed[5],
        summed[6],
        summed[7],
        summed[8],
        summed[9],
        summed[10],
    )


def solution(mesh):
    return jax.shard_map(
        on_device,
        mesh=mesh,
        in_specs=(
            P(("tgt", "mem"), None, None),
            P("tgt", "mem", None),
            P("tgt"),
            P("tgt", "mem"),
            P(("tgt", "mem"), None, None),
            P(),
            P(),
            P(),
            P(),
            P("tgt", None),
            P("tgt", None),
            P("tgt", None),
            P("tgt", None),
            P("tgt", None),
            P("tgt", None),
            P("tgt", None),
            P("tgt", None),
            P("tgt", None),
            P("tgt", None),
            P("tgt", None),
        ),
        out_specs=(
            P(("tgt", "mem"), None, None),
            P(("tgt", "mem"), None, None),
            P("tgt", "mem", None),
            P(),
            P(),
            P(),
            P(),
            P("tgt", None),
            P("tgt", None),
            P("tgt", None),
            P("tgt", None),
            P("tgt", None),
            P("tgt", None),
            P("tgt", None),
            P("tgt", None),
            P("tgt", None),
            P("tgt", None),
            P("tgt", None),
        ),
        check_vma=False,
    )
```

profile of v0, /device:TPU:0, one launch (start us, length us, event | category | flops | bytes accessed | tf_op | source)
XLA Modules:
  0.0 4995.1 jit_solution(5037040308933738661)
XLA Ops:
  25.3 28.4 all-gather.48.cloned.1.call-done
  55.7 39.8 all-gather.50.cloned.1.call-done
  97.4 39.8 all-gather.52.cloned.1.call-done
  148.6 30.7 all-gather.54.cloned.1.call-done
  181.2 39.6 all-gather.58.cloned.1.call-done
  231.6 30.9 all-gather.60.cloned.1.call-done
  411.2 150.6 %all-gather.64.cloned.1.call-done = bf16[1472,3584]{1,0:T(8,128)(2,1)} async-done(((bf16[184,3584]{1,0:T(8,128)(2,1)}), bf16[1472,3584]{1,0:T(8,128)(2,1)}) %all-gather.64.cloned.1.call-update) | async-done | bytes 10551312 | tf_op jit(solution)/shard_map/all_gather | solution.py:242
  569.6 144.0 %all-gather.66.cloned.1.call-done = bf16[1472,3584]{1,0:T(8,128)(2,1)} async-done(((bf16[184,3584]{1,0:T(8,128)(2,1)}), bf16[1472,3584]{1,0:T(8,128)(2,1)}) %all-gather.66.cloned.1.call-update) | async-done | bytes 10551312 | tf_op jit(solution)/shard_map/all_gather | solution.py:243
  721.5 149.8 %all-gather.68.cloned.1.call-done = bf16[3584,1472]{1,0:T(8,128)(2,1)} async-done(((bf16[448,1472]{1,0:T(8,128)(2,1)}), bf16[3584,1472]{1,0:T(8,128)(2,1)}) %all-gather.68.cloned.1.call-update) | async-done | bytes 10551312 | tf_op jit(solution)/shard_map/all_gather | solution.py:244
  1180.5 225.6 %reduce-scatter.143.cloned.1.call-done = f32[448,1472]{1,0:T(8,128)} async-done(((f32[3584,1472]{1,0:T(8,128)}), f32[448,1472]{1,0:T(8,128)}) %reduce-scatter.143.cloned.1.call-update) | async-done | bytes 2637840 | tf_op jit(solution)/shard_map/reduce_scatter | solution.py:96
  1409.8 358.2 %reduce-scatter.141.cloned.1.call-done = f32[448,1472]{1,0:T(8,128)} async-done(((f32[3584,1472]{1,0:T(8,128)}), f32[448,1472]{1,0:T(8,128)}) %reduce-scatter.141.cloned.1.call-update) | async-done | bytes 2637840 | tf_op jit(solution)/shard_map/reduce_scatter | solution.py:96
  1771.7 345.5 %reduce-scatter.135.cloned.1.call-done = f32[184,3584]{1,0:T(8,128)} async-done(((f32[1472,3584]{1,0:T(8,128)}), f32[184,3584]{1,0:T(8,128)}) %reduce-scatter.135.cloned.1.call-update) | async-done | bytes 2637840 | tf_op jit(solution)/shard_map/reduce_scatter | solution.py:94
  2121.9 345.2 %reduce-scatter.133.cloned.1.call-done = f32[184,3584]{1,0:T(8,128)} async-done(((f32[1472,3584]{1,0:T(8,128)}), f32[184,3584]{1,0:T(8,128)}) %reduce-scatter.133.cloned.1.call-update) | async-done | bytes 2637840 | tf_op jit(solution)/shard_map/reduce_scatter | solution.py:94
  2471.4 66.7 %reduce-scatter.207.cloned.1.call-done = f32[184,384]{1,0:T(8,128)} async-done(((f32[1472,384]{1,0:T(8,128)}), f32[184,384]{1,0:T(8,128)}) %reduce-scatter.207.cloned.1.call-update) | async-done | bytes 282640
  2539.9 69.7 %reduce-scatter.205.cloned.1.call-done = f32[184,384]{1,0:T(8,128)} async-done(((f32[1472,384]{1,0:T(8,128)}), f32[184,384]{1,0:T(8,128)}) %reduce-scatter.205.cloned.1.call-update) | async-done | bytes 282640
  2611.5 347.2 %reduce-scatter.139.cloned.1.call-done = f32[184,3584]{1,0:T(8,128)} async-done(((f32[1472,3584]{1,0:T(8,128)}), f32[184,3584]{1,0:T(8,128)}) %reduce-scatter.139.cloned.1.call-update) | async-done | bytes 2637840 | tf_op jit(solution)/shard_map/reduce_scatter | solution.py:95
  2963.0 67.4 %reduce-scatter.211.cloned.1.call-done = f32[184,384]{1,0:T(8,128)} async-done(((f32[1472,384]{1,0:T(8,128)}), f32[184,384]{1,0:T(8,128)}) %reduce-scatter.211.cloned.1.call-update) | async-done | bytes 282640
  3032.2 68.9 %reduce-scatter.209.cloned.1.call-done = f32[184,384]{1,0:T(8,128)} async-done(((f32[1472,384]{1,0:T(8,128)}), f32[184,384]{1,0:T(8,128)}) %reduce-scatter.209.cloned.1.call-update) | async-done | bytes 282640
  3103.0 70.5 %reduce-scatter.131.cloned.1.call-done = f32[48,1472]{1,0:T(8,128)} async-done(((f32[384,1472]{1,0:T(8,128)}), f32[48,1472]{1,0:T(8,128)}) %reduce-scatter.131.cloned.1.call-update) | async-done | bytes 282640 | tf_op jit(solution)/shard_map/reduce_scatter | solution.py:93
  3175.5 70.2 %reduce-scatter.129.cloned.1.call-done = f32[48,1472]{1,0:T(8,128)} async-done(((f32[384,1472]{1,0:T(8,128)}), f32[48,1472]{1,0:T(8,128)}) %reduce-scatter.129.cloned.1.call-update) | async-done | bytes 282640 | tf_op jit(solution)/shard_map/reduce_scatter | solution.py:93
  3247.7 69.7 %reduce-scatter.191.cloned.1.call-done = f32[184,384]{1,0:T(8,128)} async-done(((f32[1472,384]{1,0:T(8,128)}), f32[184,384]{1,0:T(8,128)}) %reduce-scatter.191.cloned.1.call-update) | async-done | bytes 282640
  3319.3 69.1 %reduce-scatter.189.cloned.1.call-done = f32[184,384]{1,0:T(8,128)} async-done(((f32[1472,384]{1,0:T(8,128)}), f32[184,384]{1,0:T(8,128)}) %reduce-scatter.189.cloned.1.call-update) | async-done | bytes 282640
  3390.3 70.2 %reduce-scatter.195.cloned.1.call-done = f32[184,384]{1,0:T(8,128)} async-done(((f32[1472,384]{1,0:T(8,128)}), f32[184,384]{1,0:T(8,128)}) %reduce-scatter.195.cloned.1.call-update) | async-done | bytes 282640
  3462.3 69.0 %reduce-scatter.193.cloned.1.call-done = f32[184,384]{1,0:T(8,128)} async-done(((f32[1472,384]{1,0:T(8,128)}), f32[184,384]{1,0:T(8,128)}) %reduce-scatter.193.cloned.1.call-update) | async-done | bytes 282640
  3533.2 70.2 %reduce-scatter.199.cloned.1.call-done = f32[184,384]{1,0:T(8,128)} async-done(((f32[1472,384]{1,0:T(8,128)}), f32[184,384]{1,0:T(8,128)}) %reduce-scatter.199.cloned.1.call-update) | async-done | bytes 282640
  3605.2 69.1 %reduce-scatter.197.cloned.1.call-done = f32[184,384]{1,0:T(8,128)} async-done(((f32[1472,384]{1,0:T(8,128)}), f32[184,384]{1,0:T(8,128)}) %reduce-scatter.197.cloned.1.call-update) | async-done | bytes 282640
  3676.2 70.5 %reduce-scatter.127.cloned.1.call-done = f32[48,1472]{1,0:T(8,128)} async-done(((f32[384,1472]{1,0:T(8,128)}), f32[48,1472]{1,0:T(8,128)}) %reduce-scatter.127.cloned.1.call-update) | async-done | bytes 282640 | tf_op jit(solution)/shard_map/reduce_scatter | solution.py:89
  3748.6 70.6 %reduce-scatter.125.cloned.1.call-done = f32[48,1472]{1,0:T(8,128)} async-done(((f32[384,1472]{1,0:T(8,128)}), f32[48,1472]{1,0:T(8,128)}) %reduce-scatter.125.cloned.1.call-update) | async-done | bytes 282640 | tf_op jit(solution)/shard_map/reduce_scatter | solution.py:89
  3821.2 347.8 %reduce-scatter.137.cloned.1.call-done = f32[184,3584]{1,0:T(8,128)} async-done(((f32[1472,3584]{1,0:T(8,128)}), f32[184,3584]{1,0:T(8,128)}) %reduce-scatter.137.cloned.1.call-update) | async-done | bytes 2637840 | tf_op jit(solution)/shard_map/reduce_scatter | solution.py:95
  4173.2 66.8 %reduce-scatter.203.cloned.1.call-done = f32[184,384]{1,0:T(8,128)} async-done(((f32[1472,384]{1,0:T(8,128)}), f32[184,384]{1,0:T(8,128)}) %reduce-scatter.203.cloned.1.call-update) | async-done | bytes 282640
  4241.9 69.8 %reduce-scatter.201.cloned.1.call-done = f32[184,384]{1,0:T(8,128)} async-done(((f32[1472,384]{1,0:T(8,128)}), f32[184,384]{1,0:T(8,128)}) %reduce-scatter.201.cloned.1.call-update) | async-done | bytes 282640
  4457.9 40.1 all-reduce.12
  (899 shorter events, 1205.7 us)
Async XLA Ops:
  1030.6 1436.6 %reduce-scatter.133.cloned.1.call-start = ((), (), s32[]{:S(2)}) async-start(), calls=%async_computation.67 | async-start | bytes 23740416 | tf_op jit(solution)/shard_map/reduce_scatter | solution.py:94
  1042.5 1495.6 %reduce-scatter.207.cloned.1.call-start = ((), (), s32[]{:S(2)}) async-start(), calls=%async_computation.110 | async-start | bytes 2543616
  1060.8 1548.8 %reduce-scatter.205.cloned.1.call-start = ((), (), s32[]{:S(2)}) async-start(), calls=%async_computation.109 | async-start | bytes 2543616
  1072.6 1886.1 %reduce-scatter.139.cloned.1.call-start = ((), (), s32[]{:S(2)}) async-start(), calls=%async_computation.73 | async-start | bytes 23740416 | tf_op jit(solution)/shard_map/reduce_scatter | solution.py:95
  1082.8 1947.5 %reduce-scatter.211.cloned.1.call-start = ((), (), s32[]{:S(2)}) async-start(), calls=%async_computation.112 | async-start | bytes 2543616
  1092.9 2008.2 %reduce-scatter.209.cloned.1.call-start = ((), (), s32[]{:S(2)}) async-start(), calls=%async_computation.111 | async-start | bytes 2543616
  1102.9 2070.6 %reduce-scatter.131.cloned.1.call-start = ((), (), s32[]{:S(2)}) async-start(), calls=%async_computation.66 | async-start | bytes 2654208 | tf_op jit(solution)/shard_map/reduce_scatter | solution.py:93
  1106.2 2139.5 %reduce-scatter.129.cloned.1.call-start = ((), (), s32[]{:S(2)}) async-start(), calls=%async_computation.65 | async-start | bytes 2654208 | tf_op jit(solution)/shard_map/reduce_scatter | solution.py:93
  1109.5 2208.0 %reduce-scatter.191.cloned.1.call-start = ((), (), s32[]{:S(2)}) async-start(), calls=%async_computation.102 | async-start | bytes 2543616
  1128.3 2260.1 %reduce-scatter.189.cloned.1.call-start = ((), (), s32[]{:S(2)}) async-start(), calls=%async_computation.101 | async-start | bytes 2543616
  1137.9 2322.6 %reduce-scatter.195.cloned.1.call-start = ((), (), s32[]{:S(2)}) async-start(), calls=%async_computation.104 | async-start | bytes 2543616
  1142.2 2389.1 %reduce-scatter.193.cloned.1.call-start = ((), (), s32[]{:S(2)}) async-start(), calls=%async_computation.103 | async-start | bytes 2543616
  1146.6 2456.7 %reduce-scatter.199.cloned.1.call-start = ((), (), s32[]{:S(2)}) async-start(), calls=%async_computation.106 | async-start | bytes 2543616
  1151.2 2523.1 %reduce-scatter.197.cloned.1.call-start = ((), (), s32[]{:S(2)}) async-start(), calls=%async_computation.105 | async-start | bytes 2543616
  1155.8 2590.9 %reduce-scatter.127.cloned.1.call-start = ((), (), s32[]{:S(2)}) async-start(), calls=%async_computation.64 | async-start | bytes 2654208 | tf_op jit(solution)/shard_map/reduce_scatter | solution.py:89
  1159.1 2660.1 %reduce-scatter.125.cloned.1.call-start = ((), (), s32[]{:S(2)}) async-start(), calls=%async_computation.63 | async-start | bytes 2654208 | tf_op jit(solution)/shard_map/reduce_scatter | solution.py:89
  1162.5 3006.5 %reduce-scatter.137.cloned.1.call-start = ((), (), s32[]{:S(2)}) async-start(), calls=%async_computation.71 | async-start | bytes 23740416 | tf_op jit(solution)/shard_map/reduce_scatter | solution.py:95
  1174.2 3065.8 %reduce-scatter.203.cloned.1.call-start = ((), (), s32[]{:S(2)}) async-start(), calls=%async_computation.108 | async-start | bytes 2543616
  1177.3 3134.3 %reduce-scatter.201.cloned.1.call-start = ((), (), s32[]{:S(2)}) async-start(), calls=%async_computation.107 | async-start | bytes 2543616
  1180.5 3160.4 %reduce-scatter.187.cloned.1.call-start = ((), (), s32[]{:S(2)}) async-start(), calls=%async_computation.100 | async-start | bytes 1884160
  1409.8 2961.5 %reduce-scatter.185.cloned.1.call-start = ((), (), s32[]{:S(2)}) async-start(), calls=%async_computation.99 | async-start | bytes 1884160
  1771.7 2632.0 %reduce-scatter.179.cloned.1.call-start = ((), (), s32[]{:S(2)}) async-start(), calls=%async_computation.96 | async-start | bytes 2293760
  2121.4 2314.8 %reduce-scatter.177.cloned.1.call-start = ((), (), s32[]{:S(2)}) async-start(), calls=%async_computation.95 | async-start | bytes 2293760
  2471.4 2026.7 %reduce-scatter.167.cloned.1.call-start = ((), (), s32[]{:S(2)}) async-start(), calls=%async_computation.90 | async-start | bytes 245760
  2539.9 1959.1 %reduce-scatter.165.cloned.1.call-start = ((), (), s32[]{:S(2)}) async-start(), calls=%async_computation.89 | async-start | bytes 245760
  2611.5 1904.0 %reduce-scatter.183.cloned.1.call-start = ((), (), s32[]{:S(2)}) async-start(), calls=%async_computation.98 | async-start | bytes 2293760
  2962.9 1574.7 %reduce-scatter.171.cloned.1.call-start = ((), (), s32[]{:S(2)}) async-start(), calls=%async_computation.92 | async-start | bytes 245760
  3032.2 1527.7 %reduce-scatter.169.cloned.1.call-start = ((), (), s32[]{:S(2)}) async-start(), calls=%async_computation.91 | async-start | bytes 245760
  3102.9 1480.2 %reduce-scatter.175.cloned.1.call-start = ((), (), s32[]{:S(2)}) async-start(), calls=%async_computation.94 | async-start | bytes 471040
  3175.5 1430.9 %reduce-scatter.173.cloned.1.call-start = ((), (), s32[]{:S(2)}) async-start(), calls=%async_computation.93 | async-start | bytes 471040
  3247.6 1381.6 %reduce-scatter.147.cloned.1.call-start = ((), (), s32[]{:S(2)}) async-start(), calls=%async_computation.80 | async-start | bytes 245760
  3319.2 1332.3 %reduce-scatter.145.cloned.1.call-start = ((), (), s32[]{:S(2)}) async-start(), calls=%async_computation.79 | async-start | bytes 245760
  (243 other events, 23370.2 us)
Sparse Core Ops, SparseCore 0:
  10.3 43.3 all-gather.47
  55.9 39.5 all-gather.49
  97.7 39.5 all-gather.51
  139.3 39.8 all-gather.53
  222.9 39.5 all-gather.59
  264.7 39.5 all-gather.55
  306.5 39.8 all-gather.61
  410.0 151.6 all-gather.63
  563.8 149.8 all-gather.65
  715.8 155.4 all-gather.67
  1047.6 358.4 reduce-scatter.142
  1410.4 357.6 reduce-scatter.140
  1771.8 345.4 reduce-scatter.134
  2121.6 345.4 reduce-scatter.132
  2470.6 67.4 reduce-scatter.206
  2542.1 67.5 reduce-scatter.204
  2613.5 345.1 reduce-scatter.138
  2962.7 67.6 reduce-scatter.210
  3033.8 67.2 reduce-scatter.208
  3105.6 67.8 reduce-scatter.130
  3177.8 67.8 reduce-scatter.128
  3249.6 67.8 reduce-scatter.190
  3321.0 67.3 reduce-scatter.188
  3392.4 67.9 reduce-scatter.194
  3463.9 67.4 reduce-scatter.192
  3535.3 67.9 reduce-scatter.198
  3606.9 67.2 reduce-scatter.196
  3678.6 67.9 reduce-scatter.126
  3751.1 68.0 reduce-scatter.124
  3823.6 345.3 reduce-scatter.136
  4172.4 67.5 reduce-scatter.202
  4243.9 67.7 reduce-scatter.200
  (33 shorter events, 752.3 us)
where the time goes:
time: 5010 us; the launch traced here: 5000 us
  waiting for transfers between devices  4220 us (84%)
  matrix products  339 us (7%)
  blocking collectives  197 us (4%)
  local copies, waits for them, and re-layouts  150 us (3%)
  other arithmetic  64.2 us (1%)
    unnamed x99, waiting for transfers between devices  1170 us
    reduce_scatter x2, waiting for transfers between devices, reduce_grads(): lax.psum_scatter(grads[9], 'tgt', scatter_dimension=0, tiled=True)  695 us
    reduce_scatter x2, waiting for transfers between devices, reduce_grads(): lax.psum_scatter(grads[8], 'tgt', scatter_dimension=0, tiled=True)  691 us
    reduce_scatter x2, waiting for transfers between devices, reduce_grads(): lax.psum_scatter(grads[10], 'tgt', scatter_dimension=0, tiled=True)  584 us
    all_gather x1, waiting for transfers between devices, on_device(): lax.all_gather(ffn_gate, 'tgt', axis=0, tiled=True)  151 us
    all_gather x1, waiting for transfers between devices, on_device(): lax.all_gather(ffn_down, 'tgt', axis=0, tiled=True)  150 us
    all_gather x1, waiting for transfers between devices, on_device(): lax.all_gather(ffn_up, 'tgt', axis=0, tiled=True)  144 us
    reduce_scatter x2, waiting for transfers between devices, reduce_grads(): lax.psum_scatter(grads[3], 'tgt', scatter_dimension=0, tiled=True)  141 us
  transfers between devices with their start and end apart: 65, of which 59 were waited for; matrix products, arithmetic and copies ran while one was open for 9% of the time, Pallas kernels for 0%

commit v1 on v0

v1 whole, which is shorter than its diff:
```python
import functools

import jax
import jax.numpy as jnp
import numpy as np
from jax import lax
from jax.experimental import pallas as pl
from jax.experimental.pallas import tpu as pltpu
from jax.sharding import PartitionSpec as P

HEADS = 6
HEAD = 64
BUCKETS = 32
MAX_DIST = 128
ROWS = 192
SPAN = 256
STATS = 128

EPS = 1e-06
NEG = -1e30
HIGH = lax.Precision.HIGHEST
BF = jnp.bfloat16
F32 = jnp.float32
MESH = pl.DeviceIdType.MESH
NT = (((1,), (1,)), ((), ()))
TN = (((0,), (0,)), ((), ()))
VMEM_SPEC = pl.BlockSpec(memory_space=pltpu.VMEM)
ANY_SPEC = pl.BlockSpec(memory_space=pl.ANY)
VMEM_CAP = 56 * 1024 * 1024


def distance_onehot():
    distance = (SPAN - np.arange(SPAN)) % SPAN
    exact_max = BUCKETS // 2
    scaled = (
        np.log(np.maximum(distance, 1) / exact_max)
        / np.log(MAX_DIST / exact_max)
        * (BUCKETS - exact_max)
    )
    far = np.minimum(
        exact_max + np.floor(np.maximum(scaled, 0.0)).astype(np.int64), BUCKETS - 1
    )
    bucket = np.where(distance < exact_max, distance, far)
    return (np.arange(BUCKETS)[:, None] == bucket[None, :]).astype(np.float32)


def dot(left, right):
    return jnp.dot(left, right, preferred_element_type=F32)


def dot_nt(left, right):
    return lax.dot_general(left, right, NT, preferred_element_type=F32)


def dot_tn(left, right):
    return lax.dot_general(left, right, TN, preferred_element_type=F32)


def rms_scale(inputs):
    return lax.rsqrt(jnp.mean(inputs * inputs, axis=-1, keepdims=True) + EPS)


def rms_back(inputs, gain, upstream):
    scale = rms_scale(inputs)
    gu = gain * upstream
    inner = jnp.mean(inputs * gu, axis=-1, keepdims=True)
    dx = scale * gu - inputs * (scale * scale * scale * inner)
    return dx, jnp.sum(upstream * inputs * scale, axis=0)


def half_masks():
    lane = lax.broadcasted_iota(jnp.int32, (1, 2 * HEAD), 1)
    low = (lane < HEAD).astype(BF)
    return low, 1 - low


def pair(index):
    return slice(index * 2 * HEAD, (index + 1) * 2 * HEAD)


def head_bias(base_ref, head):
    row = jnp.broadcast_to(base_ref[head : head + 1, :], (ROWS, SPAN))
    return pltpu.roll(row, 0, 1, stride=1, stride_axis=0)


def causal_mask():
    rows = lax.broadcasted_iota(jnp.int32, (ROWS, SPAN), 0)
    cols = lax.broadcasted_iota(jnp.int32, (ROWS, SPAN), 1)
    return cols <= rows


def self_fwd_kernel(items, qkv_ref, base_ref, att_ref, k_pad, v_pad):
    inner = HEADS * HEAD
    k_pad[...] = jnp.zeros_like(k_pad)
    v_pad[...] = jnp.zeros_like(v_pad)
    for item in range(items):
        k_pad[item, :ROWS, :] = qkv_ref[item, :, inner : 2 * inner]
        v_pad[item, :ROWS, :] = qkv_ref[item, :, 2 * inner :]
    causal = causal_mask()
    masks = half_masks()
    for index in range(HEADS // 2):
        sums = [None] * items
        for half in range(2):
            bias = head_bias(base_ref, 2 * index + half)
            for item in range(items):
                query = qkv_ref[item, :, pair(index)] * masks[half]
                scores = dot_nt(query, k_pad[item, :, pair(index)]) + bias
                scores = jnp.where(causal, scores, NEG)
                top = jnp.max(scores, axis=-1, keepdims=True)
                probs = jnp.exp(scores - top)
                probs = probs * (1.0 / jnp.sum(probs, axis=-1, keepdims=True))
                part = dot(probs.astype(BF), v_pad[item, :, pair(index)] * masks[half])
                sums[item] = part if half == 0 else sums[item] + part
        for item in range(items):
            att_ref[item, :, pair(index)] = sums[item].astype(BF)


def self_fwd(qkv, base):
    items = qkv.shape[0]
    inner = HEADS * HEAD
    return pl.pallas_call(
        functools.partial(self_fwd_kernel, items),
        out_shape=jax.ShapeDtypeStruct((items, ROWS, inner), BF),
        in_specs=[VMEM_SPEC] * 2,
        out_specs=VMEM_SPEC,
        scratch_shapes=[pltpu.VMEM((items, SPAN, inner), BF)] * 2,
        compiler_params=pltpu.CompilerParams(vmem_limit_bytes=VMEM_CAP),
        cost_estimate=pl.CostEstimate(
            flops=items * HEADS * ROWS * SPAN * 128 * 4,
            bytes_accessed=items * ROWS * inner * 8,
            transcendentals=items * HEADS * ROWS * SPAN,
        ),
        name="self_fwd",
    )(qkv, base)


def diagonal_sums(values):
    total = values[:8]
    for start in range(8, ROWS, 8):
        total = total + pltpu.roll(values[start : start + 8], SPAN - start, 1)
    row = lax.broadcasted_iota(jnp.int32, (8, SPAN), 0)
    for bit in (1, 2, 4):
        total = jnp.where((row & bit) > 0, pltpu.roll(total, SPAN - bit, 1), total)
    return jnp.sum(total, axis=0, keepdims=True)


def self_bwd_kernel(items, qkv_ref, datt_ref, base_ref, dqkv_ref, diag_ref, k_pad, v_pad):
    inner = HEADS * HEAD
    k_pad[...] = jnp.zeros_like(k_pad)
    v_pad[...] = jnp.zeros_like(v_pad)
    diag_ref[...] = jnp.zeros_like(diag_ref)
    for item in range(items):
        k_pad[item, :ROWS, :] = qkv_ref[item, :, inner : 2 * inner]
        v_pad[item, :ROWS, :] = qkv_ref[item, :, 2 * inner :]
    causal = causal_mask()
    masks = half_masks()
    for index in range(HEADS // 2):
        dq = [None] * items
        dk = [None] * items
        dv = [None] * items
        for half in range(2):
            head = 2 * index + half
            bias = head_bias(base_ref, head)
            ds_sum = None
            for item in range(items):
                query = qkv_ref[item, :, pair(index)] * masks[half]
                upstream = datt_ref[item, :, pair(index)] * masks[half]
                keys = k_pad[item, :, pair(index)]
                scores = dot_nt(query, keys) + bias
                scores = jnp.where(causal, scores, NEG)
                top = jnp.max(scores, axis=-1, keepdims=True)
                probs = jnp.exp(scores - top)
                probs = probs * (1.0 / jnp.sum(probs, axis=-1, keepdims=True))
                dprobs = dot_nt(upstream, v_pad[item, :, pair(index)])
                delta = jnp.sum(probs * dprobs, axis=-1, keepdims=True)
                ds = probs * (dprobs - delta)
                ds_sum = ds if item == 0 else ds_sum + ds
                ds_low = ds.astype(BF)
                q_part = dot(ds_low, keys * masks[half])
                k_part = dot_tn(ds_low, query)[:ROWS]
                v_part = dot_tn(probs.astype(BF), upstream)[:ROWS]
                dq[item] = q_part if half == 0 else dq[item] + q_part
                dk[item] = k_part if half == 0 else dk[item] + k_part
                dv[item] = v_part if half == 0 else dv[item] + v_part
            diag_ref[head : head + 1, :] = diagonal_sums(ds_sum)
        for item in range(items):
            dqkv_ref[item, :, pair(index)] = dq[item].astype(BF)
            dqkv_ref[item, :, pair(index + 3)] = dk[item].astype(BF)
            dqkv_ref[item, :, pair(index + 6)] = dv[item].astype(BF)


def self_bwd(qkv, datt, base):
    items = qkv.shape[0]
    inner = HEADS * HEAD
    return pl.pallas_call(
        functools.partial(self_bwd_kernel, items),
        out_shape=(
            jax.ShapeDtypeStruct((items, ROWS, 3 * inner), BF),
            jax.ShapeDtypeStruct((8, SPAN), F32),
        ),
        in_specs=[VMEM_SPEC] * 3,
        out_specs=(VMEM_SPEC, VMEM_SPEC),
        scratch_shapes=[pltpu.VMEM((items, SPAN, inner), BF)] * 2,
        compiler_params=pltpu.CompilerParams(vmem_limit_bytes=VMEM_CAP),
        cost_estimate=pl.CostEstimate(
            flops=items * HEADS * ROWS * SPAN * 128 * 10,
            bytes_accessed=items * ROWS * inner * 14,
            transcendentals=items * HEADS * ROWS * SPAN,
        ),
        name="self_bwd",
    )(qkv, datt, base)


def greet(axis, offsets):
    me = lax.axis_index(axis)
    barrier = pltpu.get_barrier_semaphore()
    for offset in offsets:
        pl.semaphore_signal(
            barrier, inc=1, device_id={axis: jnp.bitwise_xor(me, offset)}, device_id_type=MESH
        )
    pl.semaphore_wait(barrier, len(offsets))


def send(src, dst, send_sem, recv_sem, offset):
    me = lax.axis_index("mem")
    return pltpu.make_async_remote_copy(
        src_ref=src,
        dst_ref=dst,
        send_sem=send_sem,
        recv_sem=recv_sem,
        device_id={"mem": jnp.bitwise_xor(me, offset)},
        device_id_type=MESH,
    )


def column(stats, index):
    return stats[:, index : index + 1]


def spread(stats, index, masks):
    return jnp.where(masks, column(stats, 2 * index), column(stats, 2 * index + 1))


def cross_fwd_kernel(
    items, q_ref, k_ref, v_ref, bias_ref, all_ref, att_ref, lse_ref,
    out_o, out_s, in_o, in_s, q_send, q_recv, o_send, o_recv, s_send, s_recv,
):
    me = lax.axis_index("mem")
    greet("mem", (1, 2, 3))
    q_to_core = send(q_ref, all_ref.at[1], q_send.at[0], q_recv.at[0], 1)
    q_to_far = send(q_ref, all_ref.at[2], q_send.at[1], q_recv.at[1], 2)
    q_relay = send(all_ref.at[2], all_ref.at[3], q_send.at[2], q_recv.at[2], 1)
    q_to_far.start()
    q_to_core.start()
    all_ref[0] = q_ref[...]
    low, high = half_masks()
    lane = lax.broadcasted_iota(jnp.int32, (1, STATS), 1)
    is_low = lax.broadcasted_iota(jnp.int32, (1, 2 * HEAD), 1) < HEAD
    copies = []
    for slot in (0, 2, 3, 1):
        if slot == 2:
            q_to_far.wait_recv()
            q_relay.start()
        if slot == 3:
            q_relay.wait_recv()
        if slot == 1:
            q_to_core.wait_recv()
        owner = jnp.bitwise_xor(me, slot)
        for item in range(items):
            place = owner * items + item
            bias = bias_ref[place]
            stats = jnp.zeros((ROWS, STATS), F32)
            for index in range(HEADS // 2):
                both = all_ref[slot, item, :, pair(index)]
                keys = k_ref[place, :, pair(index)]
                values = v_ref[place, :, pair(index)]
                total = None
                scales = []
                for half, mask in ((0, low), (1, high)):
                    scores = dot_nt(both * mask, keys) + bias
                    top = jnp.max(scores, axis=-1, keepdims=True)
                    probs = jnp.exp(scores - top)
                    amount = jnp.sum(probs, axis=-1, keepdims=True)
                    part = dot(probs.astype(BF), values * mask)
                    total = part if half == 0 else total + part
                    scales.append(1.0 / amount)
                    stats = jnp.where(
                        lane == 2 * index + half, top + jnp.log(amount), stats
                    )
                total = total * jnp.where(is_low, scales[0], scales[1])
                out_o[slot, item, :, pair(index)] = total.astype(BF)
            out_s[slot, item] = stats
        if slot:
            copies.append(send(out_o.at[slot], in_o.at[slot], o_send.at[slot], o_recv.at[slot], slot))
            copies.append(send(out_s.at[slot], in_s.at[slot], s_send.at[slot], s_recv.at[slot], slot))
            copies[-2].start()
            copies[-1].start()
    q_to_core.wait_send()
    q_to_far.wait_send()
    q_relay.wait_send()
    for copy in copies:
        copy.wait()
    for item in range(items):
        stats = [out_s[0, item]] + [in_s[slot, item] for slot in (1, 2, 3)]
        top = jnp.maximum(jnp.maximum(stats[0], stats[1]), jnp.maximum(stats[2], stats[3]))
        shares = [jnp.exp(part - top) for part in stats]
        amount = shares[0] + shares[1] + shares[2] + shares[3]
        lse_ref[item] = top + jnp.log(amount)
        scale = 1.0 / amount
        shares = [part * scale for part in shares]
        for index in range(HEADS // 2):
            total = out_o[0, item, :, pair(index)].astype(F32) * spread(shares[0], index, is_low)
            for slot in (1, 2, 3):
                total += in_o[slot, item, :, pair(index)].astype(F32) * spread(
                    shares[slot], index, is_low
                )
            att_ref[item, :, pair(index)] = total.astype(BF)


def cross_fwd(queries, keys, values, bias):
    items = queries.shape[0]
    inner = HEADS * HEAD
    block = (4, items, ROWS, inner)
    stat_block = (4, items, ROWS, STATS)
    flops = 4 * items * HEADS * ROWS * SPAN * 128 * 4
    return pl.pallas_call(
        functools.partial(cross_fwd_kernel, items),
        out_shape=(
            jax.ShapeDtypeStruct(block, BF),
            jax.ShapeDtypeStruct((items, ROWS, inner), BF),
            jax.ShapeDtypeStruct((items, ROWS, STATS), F32),
        ),
        in_specs=[VMEM_SPEC] * 4,
        out_specs=(VMEM_SPEC,) * 3,
        scratch_shapes=[
            pltpu.VMEM(block, BF),
            pltpu.VMEM(stat_block, F32),
            pltpu.VMEM(block, BF),
            pltpu.VMEM(stat_block, F32),
            pltpu.SemaphoreType.DMA((3,)),
            pltpu.SemaphoreType.DMA((3,)),
            pltpu.SemaphoreType.DMA((4,)),
            pltpu.SemaphoreType.DMA((4,)),
            pltpu.SemaphoreType.DMA((4,)),
            pltpu.SemaphoreType.DMA((4,)),
        ],
        compiler_params=pltpu.CompilerParams(
            collective_id=1, has_side_effects=True, vmem_limit_bytes=VMEM_CAP
        ),
        cost_estimate=pl.CostEstimate(
            flops=flops, bytes_accessed=8 * 1024 * 1024, transcendentals=flops // 512
        ),
        name="cross_fwd",
    )(queries, keys, values, bias)


def cross_bwd_kernel(
    items, all_ref, back_ref, stat_ref, k_ref, v_ref, bias_ref, dk_ref, dv_ref, dq_ref,
    all_b, all_s, out_q, in_q, b_send, b_recv, s_send, s_recv, q_send, q_recv,
):
    me = lax.axis_index("mem")
    greet("mem", (1, 2, 3))
    moves = []
    for offset, slot, source in ((2, 2, None), (1, 1, None), (1, 3, 2)):
        number = len(moves)
        moves.append(
            (
                send(back_ref if source is None else all_b.at[source], all_b.at[slot],
                     b_send.at[number], b_recv.at[number], offset),
                send(stat_ref if source is None else all_s.at[source], all_s.at[slot],
                     s_send.at[number], s_recv.at[number], offset),
            )
        )
    for move in moves[:2]:
        for copy in move:
            copy.start()
    low, high = half_masks()
    copies = []
    for slot in (0, 2, 3, 1):
        if slot == 2:
            for copy in moves[0]:
                copy.wait_recv()
            for copy in moves[2]:
                copy.start()
        if slot == 3:
            for copy in moves[2]:
                copy.wait_recv()
        if slot == 1:
            for copy in moves[1]:
                copy.wait_recv()
        owner = jnp.bitwise_xor(me, slot)
        for item in range(items):
            place = owner * items + item
            bias = bias_ref[place]
            stats = stat_ref[item] if slot == 0 else all_s[slot, item]
            for index in range(HEADS // 2):
                both = all_ref[slot, item, :, pair(index)]
                if slot == 0:
                    upstream = back_ref[item, :, pair(index)]
                else:
                    upstream = all_b[slot, item, :, pair(index)]
                keys = k_ref[place, :, pair(index)]
                values = v_ref[place, :, pair(index)]
                dq = dk = dv = None
                for half, mask in ((0, low), (1, high)):
                    head = 2 * index + half
                    query = both * mask
                    back = upstream * mask
                    scores = dot_nt(query, keys) + bias
                    probs = jnp.exp(scores - column(stats, head))
                    dprobs = dot_nt(back, values)
                    ds = (probs * (dprobs - column(stats, 8 + head))).astype(BF)
                    q_part = dot(ds, keys * mask)
                    k_part = dot_tn(ds, query)
                    v_part = dot_tn(probs.astype(BF), back)
                    dq = q_part if half == 0 else dq + q_part
                    dk = k_part if half == 0 else dk + k_part
                    dv = v_part if half == 0 else dv + v_part
                out_q[slot, item, :, pair(index)] = dq.astype(BF)
                dk_ref[place, :, pair(index)] = dk.astype(BF)
                dv_ref[place, :, pair(index)] = dv.astype(BF)
        if slot:
            copies.append(send(out_q.at[slot], in_q.at[slot], q_send.at[slot], q_recv.at[slot], slot))
            copies[-1].start()
    for move in moves:
        for copy in move:
            copy.wait_send()
    for copy in copies:
        copy.wait()
    for item in range(items):
        for index in range(HEADS // 2):
            total = out_q[0, item, :, pair(index)].astype(F32)
            for slot in (1, 2, 3):
                total += in_q[slot, item, :, pair(index)].astype(F32)
            dq_ref[item, :, pair(index)] = total.astype(BF)


def cross_bwd(all_queries, back, stats, keys, values, bias):
    items = back.shape[0]
    inner = HEADS * HEAD
    block = (4, items, ROWS, inner)
    flops = 4 * items * HEADS * ROWS * SPAN * 128 * 10
    return pl.pallas_call(
        functools.partial(cross_bwd_kernel, items),
        out_shape=(
            jax.ShapeDtypeStruct(keys.shape, BF),
            jax.ShapeDtypeStruct(keys.shape, BF),
            jax.ShapeDtypeStruct((items, ROWS, inner), BF),
        ),
        in_specs=[VMEM_SPEC] * 6,
        out_specs=(VMEM_SPEC,) * 3,
        scratch_shapes=[
            pltpu.VMEM(block, BF),
            pltpu.VMEM((4, items, ROWS, STATS), F32),
            pltpu.VMEM(block, BF),
            pltpu.VMEM(block, BF),
            pltpu.SemaphoreType.DMA((3,)),
            pltpu.SemaphoreType.DMA((3,)),
            pltpu.SemaphoreType.DMA((3,)),
            pltpu.SemaphoreType.DMA((3,)),
            pltpu.SemaphoreType.DMA((4,)),
            pltpu.SemaphoreType.DMA((4,)),
        ],
        compiler_params=pltpu.CompilerParams(
            collective_id=2, has_side_effects=True, vmem_limit_bytes=VMEM_CAP
        ),
        cost_estimate=pl.CostEstimate(
            flops=flops, bytes_accessed=12 * 1024 * 1024, transcendentals=flops // 1280
        ),
        name="cross_bwd",
    )(all_queries, back, stats, keys, values, bias)


def over_mem(value, offset):
    return lax.ppermute(value, "mem", [(i, i ^ offset) for i in range(4)])


def gather_mem(value):
    far = over_mem(value, 2)
    near = over_mem(value, 1)
    return value, near, far, over_mem(far, 1)


def owner_sum(own, near, far, far_near):
    far = (far + over_mem(far_near.astype(BF), 1).astype(F32)).astype(BF)
    total = own + over_mem(near.astype(BF), 1).astype(F32)
    return total + over_mem(far, 2).astype(F32)


def gather_tgt(shard):
    return lax.all_gather(shard, "tgt", axis=0, tiled=True)


def scatter_tgt(partial):
    return lax.psum_scatter(partial, "tgt", scatter_dimension=0, tiled=True)


def on_device(
    target, memory, lengths, gate_bias, out_grad, gain_self, gain_cross, gain_ffn, rel_table,
    self_q, self_k, self_v, self_o, cross_q, cross_k, cross_v, cross_o, ffn_gate, ffn_up, ffn_down,
):
    groups = lax.axis_size("mem")
    tgts = lax.axis_size("tgt")
    mem_index = lax.axis_index("mem")
    items, seq, model = target.shape
    all_items, positions_dev, _ = memory.shape
    inner = HEADS * HEAD
    tokens = items * ROWS
    shard_in = ffn_gate.shape[0]
    hidden_shard = ffn_down.shape[0]
    piece = hidden_shard // groups
    quarter = tgts * piece

    def padded(value):
        return jnp.pad(value, ((0, 0), (0, ROWS - seq), (0, 0))).reshape(tokens, model)

    def trimmed(value):
        return value.reshape(items, ROWS, model)[:, :seq]

    def my_columns(weight):
        parts = weight.reshape(shard_in, tgts, groups, piece)
        return lax.dynamic_index_in_dim(parts, mem_index, 2, keepdims=False).reshape(
            shard_in, quarter
        )

    def whole_columns(parts):
        return (
            parts.reshape(groups, shard_in, tgts, piece)
            .transpose(1, 2, 0, 3)
            .reshape(shard_in, tgts * hidden_shard)
            .astype(F32)
        )

    norm_self = gain_self.astype(F32)
    norm_cross = gain_cross.astype(F32)
    norm_ffn = gain_ffn.astype(F32)
    onehot = jnp.asarray(distance_onehot())
    base = jnp.pad(
        lax.dot_general(rel_table, onehot, TN, precision=HIGH), ((0, 2), (0, 0))
    )
    positions = mem_index * positions_dev + jnp.arange(positions_dev)
    bias = jnp.where(positions[None, :] < lengths[:, None], gate_bias, NEG)[:, None, :]

    attn = gather_tgt(
        jnp.concatenate([self_q, self_k, self_v, cross_q, cross_k, cross_v], axis=1)
    )
    self_w = attn[:, : 3 * inner]
    cross_q_w = attn[:, 3 * inner : 4 * inner]
    cross_kv_w = attn[:, 4 * inner :]
    self_o_w = gather_tgt(self_o)
    cross_o_w = gather_tgt(cross_o)
    gate_up = gather_tgt(jnp.concatenate([my_columns(ffn_gate), my_columns(ffn_up)], axis=1))
    down = gather_tgt(
        lax.dynamic_slice_in_dim(ffn_down, mem_index * piece, piece, axis=0)
    )

    inputs = padded(target).astype(F32)
    upstream_low = padded(out_grad)
    upstreams = gather_mem(upstream_low)
    mem_flat = memory.reshape(all_items * positions_dev, model)

    h1 = (inputs * rms_scale(inputs) * norm_self).astype(BF)
    qkv = dot(h1, self_w).astype(BF).reshape(items, ROWS, 3 * inner)
    att = self_fwd(qkv, base).reshape(tokens, inner)
    y1 = inputs + dot(att, self_o_w)
    h2 = (y1 * rms_scale(y1) * norm_cross).astype(BF)
    cq = dot(h2, cross_q_w).astype(BF).reshape(items, ROWS, inner)
    ckv = dot(mem_flat, cross_kv_w).astype(BF)
    ck = ckv[:, :inner].reshape(all_items, positions_dev, inner)
    cv = ckv[:, inner:].reshape(all_items, positions_dev, inner)
    all_queries, catt, lse = cross_fwd(cq, ck, cv, bias)
    catt = catt.reshape(tokens, inner)
    y2 = y1 + dot(catt, cross_o_w)
    h3 = (y2 * rms_scale(y2) * norm_ffn).astype(BF)
    h3s = gather_mem(h3)

    near_far = []
    for part in (0, 1):
        h3_two = jnp.concatenate(h3s[2 * part : 2 * part + 2], axis=0)
        up_two = jnp.concatenate(upstreams[2 * part : 2 * part + 2], axis=0)
        both = dot(h3_two, gate_up)
        gate_pre, up_pre = both[:, :quarter], both[:, quarter:]

        def gated(gate_in, up_in):
            return jax.nn.gelu(gate_in, approximate=True) * up_in

        gated_out, pull = jax.vjp(gated, gate_pre, up_pre)
        hidden = gated_out.astype(BF)
        hidden_back = dot_nt(up_two, down).astype(BF)
        gate_back, up_back = pull(hidden_back.astype(F32))
        two_back = jnp.concatenate([gate_back.astype(BF), up_back.astype(BF)], axis=1)
        h3_back = dot_nt(two_back, gate_up)
        out_part = dot(hidden, down)
        near_far.append((h3_two, up_two, hidden, two_back, h3_back, out_part))
    near, far = near_far
    h3_back = owner_sum(near[4][:tokens], near[4][tokens:], far[4][:tokens], far[4][tokens:])
    out_sum = owner_sum(near[5][:tokens], near[5][tokens:], far[5][:tokens], far[5][tokens:])
    layer_out = trimmed((y2 + out_sum).astype(BF))

    grad_gate_up = (dot_tn(near[0], near[3]) + dot_tn(far[0], far[3])).astype(BF)
    grad_down = (dot_tn(near[2], near[1]) + dot_tn(far[2], far[1])).astype(BF)
    grad_gate_up = scatter_tgt(grad_gate_up)
    grad_down = scatter_tgt(grad_down)
    grad_gate_up = lax.all_gather(grad_gate_up, "mem", axis=0)
    grad_down = lax.all_gather(grad_down, "mem", axis=0, tiled=True).astype(F32)
    grad_gate = whole_columns(grad_gate_up[:, :, :quarter])
    grad_up = whole_columns(grad_gate_up[:, :, quarter:])

    dx, grad_norm_ffn = rms_back(y2, norm_ffn, h3_back)
    dy2 = upstream_low.astype(F32) + dx
    e2 = dy2.astype(BF)
    grad_cross_o = dot_tn(catt, e2)
    dcatt = dot_nt(e2, cross_o_w).astype(BF)
    delta = jnp.sum(
        (dcatt.astype(F32) * catt.astype(F32)).reshape(tokens, HEADS, HEAD), axis=-1
    ).reshape(items, ROWS, HEADS)
    stats = jnp.concatenate(
        [lse[:, :, :8], delta, jnp.zeros((items, ROWS, STATS - 8 - HEADS), F32)], axis=-1
    )
    dck, dcv, dcq = cross_bwd(
        all_queries, dcatt.reshape(items, ROWS, inner), stats, ck, cv, bias
    )
    dckv = jnp.concatenate([dck, dcv], axis=-1).reshape(all_items * positions_dev, 2 * inner)
    dcq = dcq.reshape(tokens, inner)
    grad_cross_kv = dot_tn(mem_flat, dckv)
    memory_grad = dot_nt(dckv, cross_kv_w).astype(BF).reshape(memory.shape)
    grad_cross_q = dot_tn(h2, dcq)
    dx, grad_norm_cross = rms_back(y1, norm_cross, dot_nt(dcq, cross_q_w))
    dy1 = dy2 + dx
    e1 = dy1.astype(BF)
    grad_self_o = dot_tn(att, e1)
    datt = dot_nt(e1, self_o_w).astype(BF).reshape(items, ROWS, inner)
    dqkv, diag = self_bwd(qkv, datt, base)
    dqkv = dqkv.reshape(tokens, 3 * inner)
    grad_self = dot_tn(h1, dqkv)
    dx, grad_norm_self = rms_back(inputs, norm_self, dot_nt(dqkv, self_w))
    target_grad = trimmed((dy1 + dx).astype(BF))
    table = lax.dot_general(
        onehot, diag[:HEADS], NT, precision=HIGH
    )

    wide = jnp.concatenate([grad_self, grad_cross_q, grad_cross_kv], axis=1).astype(BF)
    wide = scatter_tgt(wide)
    wide = lax.psum(wide.astype(F32), "mem")
    outs = scatter_tgt(
        jnp.concatenate([grad_self_o.astype(BF).reshape(tgts, -1, model),
                         grad_cross_o.astype(BF).reshape(tgts, -1, model)], axis=1)
        .reshape(-1, model)
    )
    outs = lax.psum(outs.astype(F32), "mem")
    rows = outs.shape[0] // 2
    small = lax.psum((grad_norm_self, grad_norm_cross, grad_norm_ffn, table), ("tgt", "mem"))
    columns = [wide[:, i * inner : (i + 1) * inner] for i in range(6)]
    return (
        layer_out,
        target_grad,
        memory_grad,
        *small,
        columns[0],
        columns[1],
        columns[2],
        outs[:rows],
        columns[3],
        columns[4],
        columns[5],
        outs[rows:],
        grad_gate,
        grad_up,
        grad_down,
    )


def solution(mesh):
    owned = P(("tgt", "mem"), None, None)
    held = P("tgt", "mem", None)
    rows = P("tgt", None)
    return jax.shard_map(
        on_device,
        mesh=mesh,
        in_specs=(owned, held, P("tgt"), P("tgt", "mem"), owned, P(), P(), P(), P()) + (rows,) * 11,
        out_specs=(owned, owned, held, P(), P(), P(), P()) + (rows,) * 11,
        check_vma=False,
    )
```

time: 5010 us -> 874 us (0.17)
  waiting for transfers between devices: 4220 us -> 393 us
  matrix products: 339 us -> 128 us
  blocking collectives: 197 us -> 86 us
  Pallas kernels: 0 us -> 86.9 us
    reduce_scatter x14 -> x4, waiting for transfers between devices: 2300 us -> 130 us  [scatter_tgt(): return lax.psum_scatter(partial, 'tgt', scatter_dimension=0, tiled=True)]
    unnamed x99 -> x11, waiting for transfers between devices: 1170 us -> 2.16 us
    all_gather x17 -> x7, waiting for transfers between devices: 751 us -> 194 us  [the longest x5 171 us: gather_tgt(): return lax.all_gather(shard, 'tgt', axis=0, tiled=True)]
    dot_general x93 -> x29, matrix products: 339 us -> 128 us  [the longest x9 51.7 us: dot_nt(): return lax.dot_general(left, right, NT, preferred_element_type=F32)]
    all_gather x24 -> x0, blocking collectives: 145 us -> none  [the longest x4 21.9 us: joined(): pieces = jax.tree.map(lambda part: lax.all_gather(part, axis), value)]
    pallas_call x0 -> x4, Pallas kernels: none -> 86.9 us  [the longest x1 37.9 us: cross_fwd(): pl.pallas_call(functools.partial(cross_fwd_kernel, items), out_shape=(jax...]
    unnamed x469 -> x144, local copies, waits for them, and re-layouts: 93.8 us -> 25.7 us
    ppermute x0 -> x12, waiting for transfers between devices: none -> 66.4 us  [over_mem(): return lax.ppermute(value, 'mem', [(i, i ^ offset) for i in range(4)])]
  transfers between devices with their start and end apart: 65 -> 23, of which waited for: 59 -> 11; matrix products, arithmetic and copies ran while one was open for 9% -> 27% of each run, Pallas kernels for 0% -> 10%
where the time goes in v1:
time: 874 us; the launch traced here: 864 us
  waiting for transfers between devices  393 us (45%)
  matrix products  128 us (15%)
  local copies, waits for them, and re-layouts  113 us (13%)
  Pallas kernels  86.9 us (10%)
  blocking collectives  86 us (10%)
  other arithmetic  33.5 us (4%)
  between operations  15.1 us (2%)
    all_gather x5, waiting for transfers between devices, gather_tgt(): return lax.all_gather(shard, 'tgt', axis=0, tiled=True)  171 us
    reduce_scatter x4, waiting for transfers between devices, scatter_tgt(): return lax.psum_scatter(partial, 'tgt', scatter_dimension=0, tiled=True)  130 us
    ppermute x12, waiting for transfers between devices, over_mem(): return lax.ppermute(value, 'mem', [(i, i ^ offset) for i in range(4)])  66.4 us
    dot_general x9, matrix products, dot_nt(): return lax.dot_general(left, right, NT, preferred_element_type=F32)  51.7 us
    psum x1, blocking collectives, on_device(): wide = lax.psum(wide.astype(F32), 'mem')  45.5 us
    psum x1, blocking collectives, on_device(): lax.psum((grad_norm_self, grad_norm_cross, grad_norm_ffn, table), ('tgt',...  40.5 us
    dot_general x9, matrix products, dot(): return jnp.dot(left, right, preferred_element_type=F32)  40.4 us
    pallas_call x1, Pallas kernels, cross_fwd(): pl.pallas_call(functools.partial(cross_fwd_kernel, items), out_shape=(jax...  37.9 us
  transfers between devices with their start and end apart: 23, of which 11 were waited for; matrix products, arithmetic and copies ran while one was open for 27% of the time, Pallas kernels for 10%

profile of v1, /device:TPU:0, one launch (start us, length us, event | category | flops | bytes accessed | tf_op | source)
XLA Modules:
  0.0 864.2 jit_solution(2024449332614934709)
XLA Ops:
  15.4 5.2 reshape.226
  20.7 5.9 reshape.224
  26.6 6.9 dynamic-slice_reduce_fusion
  53.1 6.2 copy.138
  66.5 55.4 %all-gather.9.cloned.1.call-done = bf16[1472,2304]{1,0:T(8,128)(2,1)} async-done(((bf16[184,2304]{1,0:T(8,128)(2,1)}), bf16[1472,2304]{1,0:T(8,128)(2,1)}) %all-gather.9.cloned.1.call-update) | async-done | bytes 6782992 | tf_op jit(solution)/shard_map/all_gather | solution.py:491
  121.9 8.5 fusion.1
  144.1 19.2 %all-gather.11.cloned.1.call-done = bf16[384,1472]{1,0:T(8,128)(2,1)} async-done(((bf16[48,1472]{1,0:T(8,128)(2,1)}), bf16[384,1472]{1,0:T(8,128)(2,1)}) %all-gather.11.cloned.1.call-update) | async-done | bytes 1130512 | tf_op jit(solution)/shard_map/all_gather | solution.py:491
  169.4 37.9 %cross_fwd.1 = (bf16[4,2,192,384]{3,2,1,0:T(8,128)(2,1)}, bf16[2,192,384]{2,1,0:T(8,128)(2,1)}, f32[2,192,128]{2,1,0:T(8,128)}) custom-call(bf16[2,192,384]{2,1,0:T(8,128)(2,1)} %bitcast.123, bf16[8,256,384]{2,1,0:T(8,128)(2,1)} %bitcast.109, bf16[8,256,384]{2,1,0:T(8,128)(2,1)} %bitcast.111, f32[8,1,256]{2,1,0:T(1,128)} %broadcast_in_dim.9.bias_ref), custom_call_target="tpu_custom_call" | custom-call | flops 1207959552 | bytes 8388608 | tf_op jit(solution)/shard_map/cross_fwd/pallas_call | solution.py:326
  221.6 19.2 %collective-permute-done.2 = bf16[384,1472]{0,1:T(8,128)(2,1)} collective-permute-done((bf16[384,1472]{0,1:T(8,128)(2,1)}, bf16[384,1472]{0,1:T(8,128)(2,1)}, u32[]{:S(2)}, u32[]{:S(2)}) %collective-permute-start.2) | collective-permute-done | bytes 1130528 | tf_op jit(solution)/shard_map/ppermute | solution.py:475
  243.1 49.8 %all-gather.15.cloned.1.call-done = bf16[1472,1792]{1,0:T(8,128)(2,1)} async-done(((bf16[184,1792]{1,0:T(8,128)(2,1)}), bf16[1472,1792]{1,0:T(8,128)(2,1)}) %all-gather.15.cloned.1.call-update) | async-done | bytes 5275664 | tf_op jit(solution)/shard_map/all_gather | solution.py:491
  292.9 10.1 %fusion.38 = f32[768,1792]{1,0:T(8,128)} fusion(bf16[1472,1792]{1,0:T(8,128)(2,1)} %all-gather.15.cloned.1.call-done, bf16[384,1472]{0,1:T(8,128)(2,1)} %collective-permute-done, bf16[384,1472]{0,1:T(8,128)(2,1)} %multiply_convert_fusion.3), kind=kOutput, calls=%fused_computation.94 | convolution fusion | flops 4056219648 | bytes 13041664 | tf_op jit(solution)/shard_map/dot_general | solution.py:48
  303.1 46.2 %all-gather.17.cloned.1.call-done = bf16[896,1472]{1,0:T(8,128)(2,1)} async-done(((bf16[112,1472]{1,0:T(8,128)(2,1)}), bf16[896,1472]{1,0:T(8,128)(2,1)}) %all-gather.17.cloned.1.call-update) | async-done | bytes 2637840 | tf_op jit(solution)/shard_map/all_gather | solution.py:491
  349.2 9.8 %fusion.18 = (bf16[768,896]{1,0:T(8,128)(2,1)}, bf16[768,896]{1,0:T(8,128)(2,1)}, bf16[768,896]{1,0:T(8,128)(2,1)S(1)}) fusion(f32[768,1792]{1,0:T(8,128)} %fusion.38, bf16[896,1472]{1,0:T(8,128)(2,1)} %all-gather.17.cloned.1.call-done, bf16[384,1472]{1,0:T(8,128)(2,1)} %copy.117, bf16[384,1472]{1,0:T(8,128)(2,1)S(1)} %bitcast.89), kind=kOutput, calls=%fused_computation.39 | convolution fusion | flops 2049638400 | bytes 14532608 | tf_op jit(solution)/shard_map/dot_general | solution.py:52
  369.4 7.9 fusion.25
  378.5 5.6 add_convert_fusion.1
  384.2 7.0 fusion.35
  391.3 6.0 add_convert_fusion
  397.7 7.3 fusion.34
  405.3 6.5 fusion.36
  421.7 21.6 %collective-permute-done.11 = bf16[384,1472]{0,1:T(8,128)(2,1)S(1)} collective-permute-done((bf16[384,1472]{0,1:T(8,128)(2,1)S(1)}, bf16[384,1472]{0,1:T(8,128)(2,1)S(1)}, u32[]{:S(2)}, u32[]{:S(2)}) %collective-permute-start.11) | collective-permute-done | bytes 1130528 | tf_op jit(solution)/shard_map/ppermute | solution.py:475
  444.9 22.0 %collective-permute-done.5 = bf16[384,1472]{0,1:T(8,128)(2,1)S(1)} collective-permute-done((bf16[384,1472]{0,1:T(8,128)(2,1)S(1)}, bf16[384,1472]{0,1:T(8,128)(2,1)S(1)}, u32[]{:S(2)}, u32[]{:S(2)}) %collective-permute-start.5) | collective-permute-done | bytes 1130528 | tf_op jit(solution)/shard_map/ppermute | solution.py:475
  482.5 35.1 %cross_bwd.1 = (bf16[8,256,384]{2,1,0:T(8,128)(2,1)}, bf16[8,256,384]{2,1,0:T(8,128)(2,1)}, bf16[2,192,384]{2,1,0:T(8,128)(2,1)}) custom-call(bf16[4,2,192,384]{3,2,1,0:T(8,128)(2,1)} %get-tuple-element.27.all_ref, bf16[2,192,384]{2,1,0:T(8,128)(2,1)} %bitcast.119, f32[2,192,128]{2,1,0:T(8,128)} %maximum_maximum_fusion.stat_ref, ...), custom_call_target="tpu_custom_call" | custom-call | flops 3019898880 | bytes 12582912 | tf_op jit(solution)/shard_map/cross_bwd/pallas_call | solution.py:443
  531.3 28.6 %reduce-scatter.9.cloned.1.call-done = bf16[184,1792]{1,0:T(8,128)(2,1)} async-done(((bf16[1472,1792]{1,0:T(8,128)(2,1)}), bf16[184,1792]{1,0:T(8,128)(2,1)}) %reduce-scatter.9.cloned.1.call-update) | async-done | bytes 659472 | tf_op jit(solution)/shard_map/reduce_scatter | solution.py:495
  564.5 9.5 %self_bwd.1 = (bf16[2,192,1152]{2,1,0:T(8,128)(2,1)}, f32[8,256]{1,0:T(8,128)}) custom-call(bf16[2,192,1152]{2,1,0:T(8,128)(2,1)} %bitcast.116, bf16[2,192,384]{2,1,0:T(8,128)(2,1)} %bitcast.120, f32[8,256]{1,0:T(8,128)} %pad.12.base_ref), custom_call_target="tpu_custom_call" | custom-call | flops 754974720 | bytes 2064384 | tf_op jit(solution)/shard_map/self_bwd/pallas_call | solution.py:195
  580.4 5.2 fusion.2
  601.5 7.5 convolution_convert_fusion
  612.2 40.5 %all-reduce.3 = (f32[1472]{0:T(1024)}, f32[1472]{0:T(1024)}, f32[1472]{0:T(1024)}, f32[32,6]{0,1:T(8,128)}) all-reduce(f32[1472]{0:T(1024)S(1)} %get-tuple-element.110, f32[1472]{0:T(1024)S(1)} %copy-done.39, f32[1472]{0:T(1024)S(1)} %copy-done.38, f32[32,6]{0,1:T(8,128)S(1)} %fusion.49), channel_id=1, replica_groups=mesh['tgt'=8,'mem'=4] {'tgt','mem'}, use_global_device_ids=true, to_apply=%region_8.9 | all-reduce | flops 4608 | bytes 36864 | tf_op jit(solution)/shard_map/psum | solution.py:652
  656.0 23.7 %all-gather.21.cloned.1.call-done = bf16[736,1792]{1,0:T(8,128)(2,1)} async-done(((bf16[184,1792]{1,0:T(8,128)(2,1)}), bf16[736,1792]{1,0:T(8,128)(2,1)}) %all-gather.21.cloned.1.call-update) | async-done | bytes 2637840 | tf_op jit(solution)/shard_map/all_gather | solution.py:604
  690.9 5.2 reshape.243
  702.9 5.2 reshape.244
  708.1 101.7 %reduce-scatter.5.cloned.1.call-done = bf16[184,2304]{1,0:T(8,128)(2,1)} async-done(((bf16[1472,2304]{1,0:T(8,128)(2,1)}), bf16[184,2304]{1,0:T(8,128)(2,1)}) %reduce-scatter.5.cloned.1.call-update) | async-done | bytes 847888 | tf_op jit(solution)/shard_map/reduce_scatter | solution.py:495
  809.7 45.5 %all-reduce.6 = (f32[184,2304]{1,0:T(8,128)S(1)}, f32[96,1472]{1,0:T(8,128)}) all-reduce(bf16[184,2304]{1,0:T(8,128)(2,1)} %reduce-scatter.5.cloned.1.call-done, bf16[96,1472]{1,0:T(8,128)(2,1)S(1)} %copy-done.30), channel_id=1, replica_groups=mesh['tgt'=8,'mem'=4] {'mem'}, use_global_device_ids=true, to_apply=%region_15.16 | all-reduce | flops 565248 | bytes 3391488 | tf_op jit(solution)/shard_map/psum | solution.py:644
  (276 shorter events, 177.2 us)
Async XLA Ops:
  7.2 34.1 %copy-start = (bf16[448,1472]{1,0:T(8,128)(2,1)S(1)}, bf16[448,1472]{1,0:T(8,128)(2,1)}, u32[]{:S(2)}) copy-start(bf16[448,1472]{1,0:T(8,128)(2,1)} %param.40) | copy-start | bytes 3956740
  7.2 114.7 %all-gather.9.cloned.1.call-start = ((), (), s32[]{:S(2)}) async-start(), calls=%async_computation.4 | async-start | bytes 7630848 | tf_op jit(solution)/shard_map/all_gather | solution.py:491
  13.9 149.4 %all-gather.11.cloned.1.call-start = ((), (), s32[]{:S(2)}) async-start(), calls=%async_computation.5 | async-start | bytes 1327104 | tf_op jit(solution)/shard_map/all_gather | solution.py:491
  14.6 192.7 %all-gather.13.cloned.1.call-start = ((), (), s32[]{:S(2)}) async-start(), calls=%async_computation.6 | async-start | bytes 1327104 | tf_op jit(solution)/shard_map/all_gather | solution.py:491
  15.4 277.6 %all-gather.15.cloned.1.call-start = ((), (), s32[]{:S(2)}) async-start(), calls=%async_computation.7 | async-start | bytes 5935104 | tf_op jit(solution)/shard_map/all_gather | solution.py:491
  36.1 313.1 %all-gather.17.cloned.1.call-start = ((), (), s32[]{:S(2)}) async-start(), calls=%async_computation.8 | async-start | bytes 3096576 | tf_op jit(solution)/shard_map/all_gather | solution.py:491
  38.3 28.2 %collective-permute-start.8 = (bf16[384,1472]{0,1:T(8,128)(2,1)}, bf16[384,1472]{0,1:T(8,128)(2,1)}, u32[]{:S(2)}, u32[]{:S(2)}) collective-permute-start(bf16[384,1472]{0,1:T(8,128)(2,1)} %copy.115), channel_id=1, source_target_pairs={{0,2},{1,3},{2,0},{3,1},{4,6},{5,7},{6,4},{7,5},{8,10},{9,11},{10,... | collective-permute-start | bytes 3391496 | tf_op jit(solution)/shard_map/ppermute | solution.py:475
  41.2 173.0 %collective-permute-start.6 = (bf16[384,1472]{0,1:T(8,128)(2,1)}, bf16[384,1472]{0,1:T(8,128)(2,1)}, u32[]{:S(2)}, u32[]{:S(2)}) collective-permute-start(bf16[384,1472]{0,1:T(8,128)(2,1)} %copy.115), channel_id=1, source_target_pairs={{0,1},{1,0},{2,3},{3,2},{4,5},{5,4},{6,7},{7,6},{8,9},{9,8},{10,11... | collective-permute-start | bytes 3391496 | tf_op jit(solution)/shard_map/ppermute | solution.py:475
  42.0 488.6 %reduce-scatter.11.cloned.1.call-start = ((), (), s32[]{:S(2)}) async-start(), calls=%async_computation.12 | async-start | bytes 3096576 | tf_op jit(solution)/shard_map/reduce_scatter | solution.py:495
  48.7 83.7 %copy-start.9 = (f32[384,1472]{0,1:T(8,128)}, f32[384,1472]{0,1:T(8,128)S(1)}, u32[]{:S(2)}) copy-start(f32[384,1472]{0,1:T(8,128)S(1)} %copy.107) | copy-start | bytes 6782980
  66.5 152.7 %collective-permute-start.9 = (bf16[384,1472]{0,1:T(8,128)(2,1)}, bf16[384,1472]{0,1:T(8,128)(2,1)}, u32[]{:S(2)}, u32[]{:S(2)}) collective-permute-start(bf16[384,1472]{0,1:T(8,128)(2,1)} %collective-permute-done.8), channel_id=1, source_target_pairs={{0,1},{1,0},{2,3},{3,2},{4,5},{5,4},{6,7},{7,6},{8,9},{9,8},{10,11... | collective-permute-start | bytes 3391496 | tf_op jit(solution)/shard_map/ppermute | solution.py:475
  212.9 27.9 %collective-permute-start.2 = (bf16[384,1472]{0,1:T(8,128)(2,1)}, bf16[384,1472]{0,1:T(8,128)(2,1)}, u32[]{:S(2)}, u32[]{:S(2)}) collective-permute-start(bf16[384,1472]{0,1:T(8,128)(2,1)} %multiply_convert_fusion.3), channel_id=1, source_target_pairs={{0,2},{1,3},{2,0},{3,1},{4,6},{5,7},{6,4},{7,5},{8,10},{9,11},{10,... | collective-permute-start | bytes 3391496 | tf_op jit(solution)/shard_map/ppermute | solution.py:475
  213.4 79.5 %collective-permute-start = (bf16[384,1472]{0,1:T(8,128)(2,1)}, bf16[384,1472]{0,1:T(8,128)(2,1)}, u32[]{:S(2)}, u32[]{:S(2)}) collective-permute-start(bf16[384,1472]{0,1:T(8,128)(2,1)} %multiply_convert_fusion.3), channel_id=1, source_target_pairs={{0,1},{1,0},{2,3},{3,2},{4,5},{5,4},{6,7},{7,6},{8,9},{9,8},{10,11... | collective-permute-start | bytes 3391496 | tf_op jit(solution)/shard_map/ppermute | solution.py:475
  240.7 120.6 %collective-permute-start.3 = (bf16[384,1472]{0,1:T(8,128)(2,1)}, bf16[384,1472]{0,1:T(8,128)(2,1)}, u32[]{:S(2)}, u32[]{:S(2)}) collective-permute-start(bf16[384,1472]{0,1:T(8,128)(2,1)} %collective-permute-done.2), channel_id=1, source_target_pairs={{0,1},{1,0},{2,3},{3,2},{4,5},{5,4},{6,7},{7,6},{8,9},{9,8},{10,11... | collective-permute-start | bytes 3391496 | tf_op jit(solution)/shard_map/ppermute | solution.py:475
  384.1 175.9 %reduce-scatter.9.cloned.1.call-start = ((), (), s32[]{:S(2)}) async-start(), calls=%async_computation.11 | async-start | bytes 5935104 | tf_op jit(solution)/shard_map/reduce_scatter | solution.py:495
  397.3 255.5 %reduce-scatter.7.cloned.1.call-start = ((), (), s32[]{:S(2)}) async-start(), calls=%async_computation.10 | async-start | bytes 2654208 | tf_op jit(solution)/shard_map/reduce_scatter | solution.py:495
  405.2 10.1 %collective-permute-start.10 = (bf16[384,1472]{0,1:T(8,128)(2,1)S(1)}, bf16[384,1472]{0,1:T(8,128)(2,1)S(1)}, u32[]{:S(2)}, u32[]{:S(2)}) collective-permute-start(bf16[384,1472]{0,1:T(8,128)(2,1)S(1)} %slice.227), channel_id=1, source_target_pairs={{0,1},{1,0},{2,3},{3,2},{4,5},{5,4},{6,7},{7,6},{8,9},{9,8},{10,11... | collective-permute-start | bytes 3391496 | tf_op jit(solution)/shard_map/ppermute | solution.py:475
  411.9 9.8 %collective-permute-start.7 = (bf16[384,1472]{0,1:T(8,128)(2,1)S(1)}, bf16[384,1472]{0,1:T(8,128)(2,1)S(1)}, u32[]{:S(2)}, u32[]{:S(2)}) collective-permute-start(bf16[384,1472]{0,1:T(8,128)(2,1)S(1)} %slice.228), channel_id=1, source_target_pairs={{0,1},{1,0},{2,3},{3,2},{4,5},{5,4},{6,7},{7,6},{8,9},{9,8},{10,11... | collective-permute-start | bytes 3391496 | tf_op jit(solution)/shard_map/ppermute | solution.py:475
  415.0 4.9 collective-permute-start.4
  415.5 27.8 %collective-permute-start.11 = (bf16[384,1472]{0,1:T(8,128)(2,1)S(1)}, bf16[384,1472]{0,1:T(8,128)(2,1)S(1)}, u32[]{:S(2)}, u32[]{:S(2)}) collective-permute-start(bf16[384,1472]{0,1:T(8,128)(2,1)S(1)} %fusion.26), channel_id=1, source_target_pairs={{0,2},{1,3},{2,0},{3,1},{4,6},{5,7},{6,4},{7,5},{8,10},{9,11},{10,... | collective-permute-start | bytes 3391496 | tf_op jit(solution)/shard_map/ppermute | solution.py:475
  419.8 25.1 %collective-permute-start.1 = (bf16[384,1472]{0,1:T(8,128)(2,1)S(1)}, bf16[384,1472]{0,1:T(8,128)(2,1)S(1)}, u32[]{:S(2)}, u32[]{:S(2)}) collective-permute-start(bf16[384,1472]{0,1:T(8,128)(2,1)S(1)} %slice.230), channel_id=1, source_target_pairs={{0,1},{1,0},{2,3},{3,2},{4,5},{5,4},{6,7},{7,6},{8,9},{9,8},{10,11... | collective-permute-start | bytes 3391496 | tf_op jit(solution)/shard_map/ppermute | solution.py:475
  420.1 46.8 %collective-permute-start.5 = (bf16[384,1472]{0,1:T(8,128)(2,1)S(1)}, bf16[384,1472]{0,1:T(8,128)(2,1)S(1)}, u32[]{:S(2)}, u32[]{:S(2)}) collective-permute-start(bf16[384,1472]{0,1:T(8,128)(2,1)S(1)} %fusion.28), channel_id=1, source_target_pairs={{0,2},{1,3},{2,0},{3,1},{4,6},{5,7},{6,4},{7,5},{8,10},{9,11},{10,... | collective-permute-start | bytes 3391496 | tf_op jit(solution)/shard_map/ppermute | solution.py:475
  421.7 45.2 %copy-start.15 = (bf16[384,1472]{0,1:T(8,128)(2,1)S(1)}, bf16[384,1472]{0,1:T(8,128)(2,1)}, u32[]{:S(2)}) copy-start(bf16[384,1472]{0,1:T(8,128)(2,1)} %copy.115) | copy-start | bytes 3391492
  444.8 26.0 %copy-start.14 = (bf16[384,1472]{1,0:T(8,128)(2,1)S(1)}, bf16[384,1472]{1,0:T(8,128)(2,1)}, u32[]{:S(2)}) copy-start(bf16[384,1472]{1,0:T(8,128)(2,1)} %all-gather.13.cloned.1.call-done) | copy-start | bytes 3391492
  444.9 26.0 %copy-start.16 = (bf16[2,192,384]{2,1,0:T(8,128)(2,1)S(1)}, bf16[2,192,384]{2,1,0:T(8,128)(2,1)}, u32[]{:S(2)}) copy-start(bf16[2,192,384]{2,1,0:T(8,128)(2,1)} %get-tuple-element.26) | copy-start | bytes 884740
  482.5 35.1 %copy-start.36 = (f32[384]{0:T(512)S(1)}, f32[384]{0:T(512)}, u32[]{:S(2)}) copy-start(f32[384]{0:T(512)} %copy-done.35) | copy-start | bytes 4612
  530.5 29.5 %copy-start.11 = (bf16[2,189,1472]{2,0,1:T(2,128)(2,1)S(1)}, bf16[2,189,1472]{2,0,1:T(2,128)(2,1)}, u32[]{:S(2)}) copy-start(bf16[2,189,1472]{2,0,1:T(2,128)(2,1)} %param.21) | copy-start | bytes 3338500
  530.5 29.5 %copy-start.34 = (f32[1472]{0:T(1024)S(1)}, f32[1472]{0:T(1024)}, u32[]{:S(2)}) copy-start(f32[1472]{0:T(1024)} %convert_element_type.185) | copy-start | bytes 17668
  530.6 122.2 %all-gather.19.cloned.1.call-start = ((), (), s32[]{:S(2)}) async-start(), calls=%async_computation.13 | async-start | bytes 1720320 | tf_op jit(solution)/shard_map/all_gather | solution.py:605
  531.3 148.4 %all-gather.21.cloned.1.call-start = ((), (), s32[]{:S(2)}) async-start(), calls=%async_computation.14 | async-start | bytes 3297280 | tf_op jit(solution)/shard_map/all_gather | solution.py:604
  560.0 249.7 %reduce-scatter.5.cloned.1.call-start = ((), (), s32[]{:S(2)}) async-start(), calls=%async_computation.9 | async-start | bytes 7630848 | tf_op jit(solution)/shard_map/reduce_scatter | solution.py:495
  702.9 106.9 %copy-start.30 = (bf16[96,1472]{1,0:T(8,128)(2,1)S(1)}, bf16[96,1472]{1,0:T(8,128)(2,1)}, u32[]{:S(2)}) copy-start(bf16[96,1472]{1,0:T(8,128)(2,1)} %reduce-scatter.7.cloned.1.call-done) | copy-start | bytes 847876
  (57 other events, 273.3 us)
Sparse Core Ops, SparseCore 0:
  14.0 107.8 all-gather.8
  124.1 39.1 all-gather.10
  165.5 39.8 all-gather.12
  207.5 85.4 all-gather.14
  295.0 54.2 all-gather.16
  384.2 69.4 reduce-scatter.10
  457.7 102.2 reduce-scatter.8
  564.4 68.2 reduce-scatter.6
  634.3 17.8 all-gather.18
  653.7 25.9 all-gather.20
  683.8 125.8 reduce-scatter.4

commit v2 on v1

--- a/solution.py
+++ b/solution.py
@@ -27,6 +27,7 @@
 VMEM_SPEC = pl.BlockSpec(memory_space=pltpu.VMEM)
 ANY_SPEC = pl.BlockSpec(memory_space=pl.ANY)
 VMEM_CAP = 56 * 1024 * 1024
+FFN_CAP = 62 * 1024 * 1024
 
 
 def distance_onehot():
@@ -471,6 +472,620 @@
     )(all_queries, back, stats, keys, values, bias)
 
 
+CUBIC = 0.044715
+ROOT = float(np.sqrt(2.0 / np.pi))
+
+
+def strips(width, step):
+    return [(start, min(step, width - start)) for start in range(0, width, step)]
+
+
+def ffn_kernel(
+    h_ref, up0_ref, up1_ref, up2_ref, up3_ref, gate_up_ref, down_ref,
+    h_back_ref, near_ref, far_ref, grad_gu_ref, grad_down_ref,
+    h_all, u_all, hidden, two_back, h_part, y_part, h_in, y_in,
+    h_send, h_recv, d_send, d_recv, y_send, y_recv,
+):
+    tokens, model = h_ref.shape
+    units = down_ref.shape[0]
+    greet("mem", (1, 2))
+    h_to_core = send(h_ref, h_all.at[1], h_send.at[0], h_recv.at[0], 1)
+    h_to_far = send(h_ref, h_all.at[2], h_send.at[1], h_recv.at[1], 2)
+    h_relay = send(h_all.at[2], h_all.at[3], h_send.at[2], h_recv.at[2], 1)
+    d_near = send(h_part.at[1], h_in.at[0], d_send.at[0], d_recv.at[0], 1)
+    d_pass = send(h_part.at[3], h_in.at[1], d_send.at[1], d_recv.at[1], 1)
+    d_far = send(h_part.at[2], h_in.at[2], d_send.at[2], d_recv.at[2], 2)
+    y_near = send(y_part.at[1], y_in.at[0], y_send.at[0], y_recv.at[0], 1)
+    y_pass = send(y_part.at[3], y_in.at[1], y_send.at[1], y_recv.at[1], 1)
+    h_to_far.start()
+    h_to_core.start()
+    h_all[0] = h_ref[...]
+    u_all[0] = up0_ref[...]
+    u_all[1] = up1_ref[...]
+    u_all[2] = up2_ref[...]
+    u_all[3] = up3_ref[...]
+
+    def token_block(slot, carry):
+        @pl.when(slot == 1)
+        def _():
+            h_to_core.wait_recv()
+
+        @pl.when(slot == 2)
+        def _():
+            d_near.start()
+            y_near.start()
+            h_to_far.wait_recv()
+            h_relay.start()
+
+        @pl.when(slot == 3)
+        def _():
+            h_relay.wait_recv()
+
+        def units_block(block, inside):
+            pairs = pl.ds(pl.multiple_of(block * 256, 256), 256)
+            ones = pl.ds(pl.multiple_of(block * 128, 128), 128)
+            both = dot(h_all[slot], gate_up_ref[:, pairs])
+            back = dot_nt(u_all[slot], down_ref[ones, :]).astype(BF).astype(F32)
+            gate, up = both[:, :128], both[:, 128:]
+            square = gate * gate
+            bend = jnp.tanh(ROOT * gate * (1.0 + CUBIC * square))
+            share = 0.5 * (1.0 + bend)
+            active = gate * share
+            slope = share + 0.5 * gate * (1.0 - bend * bend) * (
+                ROOT * (1.0 + 3.0 * CUBIC * square)
+            )
+            hidden[slot, :, ones] = (active * up).astype(BF)
+            two_back[slot, :, pairs] = jnp.concatenate(
+                [(back * up * slope).astype(BF), (back * active).astype(BF)], axis=1
+            )
+            return inside
+
+        lax.fori_loop(0, units // 128, units_block, 0)
+        for start, width in strips(model, 256):
+            part = slice(start, start + width)
+            h_part[slot, :, part] = dot_nt(two_back[slot], gate_up_ref[part, :]).astype(BF)
+            y_part[slot, :, part] = dot(hidden[slot], down_ref[:, part]).astype(BF)
+        return carry
+
+    lax.fori_loop(0, 4, token_block, 0)
+    d_pass.start()
+    y_pass.start()
+    d_pass.wait_recv()
+    h_part[2] = (h_part[2].astype(F32) + h_in[1].astype(F32)).astype(BF)
+    d_far.start()
+    count = 4 * tokens
+    for start, width in strips(model, 256):
+        part = slice(start, start + width)
+        grad_gu_ref[part, :] = dot_tn(
+            h_all[:, :, part].reshape(count, width), two_back[...].reshape(count, 2 * units)
+        ).astype(BF)
+    for start, width in strips(units, 256):
+        part = slice(start, start + width)
+        grad_down_ref[part, :] = dot_tn(
+            hidden[:, :, part].reshape(count, width), u_all[...].reshape(count, model)
+        ).astype(BF)
+    y_pass.wait_recv()
+    far_ref[...] = (y_part[2].astype(F32) + y_in[1].astype(F32)).astype(BF)
+    y_near.wait_recv()
+    near_ref[...] = (y_part[0].astype(F32) + y_in[0].astype(F32)).astype(BF)
+    d_near.wait_recv()
+    d_far.wait_recv()
+    h_back_ref[...] = (
+        h_part[0].astype(F32) + h_in[0].astype(F32) + h_in[2].astype(F32)
+    )
+    for copy in (h_to_core, h_to_far, h_relay, d_near, d_pass, d_far, y_near, y_pass):
+        copy.wait_send()
+
+
+def ffn(h3, upstreams, gate_up, down):
+    tokens, model = h3.shape
+    units = down.shape[0]
+    every = (4, tokens, model)
+    flops = 4 * tokens * model * units * 18
+    return pl.pallas_call(
+        ffn_kernel,
+        out_shape=(
+            jax.ShapeDtypeStruct((tokens, model), F32),
+            jax.ShapeDtypeStruct((tokens, model), BF),
+            jax.ShapeDtypeStruct((tokens, model), BF),
+            jax.ShapeDtypeStruct((model, 2 * units), BF),
+            jax.ShapeDtypeStruct((units, model), BF),
+        ),
+        in_specs=[VMEM_SPEC] * 7,
+        out_specs=(VMEM_SPEC,) * 5,
+        scratch_shapes=[
+            pltpu.VMEM(every, BF),
+            pltpu.VMEM(every, BF),
+            pltpu.VMEM((4, tokens, units), BF),
+            pltpu.VMEM((4, tokens, 2 * units), BF),
+            pltpu.VMEM(every, BF),
+            pltpu.VMEM(every, BF),
+            pltpu.VMEM((3, tokens, model), BF),
+            pltpu.VMEM((2, tokens, model), BF),
+            pltpu.SemaphoreType.DMA((3,)),
+            pltpu.SemaphoreType.DMA((3,)),
+            pltpu.SemaphoreType.DMA((3,)),
+            pltpu.SemaphoreType.DMA((3,)),
+            pltpu.SemaphoreType.DMA((2,)),
+            pltpu.SemaphoreType.DMA((2,)),
+        ],
+        compiler_params=pltpu.CompilerParams(
+            collective_id=3, has_side_effects=True, vmem_limit_bytes=FFN_CAP
+        ),
+        cost_estimate=pl.CostEstimate(
+            flops=flops, bytes_accessed=32 * 1024 * 1024, transcendentals=4 * tokens * units
+        ),
+        name="feed_forward",
+    )(h3, *upstreams, gate_up, down)
+
+
+def peer_copy(src, dst, send_sem, recv_sem, tgt=None, mem=None):
+    where = {}
+    if tgt is not None:
+        where["tgt"] = tgt
+    if mem is not None:
+        where["mem"] = mem
+    return pltpu.make_async_remote_copy(
+        src_ref=src, dst_ref=dst, send_sem=send_sem, recv_sem=recv_sem,
+        device_id=where, device_id_type=MESH,
+    )
+
+
+def greet_all(mem, tgt):
+    barrier = pltpu.get_barrier_semaphore()
+    for offset in (1, 2):
+        pl.semaphore_signal(
+            barrier, inc=1, device_id={"mem": jnp.bitwise_xor(mem, offset)}, device_id_type=MESH
+        )
+    for offset in (1, 2, 4, 6):
+        pl.semaphore_signal(
+            barrier, inc=1, device_id={"tgt": jnp.bitwise_xor(tgt, offset)}, device_id_type=MESH
+        )
+    pl.semaphore_wait(barrier, 6)
+
+
+FIRST = (1, 2, 4, 6)
+PASSED = (3, 5, 7)
+
+
+def gather_kernel(
+    self_q, self_k, self_v, cross_q, cross_k, cross_v, self_o, cross_o,
+    qkv_out, kv_out, cq_out, so_out, co_out,
+    t_send, t_recv, x_send, x_recv, c_send, c_recv, r_send, r_recv, own_sem,
+):
+    mem = lax.axis_index("mem")
+    tgt = lax.axis_index("tgt")
+    inner = HEADS * HEAD
+
+    def part(out, index):
+        return lambda place: out.at[place, :, index * inner : (index + 1) * inner]
+
+    def whole(out):
+        return lambda place: out.at[place]
+
+    groups = (
+        ((self_q, part(qkv_out, 0)), (self_k, part(qkv_out, 1))),
+        ((self_v, part(qkv_out, 2)), (cross_q, part(cq_out, 0))),
+        ((cross_k, part(kv_out, 0)), (cross_v, part(kv_out, 1))),
+        ((self_o, whole(so_out)), (cross_o, whole(co_out))),
+    )
+    greet_all(mem, tgt)
+    near = jnp.bitwise_xor(mem, 1)
+    far = jnp.bitwise_xor(mem, 2)
+
+    def over_tgt(member, number, step, offset):
+        src, dst = member
+        if step < 4:
+            return peer_copy(
+                src, dst(tgt), t_send.at[step, number], t_recv.at[step, number],
+                tgt=jnp.bitwise_xor(tgt, offset),
+            )
+        place = jnp.bitwise_xor(tgt, offset - 1)
+        return peer_copy(
+            dst(place), dst(place), t_send.at[step, number], t_recv.at[step, number],
+            tgt=jnp.bitwise_xor(tgt, 1),
+        )
+
+    def over_far(member, number, step, offset):
+        dst = member[1](jnp.bitwise_xor(tgt, offset))
+        return peer_copy(dst, dst, x_send.at[step, number], x_recv.at[step, number], mem=far)
+
+    def over_near(member, number, step, offset):
+        dst = member[1](jnp.bitwise_xor(tgt, offset))
+        return peer_copy(dst, dst, c_send.at[step, number], c_recv.at[step, number], mem=near)
+
+    def relay(member, number, step, offset):
+        dst = member[1](jnp.bitwise_xor(tgt, offset))
+        return peer_copy(dst, dst, r_send.at[step, number], r_recv.at[step, number], mem=near)
+
+    steps = list(enumerate(FIRST + PASSED))
+    for index, group in enumerate(groups):
+
+        @pl.when(mem == index)
+        def _(index=index, group=group):
+            members = list(enumerate(group))
+            for step, offset in steps[:4]:
+                for number, member in members:
+                    over_tgt(member, number, step, offset).start()
+            own = []
+            for place, (src, dst) in enumerate(member for all_of in groups for member in all_of):
+                own.append(pltpu.make_async_copy(src, dst(tgt), own_sem.at[place]))
+                own[-1].start()
+            for step, offset in steps:
+                for number, member in members:
+                    over_tgt(member, number, step, offset).wait_recv()
+                    if 0 < step < 4:
+                        over_tgt(member, number, step + 3, offset + 1).start()
+                    over_far(member, number, step, offset).start()
+                    over_near(member, number, step, offset).start()
+            far_members = list(enumerate(groups[index ^ 2]))
+            near_members = list(enumerate(groups[index ^ 1]))
+            last_members = list(enumerate(groups[index ^ 3]))
+            for step, offset in steps:
+                for number, member in far_members:
+                    over_far(member, number, step, offset).wait_recv()
+                    relay(member, number, step, offset).start()
+            for step, offset in steps:
+                for number, member in near_members:
+                    over_near(member, number, step, offset).wait_recv()
+                for number, member in last_members:
+                    relay(member, number, step, offset).wait_recv()
+                for number, member in members:
+                    over_tgt(member, number, step, offset).wait_send()
+                    over_far(member, number, step, offset).wait_send()
+                    over_near(member, number, step, offset).wait_send()
+                for number, member in far_members:
+                    relay(member, number, step, offset).wait_send()
+            for copy in own:
+                copy.wait()
+
+
+def gather_weights(weights):
+    tgts = lax.axis_size("tgt")
+    rows, inner = weights[0].shape
+    o_rows, model = weights[-1].shape
+
+    def out(columns, height=rows):
+        return jax.ShapeDtypeStruct((tgts, height, columns), BF)
+
+    shapes = (out(3 * inner), out(2 * inner), out(inner), out(model, o_rows), out(model, o_rows))
+    sems = [pltpu.SemaphoreType.DMA((7, 2))] * 8
+    return pl.pallas_call(
+        gather_kernel,
+        out_shape=shapes,
+        in_specs=[ANY_SPEC] * 8,
+        out_specs=(ANY_SPEC,) * 5,
+        scratch_shapes=sems + [pltpu.SemaphoreType.DMA((8,))],
+        compiler_params=pltpu.CompilerParams(collective_id=4, has_side_effects=True),
+        cost_estimate=pl.CostEstimate(
+            flops=0, bytes_accessed=150 * 1024 * 1024, transcendentals=0
+        ),
+        name="gather_weights",
+    )(*weights)
+
+
+TURNS = (7, 6, 5, 4, 3, 2, 1, 0)
+
+
+def reduce_kernel(
+    qkv_ref, kv_ref, cq_ref, so_ref, co_ref, small_ref,
+    q_out, k_out, v_out, cq_out, ck_out, cv_out, so_out, co_out, small_out,
+    small_in, s_send, s_recv,
+    wide_in, tall_in, wide_x, tall_x, wide_y, tall_y, wide_z, tall_z, wide_e, tall_e,
+    a_send, a_recv, b_send, b_recv, x_send, x_recv, y_send, y_recv, z_send, z_recv,
+    e_send, e_recv,
+):
+    mem = lax.axis_index("mem")
+    tgt = lax.axis_index("tgt")
+    inner = HEADS * HEAD
+
+    def part(ref, index):
+        return lambda place: ref.at[place, :, index * inner : (index + 1) * inner]
+
+    def whole(ref):
+        return lambda place: ref.at[place]
+
+    wide = (wide_in, wide_x, wide_y, wide_z, wide_e)
+    tall = (tall_in, tall_x, tall_y, tall_z, tall_e)
+    groups = (
+        ((part(qkv_ref, 0), q_out, wide), (part(qkv_ref, 1), k_out, wide)),
+        ((part(qkv_ref, 2), v_out, wide), (part(cq_ref, 0), cq_out, wide)),
+        ((part(kv_ref, 0), ck_out, wide), (part(kv_ref, 1), cv_out, wide)),
+        ((whole(so_ref), so_out, tall), (whole(co_ref), co_out, tall)),
+    )
+    greet_all(mem, tgt)
+    near = jnp.bitwise_xor(mem, 1)
+    far = jnp.bitwise_xor(mem, 2)
+
+    def to_near(member, number, step, lane):
+        place = jnp.bitwise_xor(tgt, TURNS[step])
+        send_sems, recv_sems = ((a_send, a_recv), (b_send, b_recv))[lane]
+        return peer_copy(
+            member[0](place), member[2][0].at[lane, step, number],
+            send_sems.at[step, number], recv_sems.at[step, number], mem=near,
+        )
+
+    def to_far(member, number, step):
+        buffer = member[2][1]
+        return peer_copy(
+            buffer.at[0, step, number], buffer.at[1, step, number],
+            x_send.at[step, number], x_recv.at[step, number], mem=far,
+        )
+
+    def to_side(member, number, turn):
+        buffer = member[2][2]
+        return peer_copy(
+            buffer.at[0, turn, number], buffer.at[1, turn, number],
+            y_send.at[turn, number], y_recv.at[turn, number], tgt=jnp.bitwise_xor(tgt, 1),
+        )
+
+    def to_owner(member, number, turn):
+        buffer = member[2][3]
+        return peer_copy(
+            buffer.at[0, turn, number], buffer.at[1, turn, number],
+            z_send.at[turn, number], z_recv.at[turn, number],
+            tgt=jnp.bitwise_xor(tgt, TURNS[2 * turn + 1]),
+        )
+
+    def to_all(member, number, lane, peer):
+        buffer = member[2][4]
+        return peer_copy(
+            buffer.at[2 if lane == 2 else 0, number],
+            buffer.at[(1, 2, 3)[lane], number],
+            e_send.at[lane, number], e_recv.at[lane, number], mem=peer,
+        )
+
+    partners = (
+        {"mem": near}, {"mem": far}, {"tgt": jnp.bitwise_xor(tgt, 1)},
+        {"tgt": jnp.bitwise_xor(tgt, 2)}, {"tgt": jnp.bitwise_xor(tgt, 4)},
+    )
+    small_moves = [
+        peer_copy(small_in.at[0, step], small_in.at[1, step], s_send.at[step], s_recv.at[step], **to)
+        for step, to in enumerate(partners)
+    ]
+
+    for index, group in enumerate(groups):
+
+        @pl.when(mem == index)
+        def _(index=index, group=group):
+            mine = list(enumerate(group))
+            near_group = list(enumerate(groups[index ^ 1]))
+            far_group = list(enumerate(groups[index ^ 2]))
+            last_group = list(enumerate(groups[index ^ 3]))
+            steps = range(len(TURNS))
+            for step in steps:
+                for number, member in last_group:
+                    to_near(member, number, step, 1).start()
+                for number, member in near_group:
+                    to_near(member, number, step, 0).start()
+            for step in steps:
+                place = jnp.bitwise_xor(tgt, TURNS[step])
+                for number, member in far_group:
+                    to_near(member, number, step, 1).wait_recv()
+                    member[2][1][0, step, number] = (
+                        member[0](place)[...].astype(F32)
+                        + member[2][0][1, step, number].astype(F32)
+                    ).astype(BF)
+                    to_far(member, number, step).start()
+            small_in[0, 0] = small_ref[...]
+            for step, move in enumerate(small_moves):
+                move.start()
+                move.wait_recv()
+                total = small_in[0, step] + small_in[1, step]
+                if step + 1 < len(small_moves):
+                    small_in[0, step + 1] = total
+                else:
+                    small_out[...] = total
+            for step in steps:
+                place = jnp.bitwise_xor(tgt, TURNS[step])
+                turn = step // 2
+                for number, member in mine:
+                    to_near(member, number, step, 0).wait_recv()
+                    to_far(member, number, step).wait_recv()
+                    total = (
+                        member[0](place)[...].astype(F32)
+                        + member[2][0][0, step, number].astype(F32)
+                        + member[2][1][1, step, number].astype(F32)
+                    )
+                    if step % 2 == 0:
+                        member[2][2][0, turn, number] = total.astype(BF)
+                        to_side(member, number, turn).start()
+                        continue
+                    to_side(member, number, turn).wait_recv()
+                    total = total + member[2][2][1, turn, number].astype(F32)
+                    if turn < 3:
+                        member[2][3][0, turn, number] = total.astype(BF)
+                        to_owner(member, number, turn).start()
+                        continue
+                    for other in range(3):
+                        to_owner(member, number, other).wait_recv()
+                        total = total + member[2][3][1, other, number].astype(F32)
+                    member[2][4][0, number] = total.astype(BF)
+                    to_all(member, number, 1, far).start()
+                    to_all(member, number, 0, near).start()
+                    member[1][...] = member[2][4][0, number]
+            for number, member in far_group:
+                to_all(member, number, 1, far).wait_recv()
+                to_all(member, number, 2, near).start()
+                member[1][...] = member[2][4][2, number]
+            for number, member in near_group:
+                to_all(member, number, 0, near).wait_recv()
+                member[1][...] = member[2][4][1, number]
+            for number, member in last_group:
+                to_all(member, number, 2, near).wait_recv()
+                member[1][...] = member[2][4][3, number]
+            for move in small_moves:
+                move.wait_send()
+            for step in steps:
+                for number, member in last_group:
+                    to_near(member, number, step, 1).wait_send()
+                for number, member in near_group:
+                    to_near(member, number, step, 0).wait_send()
+                for number, member in far_group:
+                    to_far(member, number, step).wait_send()
+            for number, member in mine:
+                for turn in range(4):
+                    to_side(member, number, turn).wait_send()
+                for turn in range(3):
+                    to_owner(member, number, turn).wait_send()
+                to_all(member, number, 0, near).wait_send()
+                to_all(member, number, 1, far).wait_send()
+            for number, member in far_group:
+                to_all(member, number, 2, near).wait_send()
+
+
+def reduce_weights(d_qkv, d_kv, d_cq, d_so, d_co, small):
+    rows, inner = d_cq.shape[1:]
+    o_rows, model = d_so.shape[1:]
+    wide, tall = (rows, inner), (o_rows, model)
+    scratch = []
+    for lead in ((2, 8, 2), (2, 8, 2), (2, 4, 2), (2, 3, 2), (4, 2)):
+        scratch += [pltpu.VMEM(lead + wide, BF), pltpu.VMEM(lead + tall, BF)]
+    sems = []
+    for count in (8, 8, 8, 4, 3, 3):
+        sems += [pltpu.SemaphoreType.DMA((count, 2))] * 2
+    return pl.pallas_call(
+        reduce_kernel,
+        out_shape=tuple(jax.ShapeDtypeStruct(wide, BF) for _ in range(6))
+        + tuple(jax.ShapeDtypeStruct(tall, BF) for _ in range(2))
+        + (jax.ShapeDtypeStruct(small.shape, F32),),
+        in_specs=[VMEM_SPEC] * 6,
+        out_specs=(VMEM_SPEC,) * 9,
+        scratch_shapes=[pltpu.VMEM((2, 5) + small.shape, F32)]
+        + [pltpu.SemaphoreType.DMA((5,))] * 2
+        + scratch
+        + sems,
+        compiler_params=pltpu.CompilerParams(
+            collective_id=5, has_side_effects=True, vmem_limit_bytes=VMEM_CAP
+        ),
+        cost_estimate=pl.CostEstimate(
+            flops=0, bytes_accessed=150 * 1024 * 1024, transcendentals=0
+        ),
+        name="reduce_weights",
+    )(d_qkv, d_kv, d_cq, d_so, d_co, small)
+
+
+def pick_kernel(tgts, groups, gate_ref, up_ref, out_ref):
+    mem = lax.axis_index("mem")
+    shard = gate_ref.shape[1] // tgts
+    piece = shard // groups
+
+    for group in range(groups):
+
+        @pl.when(mem == group)
+        def _(group=group):
+            for number, ref in enumerate((gate_ref, up_ref)):
+                parts = []
+                for place in range(tgts):
+                    start = place * shard + group * piece
+                    parts.append(ref[:, start : start + piece].astype(F32))
+                quarter = jnp.concatenate(parts, axis=1).astype(BF)
+                for block in range(quarter.shape[1] // 128):
+                    start = block * 256 + number * 128
+                    out_ref[:, start : start + 128] = quarter[:, block * 128 : block * 128 + 128]
+
+
+def pick_units(gate, up):
+    groups, tgts = lax.axis_size("mem"), lax.axis_size("tgt")
+    rows, units = gate.shape
+    return pl.pallas_call(
+        functools.partial(pick_kernel, tgts, groups),
+        out_shape=jax.ShapeDtypeStruct((rows, 2 * units // groups), BF),
+        in_specs=[VMEM_SPEC] * 2,
+        out_specs=VMEM_SPEC,
+        compiler_params=pltpu.CompilerParams(vmem_limit_bytes=VMEM_CAP),
+        name="pick_units",
+    )(gate, up)
+
+
+def place_kernel(tgts, groups, parts_ref, gate_ref, up_ref):
+    units = gate_ref.shape[1]
+    piece = units // tgts // groups
+    for number, ref in enumerate((gate_ref, up_ref)):
+        quarters = []
+        for group in range(groups):
+            blocks = [
+                parts_ref[group, :, start : start + 128]
+                for start in range(number * 128, 2 * units // groups, 256)
+            ]
+            quarters.append(jnp.concatenate(blocks, axis=1).astype(F32))
+        ref[...] = jnp.concatenate(
+            [
+                quarters[group][:, place * piece : (place + 1) * piece]
+                for place in range(tgts)
+                for group in range(groups)
+            ],
+            axis=1,
+        )
+
+
+def place_units(parts):
+    groups, tgts = lax.axis_size("mem"), lax.axis_size("tgt")
+    rows, columns = parts.shape[1:]
+    shape = jax.ShapeDtypeStruct((rows, groups * columns // 2), F32)
+    return pl.pallas_call(
+        functools.partial(place_kernel, tgts, groups),
+        out_shape=(shape, shape),
+        in_specs=[VMEM_SPEC],
+        out_specs=(VMEM_SPEC, VMEM_SPEC),
+        compiler_params=pltpu.CompilerParams(vmem_limit_bytes=VMEM_CAP),
+        name="place_units",
+    )(parts)
+
+
+def share_kernel(wide_ref, tall_ref, wide_out, tall_out, wide_send, wide_recv, tall_send, tall_recv, own):
+    mem = lax.axis_index("mem")
+    greet("mem", (1, 2))
+    near = jnp.bitwise_xor(mem, 1)
+    far = jnp.bitwise_xor(mem, 2)
+    moves = []
+    for src, out, sends, recvs in (
+        (wide_ref, wide_out, wide_send, wide_recv),
+        (tall_ref, tall_out, tall_send, tall_recv),
+    ):
+        to_far = peer_copy(src, out.at[mem], sends.at[0], recvs.at[0], mem=far)
+        to_near = peer_copy(src, out.at[mem], sends.at[1], recvs.at[1], mem=near)
+        relay = peer_copy(out.at[far], out.at[far], sends.at[2], recvs.at[2], mem=near)
+        to_far.start()
+        to_near.start()
+        moves.append((to_far, to_near, relay))
+    copies = [
+        pltpu.make_async_copy(wide_ref, wide_out.at[mem], own.at[0]),
+        pltpu.make_async_copy(tall_ref, tall_out.at[mem], own.at[1]),
+    ]
+    for copy in copies:
+        copy.start()
+    for to_far, _, relay in moves:
+        to_far.wait_recv()
+        relay.start()
+    for to_far, to_near, relay in moves:
+        to_near.wait_recv()
+        relay.wait_recv()
+        to_far.wait_send()
+        to_near.wait_send()
+        relay.wait_send()
+    for copy in copies:
+        copy.wait()
+
+
+def share(wide, tall):
+    groups = lax.axis_size("mem")
+    return pl.pallas_call(
+        share_kernel,
+        out_shape=tuple(
+            jax.ShapeDtypeStruct((groups,) + value.shape, BF) for value in (wide, tall)
+        ),
+        in_specs=[ANY_SPEC] * 2,
+        out_specs=(ANY_SPEC,) * 2,
+        scratch_shapes=[pltpu.SemaphoreType.DMA((3,))] * 4 + [pltpu.SemaphoreType.DMA((2,))],
+        compiler_params=pltpu.CompilerParams(collective_id=6, has_side_effects=True),
+        cost_estimate=pl.CostEstimate(
+            flops=0, bytes_accessed=60 * 1024 * 1024, transcendentals=0
+        ),
+        name="share_sums",
+    )(wide, tall)
+
+
 def over_mem(value, offset):
     return lax.ppermute(value, "mem", [(i, i ^ offset) for i in range(4)])
 
@@ -481,18 +1096,39 @@
     return value, near, far, over_mem(far, 1)
 
 
-def owner_sum(own, near, far, far_near):
-    far = (far + over_mem(far_near.astype(BF), 1).astype(F32)).astype(BF)
-    total = own + over_mem(near.astype(BF), 1).astype(F32)
-    return total + over_mem(far, 2).astype(F32)
-
-
 def gather_tgt(shard):
     return lax.all_gather(shard, "tgt", axis=0, tiled=True)
 
 
 def scatter_tgt(partial):
     return lax.psum_scatter(partial, "tgt", scatter_dimension=0, tiled=True)
+
+
+def attention_weights(weights):
+    if lax.axis_size("tgt") == 8:
+        return gather_weights(weights)
+    parts = [lax.all_gather(weight, "tgt", axis=0) for weight in weights]
+    return (
+        jnp.concatenate(parts[:3], axis=-1),
+        jnp.concatenate(parts[4:6], axis=-1),
+        parts[3],
+        parts[6],
+        parts[7],
+    )
+
+
+def attention_sums(partials, small):
+    if lax.axis_size("tgt") == 8:
+        return reduce_weights(*partials, small)
+    inner = HEADS * HEAD
+    totals = [
+        lax.psum_scatter(partial, "tgt", scatter_dimension=0, tiled=False) for partial in partials
+    ]
+    qkv, kv, cq, so, co = lax.psum(totals, "mem")
+    return (
+        qkv[:, :inner], qkv[:, inner : 2 * inner], qkv[:, 2 * inner :], cq,
+        kv[:, :inner], kv[:, inner:], so, co, lax.psum(small, ("tgt", "mem")),
+    )
 
 
 def on_device(
@@ -517,20 +1153,6 @@
     def trimmed(value):
         return value.reshape(items, ROWS, model)[:, :seq]
 
-    def my_columns(weight):
-        parts = weight.reshape(shard_in, tgts, groups, piece)
-        return lax.dynamic_index_in_dim(parts, mem_index, 2, keepdims=False).reshape(
-            shard_in, quarter
-        )
-
-    def whole_columns(parts):
-        return (
-            parts.reshape(groups, shard_in, tgts, piece)
-            .transpose(1, 2, 0, 3)
-            .reshape(shard_in, tgts * hidden_shard)
-            .astype(F32)
-        )
-
     norm_self = gain_self.astype(F32)
     norm_cross = gain_cross.astype(F32)
     norm_ffn = gain_ffn.astype(F32)
@@ -541,22 +1163,21 @@
     positions = mem_index * positions_dev + jnp.arange(positions_dev)
     bias = jnp.where(positions[None, :] < lengths[:, None], gate_bias, NEG)[:, None, :]
 
-    attn = gather_tgt(
-        jnp.concatenate([self_q, self_k, self_v, cross_q, cross_k, cross_v], axis=1)
-    )
-    self_w = attn[:, : 3 * inner]
-    cross_q_w = attn[:, 3 * inner : 4 * inner]
-    cross_kv_w = attn[:, 4 * inner :]
-    self_o_w = gather_tgt(self_o)
-    cross_o_w = gather_tgt(cross_o)
-    gate_up = gather_tgt(jnp.concatenate([my_columns(ffn_gate), my_columns(ffn_up)], axis=1))
+    self_w, cross_kv_w, cross_q_w, self_o_w, cross_o_w = (
+        weight.reshape(-1, weight.shape[-1])
+        for weight in attention_weights(
+            (self_q, self_k, self_v, cross_q, cross_k, cross_v, self_o, cross_o)
+        )
+    )
+    gate_up = gather_tgt(pick_units(ffn_gate, ffn_up))
     down = gather_tgt(
         lax.dynamic_slice_in_dim(ffn_down, mem_index * piece, piece, axis=0)
     )
 
     inputs = padded(target).astype(F32)
     upstream_low = padded(out_grad)
-    upstreams = gather_mem(upstream_low)
+    late, self_w = lax.optimization_barrier((upstream_low, self_w))
+    upstreams = gather_mem(late)
     mem_flat = memory.reshape(all_items * positions_dev, model)
 
     h1 = (inputs * rms_scale(inputs) * norm_self).astype(BF)
@@ -572,40 +1193,11 @@
     catt = catt.reshape(tokens, inner)
     y2 = y1 + dot(catt, cross_o_w)
     h3 = (y2 * rms_scale(y2) * norm_ffn).astype(BF)
-    h3s = gather_mem(h3)
-
-    near_far = []
-    for part in (0, 1):
-        h3_two = jnp.concatenate(h3s[2 * part : 2 * part + 2], axis=0)
-        up_two = jnp.concatenate(upstreams[2 * part : 2 * part + 2], axis=0)
-        both = dot(h3_two, gate_up)
-        gate_pre, up_pre = both[:, :quarter], both[:, quarter:]
-
-        def gated(gate_in, up_in):
-            return jax.nn.gelu(gate_in, approximate=True) * up_in
-
-        gated_out, pull = jax.vjp(gated, gate_pre, up_pre)
-        hidden = gated_out.astype(BF)
-        hidden_back = dot_nt(up_two, down).astype(BF)
-        gate_back, up_back = pull(hidden_back.astype(F32))
-        two_back = jnp.concatenate([gate_back.astype(BF), up_back.astype(BF)], axis=1)
-        h3_back = dot_nt(two_back, gate_up)
-        out_part = dot(hidden, down)
-        near_far.append((h3_two, up_two, hidden, two_back, h3_back, out_part))
-    near, far = near_far
-    h3_back = owner_sum(near[4][:tokens], near[4][tokens:], far[4][:tokens], far[4][tokens:])
-    out_sum = owner_sum(near[5][:tokens], near[5][tokens:], far[5][:tokens], far[5][tokens:])
-    layer_out = trimmed((y2 + out_sum).astype(BF))
-
-    grad_gate_up = (dot_tn(near[0], near[3]) + dot_tn(far[0], far[3])).astype(BF)
-    grad_down = (dot_tn(near[2], near[1]) + dot_tn(far[2], far[1])).astype(BF)
+
+    h3_back, out_near, out_far, grad_gate_up, grad_down = ffn(h3, upstreams, gate_up, down)
+    out_sum = over_mem(out_far, 2)
     grad_gate_up = scatter_tgt(grad_gate_up)
     grad_down = scatter_tgt(grad_down)
-    grad_gate_up = lax.all_gather(grad_gate_up, "mem", axis=0)
-    grad_down = lax.all_gather(grad_down, "mem", axis=0, tiled=True).astype(F32)
-    grad_gate = whole_columns(grad_gate_up[:, :, :quarter])
-    grad_up = whole_columns(grad_gate_up[:, :, quarter:])
-
     dx, grad_norm_ffn = rms_back(y2, norm_ffn, h3_back)
     dy2 = upstream_low.astype(F32) + dx
     e2 = dy2.astype(BF)
@@ -619,6 +1211,10 @@
     )
     dck, dcv, dcq = cross_bwd(
         all_queries, dcatt.reshape(items, ROWS, inner), stats, ck, cv, bias
+    )
+    y2_late, dcq = lax.optimization_barrier((y2, dcq))
+    layer_out = trimmed(
+        (y2_late + out_near.astype(F32) + out_sum.astype(F32)).astype(BF)
     )
     dckv = jnp.concatenate([dck, dcv], axis=-1).reshape(all_items * positions_dev, 2 * inner)
     dcq = dcq.reshape(tokens, inner)
@@ -639,31 +1235,38 @@
         onehot, diag[:HEADS], NT, precision=HIGH
     )
 
-    wide = jnp.concatenate([grad_self, grad_cross_q, grad_cross_kv], axis=1).astype(BF)
-    wide = scatter_tgt(wide)
-    wide = lax.psum(wide.astype(F32), "mem")
-    outs = scatter_tgt(
-        jnp.concatenate([grad_self_o.astype(BF).reshape(tgts, -1, model),
-                         grad_cross_o.astype(BF).reshape(tgts, -1, model)], axis=1)
-        .reshape(-1, model)
-    )
-    outs = lax.psum(outs.astype(F32), "mem")
-    rows = outs.shape[0] // 2
-    small = lax.psum((grad_norm_self, grad_norm_cross, grad_norm_ffn, table), ("tgt", "mem"))
-    columns = [wide[:, i * inner : (i + 1) * inner] for i in range(6)]
+    small = jnp.concatenate(
+        [grad_norm_self, grad_norm_cross, grad_norm_ffn, table.reshape(-1)]
+    )
+    *sums, small = attention_sums(
+        tuple(
+            partial.astype(BF).reshape(tgts, -1, partial.shape[-1])
+            for partial in (grad_self, grad_cross_kv, grad_cross_q, grad_self_o, grad_cross_o)
+        ),
+        jnp.pad(small, (0, -small.size % 1024)).reshape(-1, 128),
+    )
+    columns = [partial.astype(F32) for partial in sums]
+    grad_gate_up, grad_down, small = lax.optimization_barrier((grad_gate_up, grad_down, small))
+    grad_gate_up, grad_down = share(grad_gate_up, grad_down)
+    grad_gate, grad_up = place_units(grad_gate_up)
+    grad_down = grad_down.reshape(-1, model).astype(F32)
+    small = small.reshape(-1)
+    norms = [small[start : start + model] for start in range(0, 3 * model, model)]
+    table = small[3 * model : 3 * model + table.size].reshape(table.shape)
     return (
         layer_out,
         target_grad,
         memory_grad,
-        *small,
+        *norms,
+        table,
         columns[0],
         columns[1],
         columns[2],
-        outs[:rows],
+        columns[6],
         columns[3],
         columns[4],
         columns[5],
-        outs[rows:],
+        columns[7],
         grad_gate,
         grad_up,
         grad_down,

time: 874 us -> 550 us (0.63)
  waiting for transfers between devices: 393 us -> 3.33 us
  Pallas kernels: 86.9 us -> 392 us
  blocking collectives: 86 us -> 0 us
  matrix products: 128 us -> 45 us
  local copies, waits for them, and re-layouts: 113 us -> 60.2 us
    pallas_call x0 -> x6, Pallas kernels: none -> 304 us  [the longest x1 114 us: reduce_weights(): pl.pallas_call(reduce_kernel, out_shape=tuple((jax.ShapeDtypeStruct(wide,...]
    all_gather x5 -> x2, waiting for transfers between devices: 171 us -> 3.25 us  [gather_tgt(): return lax.all_gather(shard, 'tgt', axis=0, tiled=True)]
    reduce_scatter x4 -> x2, waiting for transfers between devices: 130 us -> 0.01 us  [scatter_tgt(): return lax.psum_scatter(partial, 'tgt', scatter_dimension=0, tiled=True)]
    psum x2 -> x0, blocking collectives: 86 us -> none  [the longest x1 45.5 us: on_device(): wide = lax.psum(wide.astype(F32), 'mem')]
    ppermute x12 -> x4, waiting for transfers between devices: 66.4 us -> 0.01 us  [over_mem(): return lax.ppermute(value, 'mem', [(i, i ^ offset) for i in range(4)])]
    dot_general x9 -> x5, matrix products: 51.7 us -> 15.8 us  [dot_nt(): return lax.dot_general(left, right, NT, preferred_element_type=F32)]
    dot_general x9 -> x5, matrix products: 40.4 us -> 13.3 us  [dot(): return jnp.dot(left, right, preferred_element_type=F32)]
    convert_element_type x10 -> x2, local copies, waits for them, and re-layouts: 31.2 us -> 4.48 us  [on_device(): partial.astype(BF).reshape(tgts, -1, partial.shape[-1])]
  transfers between devices with their start and end apart: 23 -> 8, of which waited for: 11 -> 1; matrix products, arithmetic and copies ran while one was open for 27% -> 22% of each run, Pallas kernels for 10% -> 49%
where the time goes in v2:
time: 550 us; the launch traced here: 546 us
  Pallas kernels  392 us (71%)
  local copies, waits for them, and re-layouts  60.2 us (11%)
  matrix products  45 us (8%)
  other arithmetic  27.8 us (5%)
  between operations  14.6 us (3%)
    pallas_call x1, Pallas kernels, reduce_weights(): pl.pallas_call(reduce_kernel, out_shape=tuple((jax.ShapeDtypeStruct(wide,...  114 us
    pallas_call x1, Pallas kernels, ffn(): pl.pallas_call(ffn_kernel, out_shape=(jax.ShapeDtypeStruct((tokens, model...  85.1 us
    pallas_call x1, Pallas kernels, gather_weights(): pl.pallas_call(gather_kernel, out_shape=shapes, in_specs=[ANY_SPEC] * 8,...  64.6 us
    pallas_call x1, Pallas kernels, cross_fwd(): pl.pallas_call(functools.partial(cross_fwd_kernel, items), out_shape=(jax...  38.2 us
    pallas_call x1, Pallas kernels, cross_bwd(): pl.pallas_call(functools.partial(cross_bwd_kernel, items), out_shape=(jax...  36.6 us
    pallas_call x1, Pallas kernels, share(): pl.pallas_call(share_kernel, out_shape=tuple((jax.ShapeDtypeStruct((group...  32.1 us
    dot_general x5, matrix products, dot_nt(): return lax.dot_general(left, right, NT, preferred_element_type=F32)  15.8 us
    unnamed x138, local copies, waits for them, and re-layouts  15.7 us
  transfers between devices with their start and end apart: 8, of which 1 were waited for; matrix products, arithmetic and copies ran while one was open for 22% of the time, Pallas kernels for 49%

profile of v2, /device:TPU:0, one launch (start us, length us, event | category | flops | bytes accessed | tf_op | source)
XLA Modules:
  0.0 546.1 jit_solution(1253626266445013514)
XLA Ops:
  9.4 2.9 pick_units.1
  12.6 64.6 %gather_weights.1 = (bf16[8,184,1152]{2,1,0:T(8,128)(2,1)}, bf16[8,184,768]{2,1,0:T(8,128)(2,1)}, bf16[8,184,384]{2,1,0:T(8,128)(2,1)}, bf16[8,48,1472]{2,1,0:T(8,128)(2,1)}, bf16[8,48,1472]{2,1,0:T(8,128)(2,1)}) custom-call(bf16[184,384]{1,0:T(8,128)(2,1)} %self_q.1, bf16[184,384]{1,0:T(8,128)(2,1)} %self_k.1, bf16[184,384]{1,0:T(8,128)(2,1)} %self_v.1, ...), custom_call_target="tpu_custom_call" | custom-call | bytes 157286400 | tf_op jit(solution)/shard_map/gather_weights/pallas_call | solution.py:753
  82.9 7.1 %copy.144 = bf16[8,184,8,256]{3,2,0,1:T(8,128)(2,1)} copy(bf16[8,184,8,256]{3,2,1,0:T(8,128)(2,1)} %bitcast.105) | data formatting | bytes 12058624 | tf_op jit(solution)/shard_map/reshape | solution.py:1181
  91.9 2.7 convolution_convert_fusion.5
  94.6 5.3 fusion.1
  102.5 2.6 copy.110
  105.1 3.3 copy.111
  111.6 4.5 self_fwd.1
  120.2 38.2 %cross_fwd.1 = (bf16[4,2,192,384]{3,2,1,0:T(8,128)(2,1)}, bf16[2,192,384]{2,1,0:T(8,128)(2,1)}, f32[2,192,128]{2,1,0:T(8,128)}) custom-call(bf16[2,192,384]{2,1,0:T(8,128)(2,1)} %bitcast.142, bf16[8,256,384]{2,1,0:T(8,128)(2,1)} %bitcast.131, bf16[8,256,384]{2,1,0:T(8,128)(2,1)} %bitcast.133, f32[8,1,256]{2,1,0:T(1,128)} %broadcast_in_dim.9.bias_ref), custom_call_target="tpu_custom_call" | custom-call | flops 1207959552 | bytes 8388608 | tf_op jit(solution)/shard_map/cross_fwd/pallas_call | solution.py:327
  164.3 2.6 copy.116.up2_ref
  166.9 2.4 copy.115.up1_ref
  169.3 2.1 copy.117.up3_ref
  171.4 3.2 all-gather.3.cloned.1.call-done.gate_up_ref
  174.6 85.1 %feed_forward.1 = (f32[384,1472]{1,0:T(8,128)}, bf16[384,1472]{1,0:T(8,128)(2,1)}, bf16[384,1472]{1,0:T(8,128)(2,1)}, bf16[1472,1792]{1,0:T(8,128)(2,1)}, bf16[896,1472]{1,0:T(8,128)(2,1)}) custom-call(bf16[384,1472]{1,0:T(8,128)(2,1)} %multiply_convert_fusion.1.h_ref, bf16[384,1472]{1,0:T(8,128)(2,1)} %bitcast.104, bf16[384,1472]{1,0:T(8,128)(2,1)} %copy.115.up1_ref, ...), custom_call_target="tpu_custom_call" | custom-call | flops 36465278976 | bytes 33554432 | tf_op jit(solution)/shard_map/feed_forward/pallas_call | solution.py:585
  262.1 3.7 multiply_convert_fusion
  271.1 36.6 %cross_bwd.1 = (bf16[8,256,384]{2,1,0:T(8,128)(2,1)}, bf16[8,256,384]{2,1,0:T(8,128)(2,1)}, bf16[2,192,384]{2,1,0:T(8,128)(2,1)}) custom-call(bf16[4,2,192,384]{3,2,1,0:T(8,128)(2,1)} %get-tuple-element.63.all_ref, bf16[2,192,384]{2,1,0:T(8,128)(2,1)} %bitcast.141, f32[2,192,128]{2,1,0:T(8,128)} %maximum_maximum_fusion.stat_ref, ...), custom_call_target="tpu_custom_call" | custom-call | flops 3019898880 | bytes 12582912 | tf_op jit(solution)/shard_map/cross_bwd/pallas_call | solution.py:444
  307.7 2.5 copy.120
  310.8 2.1 multiply_reduce_fusion.1
  315.8 9.4 %self_bwd.1 = (bf16[2,192,1152]{2,1,0:T(8,128)(2,1)}, f32[8,256]{1,0:T(8,128)}) custom-call(bf16[2,192,1152]{2,1,0:T(8,128)(2,1)} %bitcast.138, bf16[2,192,384]{2,1,0:T(8,128)(2,1)} %bitcast.143, f32[8,256]{1,0:T(8,128)} %pad.17.base_ref), custom_call_target="tpu_custom_call" | custom-call | flops 754974720 | bytes 2064384 | tf_op jit(solution)/shard_map/self_bwd/pallas_call | solution.py:196
  330.7 2.0 convolution_convert_fusion.4
  332.8 4.3 fusion
  337.1 3.9 fusion.9
  341.0 6.7 %convolution_convert_fusion = bf16[2048,1472]{0,1:T(8,128)(2,1)} fusion(bf16[2048,768]{1,0:T(8,128)(2,1)S(1)} %bitcast.139, bf16[1472,768]{1,0:T(8,128)(2,1)S(1)} %bitcast.150), kind=kOutput, calls=%fused_computation.1 | convolution fusion | flops 4633526272 | bytes 11436032 | tf_op jit(solution)/shard_map/dot_general | solution.py:53
  347.7 6.0 %bitcast_convert_fusion = bf16[768,1472]{0,1:T(8,128)(2,1)} fusion(bf16[8,256,1472]{1,2,0:T(8,128)(2,1)S(1)} %bitcast.107, bf16[8,256,768]{2,1,0:T(8,128)(2,1)S(1)} %constant_dynamic-update-slice_fusion), kind=kOutput, calls=%fused_computation.4 | convolution fusion | flops 4631642112 | bytes 11436032 | tf_op jit(solution)/shard_map/dot_general | solution.py:57
  354.0 2.1 copy.129
  356.0 2.4 copy.128
  359.1 114.0 %reduce_weights.1 = (bf16[184,384]{1,0:T(8,128)(2,1)}, bf16[184,384]{1,0:T(8,128)(2,1)}, bf16[184,384]{1,0:T(8,128)(2,1)}, bf16[184,384]{1,0:T(8,128)(2,1)}, bf1...) custom-call(bf16[8,184,1152]{2,1,0:T(8,128)(2,1)} %bitcast.124, ...), custom_call_target="tpu_custom_call" | custom-call | bytes 157286400 | tf_op jit(solution)/shard_map/reduce_weights/pallas_call | solution.py:947
  484.5 5.9 %copy.149 = bf16[184,8,8,256]{3,2,0,1:T(8,128)(2,1)} copy(bf16[184,8,8,256]{3,2,1,0:T(8,128)(2,1)} %bitcast.109) | data formatting | bytes 12058624 | tf_op jit(solution)/shard_map/reshape | solution.py:1222
  491.0 2.2 copy.141
  496.5 2.2 copy.140
  499.5 32.1 %share_sums.1 = (bf16[4,184,1792]{2,1,0:T(8,128)(2,1)}, bf16[4,112,1472]{2,1,0:T(8,128)(2,1)}) custom-call(bf16[184,1792]{1,0:T(8,128)(2,1)} %reduce-scatter.3.cloned.1.call-done.wide_ref, bf16[112,1472]{1,0:T(8,128)(2,1)} %reduce-scatter.5.cloned.1.call-done.tall_ref), custom_call_target="tpu_custom_call" | custom-call | bytes 62914560 | tf_op jit(solution)/shard_map/share_sums/pallas_call | solution.py:1073
  531.6 5.0 place_units.1
  (217 shorter events, 61.9 us)
Async XLA Ops:
  7.2 164.1 %all-gather.5.cloned.1.call-start = ((), (), s32[]{:S(2)}) async-start(), calls=%async_computation.3 | async-start | bytes 3096576 | tf_op jit(solution)/shard_map/all_gather | solution.py:1100
  9.3 165.3 %all-gather.3.cloned.1.call-start = ((), (), s32[]{:S(2)}) async-start(), calls=%async_computation.2 | async-start | bytes 5935104 | tf_op jit(solution)/shard_map/all_gather | solution.py:1100
  12.3 486.4 %reduce-scatter.5.cloned.1.call-start = ((), (), s32[]{:S(2)}) async-start(), calls=%async_computation.5 | async-start | bytes 3096576 | tf_op jit(solution)/shard_map/reduce_scatter | solution.py:1104
  12.5 66.3 %copy-start.15 = (bf16[2,189,1472]{2,0,1:T(2,128)(2,1)S(1)}, bf16[2,189,1472]{2,0,1:T(2,128)(2,1)}, u32[]{:S(2)}) copy-start(bf16[2,189,1472]{2,0,1:T(2,128)(2,1)} %param.21) | copy-start | bytes 3338500
  12.6 67.9 %copy-start.13 = (bf16[2,192,1472]{2,1,0:T(8,128)(2,1)}, bf16[2,192,1472]{2,1,0:T(8,128)(2,1)S(1)}, u32[]{:S(2)}) copy-start(bf16[2,192,1472]{2,1,0:T(8,128)(2,1)S(1)} %pad.16.clone) | copy-start | bytes 3391492
  78.7 79.7 %collective-permute-start.1 = (bf16[384,1472]{0,1:T(8,128)(2,1)}, bf16[384,1472]{0,1:T(8,128)(2,1)}, u32[]{:S(2)}, u32[]{:S(2)}) collective-permute-start(bf16[384,1472]{0,1:T(8,128)(2,1)} %copy.113), channel_id=1, source_target_pairs={{0,2},{1,3},{2,0},{3,1},{4,6},{5,7},{6,4},{7,5},{8,10},{9,11},{10,... | collective-permute-start | bytes 3391496 | tf_op jit(solution)/shard_map/ppermute | solution.py:1090
  78.7 88.2 %collective-permute-start = (bf16[384,1472]{0,1:T(8,128)(2,1)}, bf16[384,1472]{0,1:T(8,128)(2,1)}, u32[]{:S(2)}, u32[]{:S(2)}) collective-permute-start(bf16[384,1472]{0,1:T(8,128)(2,1)} %copy.113), channel_id=1, source_target_pairs={{0,1},{1,0},{2,3},{3,2},{4,5},{5,4},{6,7},{7,6},{8,9},{9,8},{10,11... | collective-permute-start | bytes 3391496 | tf_op jit(solution)/shard_map/ppermute | solution.py:1090
  81.1 9.5 %copy-start.41 = (f32[384]{0:T(512)}, f32[384]{0:T(512)S(1)}, u32[]{:S(2)}) copy-start(f32[384]{0:T(512)S(1)} %rsqrt.41) | copy-start | bytes 4612
  82.8 33.3 %copy-start.7 = (f32[2,192,1472]{2,1,0:T(8,128)}, f32[2,192,1472]{2,1,0:T(8,128)S(1)}, u32[]{:S(2)}) copy-start(f32[2,192,1472]{2,1,0:T(8,128)S(1)} %copy.105) | copy-start | bytes 6782980
  82.9 7.1 %copy-start.37 = (f32[32,256]{1,0:T(8,128)S(1)}, f32[32,256]{1,0:T(8,128)}, u32[]{:S(2)}) copy-start(f32[32,256]{1,0:T(8,128)} %constant.32.clone) | copy-start | bytes 98308
  82.9 7.1 %copy-start.53 = (f32[32,6]{0,1:T(8,128)S(1)}, f32[32,6]{0,1:T(8,128)}, u32[]{:S(2)}) copy-start(f32[32,6]{0,1:T(8,128)} %param.29) | copy-start | bytes 2308
  105.1 11.1 %copy-start.18 = (bf16[8,48,1472]{2,1,0:T(8,128)(2,1)S(1)}, bf16[8,48,1472]{2,1,0:T(8,128)(2,1)}, u32[]{:S(2)}) copy-start(bf16[8,48,1472]{2,1,0:T(8,128)(2,1)} %get-tuple-element.58) | copy-start | bytes 3391492
  110.3 51.8 %copy-start.39 = (f32[1472]{0:T(1024)}, f32[1472]{0:T(1024)S(1)}, u32[]{:S(2)}) copy-start(f32[1472]{0:T(1024)S(1)} %convert_element_type.146) | copy-start | bytes 17668
  118.1 41.7 %copy-start.2 = (f32[384,1472]{1,0:T(8,128)}, f32[384,1472]{1,0:T(8,128)S(1)}, u32[]{:S(2)}) copy-start(f32[384,1472]{1,0:T(8,128)S(1)} %get-tuple-element.178) | copy-start | bytes 6782980
  120.2 39.6 %copy-start.20 = (bf16[8,48,1472]{2,1,0:T(8,128)(2,1)S(1)}, bf16[8,48,1472]{2,1,0:T(8,128)(2,1)}, u32[]{:S(2)}) copy-start(bf16[8,48,1472]{2,1,0:T(8,128)(2,1)} %get-tuple-element.62) | copy-start | bytes 3391492
  158.4 10.9 %collective-permute-start.2 = (bf16[384,1472]{0,1:T(8,128)(2,1)}, bf16[384,1472]{0,1:T(8,128)(2,1)S(1)}, u32[]{:S(2)}, u32[]{:S(2)}) collective-permute-start(bf16[384,1472]{0,1:T(8,128)(2,1)} %collective-permute-done.1), channel_id=1, source_target_pairs={{0,1},{1,0},{2,3},{3,2},{4,5},{5,4},{6,7},{7,6},{8,9},{9,8},{10,11... | collective-permute-start | bytes 3391496 | tf_op jit(solution)/shard_map/ppermute | solution.py:1090
  259.7 239.0 %reduce-scatter.3.cloned.1.call-start = ((), (), s32[]{:S(2)}) async-start(), calls=%async_computation.4 | async-start | bytes 5935104 | tf_op jit(solution)/shard_map/reduce_scatter | solution.py:1104
  260.8 4.9 copy-start.17
  271.1 39.7 %copy-start.3 = (f32[384,1472]{1,0:T(8,128)S(1)}, f32[384,1472]{1,0:T(8,128)}, u32[]{:S(2)}) copy-start(f32[384,1472]{1,0:T(8,128)} %copy-done.2) | copy-start | bytes 6782980
  310.2 183.0 %collective-permute-start.3 = (bf16[384,1472]{0,1:T(8,128)(2,1)}, bf16[384,1472]{0,1:T(8,128)(2,1)}, u32[]{:S(2)}, u32[]{:S(2)}) collective-permute-start(bf16[384,1472]{0,1:T(8,128)(2,1)} %copy.120), channel_id=1, source_target_pairs={{0,2},{1,3},{2,0},{3,1},{4,6},{5,7},{6,4},{7,5},{8,10},{9,11},{10,... | collective-permute-start | bytes 3391496 | tf_op jit(solution)/shard_map/ppermute | solution.py:1090
  314.3 14.5 %copy-start.11 = (f32[384,1472]{1,0:T(8,128)}, f32[384,1472]{1,0:T(8,128)S(1)}, u32[]{:S(2)}) copy-start(f32[384,1472]{1,0:T(8,128)S(1)} %subtract_add_fusion) | copy-start | bytes 6782980
  337.0 10.6 %slice-start = ((s8[6029312]{0:T(1024)(128)(4,1)}), s8[4194304]{0:T(1024)(128)(4,1)S(1)}, s32[]{:S(2)}) async-start(s8[6029312]{0:T(1024)(128)(4,1)} %bitcast.106), calls=%async_computation.6 | async-start | bytes 8388608
  341.0 6.7 %slice-start.1 = ((s8[6029312]{0:T(1024)(128)(4,1)}), s8[1835008]{0:T(1024)(128)(4,1)S(1)}, s32[]{:S(2)}) async-start(s8[6029312]{0:T(1024)(128)(4,1)} %bitcast.106), calls=%async_computation.7 | async-start | bytes 3670016
  347.7 6.0 %copy-start.38 = (f32[32,256]{1,0:T(8,128)S(1)}, f32[32,256]{1,0:T(8,128)}, u32[]{:S(2)}) copy-start(f32[32,256]{1,0:T(8,128)} %constant.32.clone) | copy-start | bytes 98308
  347.7 6.0 %copy-start.49 = (f32[8,256]{1,0:T(8,128)S(1)}, f32[8,256]{1,0:T(8,128)}, u32[]{:S(2)}) copy-start(f32[8,256]{1,0:T(8,128)} %get-tuple-element.77) | copy-start | bytes 24580
  473.2 9.9 %copy-start.36 = (bf16[184,384]{1,0:T(8,128)(2,1)S(1)}, bf16[184,384]{1,0:T(8,128)(2,1)}, u32[]{:S(2)}) copy-start(bf16[184,384]{1,0:T(8,128)(2,1)} %get-tuple-element.85) | copy-start | bytes 423940
  473.2 10.6 %copy-start.35 = (bf16[184,384]{1,0:T(8,128)(2,1)S(1)}, bf16[184,384]{1,0:T(8,128)(2,1)}, u32[]{:S(2)}) copy-start(bf16[184,384]{1,0:T(8,128)(2,1)} %get-tuple-element.86) | copy-start | bytes 423940
  484.5 5.9 %copy-start.54 = (f32[384]{0:T(512)S(1)}, f32[384]{0:T(512)}, u32[]{:S(2)}) copy-start(f32[384]{0:T(512)} %get-tuple-element.171) | copy-start | bytes 4612
  484.5 5.9 %copy-start.12 = (f32[384,1472]{1,0:T(8,128)S(1)}, f32[384,1472]{1,0:T(8,128)}, u32[]{:S(2)}) copy-start(f32[384,1472]{1,0:T(8,128)} %copy-done.11) | copy-start | bytes 6782980
  484.5 5.9 %copy-start.27 = (f32[384,1472]{1,0:T(8,128)S(1)}, f32[384,1472]{1,0:T(8,128)}, u32[]{:S(2)}) copy-start(f32[384,1472]{1,0:T(8,128)} %get-tuple-element.184) | copy-start | bytes 6782980
  531.6 5.0 copy-start.29
  531.6 7.8 %copy-start.1 = (bf16[448,1472]{1,0:T(8,128)(2,1)S(1)}, bf16[448,1472]{1,0:T(8,128)(2,1)}, u32[]{:S(2)}) copy-start(bf16[448,1472]{1,0:T(8,128)(2,1)} %param.40) | copy-start | bytes 3956740
  (42 other events, 94.2 us)
Sparse Core Ops, SparseCore 0:
  10.2 76.2 all-gather.4
  89.3 85.2 all-gather.2
  259.9 73.8 reduce-scatter.4
  337.1 117.9 reduce-scatter.2

commit v3 on v2

--- a/solution.py
+++ b/solution.py
@@ -243,7 +243,7 @@
 
 
 def cross_fwd_kernel(
-    items, q_ref, k_ref, v_ref, bias_ref, all_ref, att_ref, lse_ref,
+    items, q_ref, kv_ref, bias_ref, all_ref, att_ref, lse_ref,
     out_o, out_s, in_o, in_s, q_send, q_recv, o_send, o_recv, s_send, s_recv,
 ):
     me = lax.axis_index("mem")
@@ -273,8 +273,8 @@
             stats = jnp.zeros((ROWS, STATS), F32)
             for index in range(HEADS // 2):
                 both = all_ref[slot, item, :, pair(index)]
-                keys = k_ref[place, :, pair(index)]
-                values = v_ref[place, :, pair(index)]
+                keys = kv_ref[place, :, pair(index)]
+                values = kv_ref[place, :, pair(index + HEADS // 2)]
                 total = None
                 scales = []
                 for half, mask in ((0, low), (1, high)):
@@ -318,7 +318,7 @@
             att_ref[item, :, pair(index)] = total.astype(BF)
 
 
-def cross_fwd(queries, keys, values, bias):
+def cross_fwd(queries, keys_values, bias):
     items = queries.shape[0]
     inner = HEADS * HEAD
     block = (4, items, ROWS, inner)
@@ -331,7 +331,7 @@
             jax.ShapeDtypeStruct((items, ROWS, inner), BF),
             jax.ShapeDtypeStruct((items, ROWS, STATS), F32),
         ),
-        in_specs=[VMEM_SPEC] * 4,
+        in_specs=[VMEM_SPEC] * 3,
         out_specs=(VMEM_SPEC,) * 3,
         scratch_shapes=[
             pltpu.VMEM(block, BF),
@@ -352,11 +352,11 @@
             flops=flops, bytes_accessed=8 * 1024 * 1024, transcendentals=flops // 512
         ),
         name="cross_fwd",
-    )(queries, keys, values, bias)
+    )(queries, keys_values, bias)
 
 
 def cross_bwd_kernel(
-    items, all_ref, back_ref, stat_ref, k_ref, v_ref, bias_ref, dk_ref, dv_ref, dq_ref,
+    items, all_ref, back_ref, stat_ref, kv_ref, bias_ref, dkv_ref, dq_ref,
     all_b, all_s, out_q, in_q, b_send, b_recv, s_send, s_recv, q_send, q_recv,
 ):
     me = lax.axis_index("mem")
@@ -400,8 +400,8 @@
                     upstream = back_ref[item, :, pair(index)]
                 else:
                     upstream = all_b[slot, item, :, pair(index)]
-                keys = k_ref[place, :, pair(index)]
-                values = v_ref[place, :, pair(index)]
+                keys = kv_ref[place, :, pair(index)]
+                values = kv_ref[place, :, pair(index + HEADS // 2)]
                 dq = dk = dv = None
                 for half, mask in ((0, low), (1, high)):
                     head = 2 * index + half
@@ -418,8 +418,8 @@
                     dk = k_part if half == 0 else dk + k_part
                     dv = v_part if half == 0 else dv + v_part
                 out_q[slot, item, :, pair(index)] = dq.astype(BF)
-                dk_ref[place, :, pair(index)] = dk.astype(BF)
-                dv_ref[place, :, pair(index)] = dv.astype(BF)
+                dkv_ref[place, :, pair(index)] = dk.astype(BF)
+                dkv_ref[place, :, pair(index + HEADS // 2)] = dv.astype(BF)
         if slot:
             copies.append(send(out_q.at[slot], in_q.at[slot], q_send.at[slot], q_recv.at[slot], slot))
             copies[-1].start()
@@ -436,7 +436,7 @@
             dq_ref[item, :, pair(index)] = total.astype(BF)
 
 
-def cross_bwd(all_queries, back, stats, keys, values, bias):
+def cross_bwd(all_queries, back, stats, keys_values, bias):
     items = back.shape[0]
     inner = HEADS * HEAD
     block = (4, items, ROWS, inner)
@@ -444,12 +444,11 @@
     return pl.pallas_call(
         functools.partial(cross_bwd_kernel, items),
         out_shape=(
-            jax.ShapeDtypeStruct(keys.shape, BF),
-            jax.ShapeDtypeStruct(keys.shape, BF),
+            jax.ShapeDtypeStruct(keys_values.shape, BF),
             jax.ShapeDtypeStruct((items, ROWS, inner), BF),
         ),
-        in_specs=[VMEM_SPEC] * 6,
-        out_specs=(VMEM_SPEC,) * 3,
+        in_specs=[VMEM_SPEC] * 5,
+        out_specs=(VMEM_SPEC,) * 2,
         scratch_shapes=[
             pltpu.VMEM(block, BF),
             pltpu.VMEM((4, items, ROWS, STATS), F32),
@@ -469,7 +468,7 @@
             flops=flops, bytes_accessed=12 * 1024 * 1024, transcendentals=flops // 1280
         ),
         name="cross_bwd",
-    )(all_queries, back, stats, keys, values, bias)
+    )(all_queries, back, stats, keys_values, bias)
 
 
 CUBIC = 0.044715
@@ -481,29 +480,77 @@
 
 
 def ffn_kernel(
-    h_ref, up0_ref, up1_ref, up2_ref, up3_ref, gate_up_ref, down_ref,
-    h_back_ref, near_ref, far_ref, grad_gu_ref, grad_down_ref,
-    h_all, u_all, hidden, two_back, h_part, y_part, h_in, y_in,
-    h_send, h_recv, d_send, d_recv, y_send, y_recv,
+    items, h_ref, up0_ref, up1_ref, up2_ref, up3_ref, gate_up_hbm, down_hbm,
+    h_back_ref, near_ref, far_ref, grad_gu_hbm, grad_down_hbm,
+    gate_up_ref, down_ref, h_all, u_all, hidden, two_back, h_part, y_part, h_in, y_in, gu_strip, down_strip,
+    h_send, h_recv, d_send, d_recv, y_send, y_recv, load_sem, up_sem, store_sem,
 ):
     tokens, model = h_ref.shape
+    rows = tokens // items
     units = down_ref.shape[0]
+    loads = [
+        pltpu.make_async_copy(gate_up_hbm, gate_up_ref, load_sem.at[0]),
+        pltpu.make_async_copy(down_hbm, down_ref, load_sem.at[1]),
+        pltpu.make_async_copy(up0_ref, u_all.at[0], load_sem.at[2]),
+        pltpu.make_async_copy(up1_ref, u_all.at[1], load_sem.at[3]),
+    ]
+    for copy in loads:
+        copy.start()
+    ups = []
+    for item in range(items):
+        mine = pl.ds(item * rows, rows)
+        for place, ref in enumerate((up2_ref, up3_ref)):
+            ups.append(
+                pltpu.make_async_copy(
+                    ref.at[mine], u_all.at[2 + item, pl.ds(place * rows, rows)],
+                    up_sem.at[item, place],
+                )
+            )
+            ups[-1].start()
     greet("mem", (1, 2))
     h_to_core = send(h_ref, h_all.at[1], h_send.at[0], h_recv.at[0], 1)
-    h_to_far = send(h_ref, h_all.at[2], h_send.at[1], h_recv.at[1], 2)
-    h_relay = send(h_all.at[2], h_all.at[3], h_send.at[2], h_recv.at[2], 1)
+    h_to_far, h_relay, d_pass, d_far, y_pass = [], [], [], [], []
+    first, second = pl.ds(0, rows), pl.ds(rows, rows)
+    for item in range(items):
+        block, at = 2 + item, 1 + item
+        h_to_far.append(
+            send(h_ref.at[pl.ds(item * rows, rows)], h_all.at[block, first],
+                 h_send.at[at], h_recv.at[at], 2)
+        )
+        h_relay.append(
+            send(h_all.at[block, first], h_all.at[block, second],
+                 h_send.at[at + items], h_recv.at[at + items], 1)
+        )
+        d_pass.append(
+            send(h_part.at[block, second], h_in.at[1, pl.ds(item * rows, rows)],
+                 d_send.at[at], d_recv.at[at], 1)
+        )
+        y_pass.append(
+            send(y_part.at[block, second], y_in.at[1, pl.ds(item * rows, rows)],
+                 y_send.at[at], y_recv.at[at], 1)
+        )
+        d_far.append(
+            send(h_part.at[block, first], h_in.at[2, pl.ds(item * rows, rows)],
+                 d_send.at[at + items], d_recv.at[at + items], 2)
+        )
     d_near = send(h_part.at[1], h_in.at[0], d_send.at[0], d_recv.at[0], 1)
-    d_pass = send(h_part.at[3], h_in.at[1], d_send.at[1], d_recv.at[1], 1)
-    d_far = send(h_part.at[2], h_in.at[2], d_send.at[2], d_recv.at[2], 2)
     y_near = send(y_part.at[1], y_in.at[0], y_send.at[0], y_recv.at[0], 1)
-    y_pass = send(y_part.at[3], y_in.at[1], y_send.at[1], y_recv.at[1], 1)
-    h_to_far.start()
+    for copy in h_to_far:
+        copy.start()
     h_to_core.start()
     h_all[0] = h_ref[...]
-    u_all[0] = up0_ref[...]
-    u_all[1] = up1_ref[...]
-    u_all[2] = up2_ref[...]
-    u_all[3] = up3_ref[...]
+    for copy in loads:
+        copy.wait()
+    for copy in ups:
+        copy.wait()
+
+    def give_back(item):
+        mine = pl.ds(item * rows, rows)
+        d_pass[item].wait_recv()
+        h_part[2 + item, first, :] = (
+            h_part[2 + item, first, :].astype(F32) + h_in[1, mine, :].astype(F32)
+        ).astype(BF)
+        d_far[item].start()
 
     def token_block(slot, carry):
         @pl.when(slot == 1)
@@ -514,12 +561,22 @@
         def _():
             d_near.start()
             y_near.start()
-            h_to_far.wait_recv()
-            h_relay.start()
-
-        @pl.when(slot == 3)
-        def _():
-            h_relay.wait_recv()
+
+        for item in range(items):
+
+            @pl.when(slot == 2 + item)
+            def _(item=item):
+                if item:
+                    d_pass[item - 1].start()
+                    y_pass[item - 1].start()
+                h_relay[item].wait_recv()
+
+        for item in range(items):
+
+            @pl.when(slot == 1 + item)
+            def _(item=item):
+                h_to_far[item].wait_recv()
+                h_relay[item].start()
 
         def units_block(block, inside):
             pairs = pl.ds(pl.multiple_of(block * 256, 256), 256)
@@ -544,46 +601,79 @@
         for start, width in strips(model, 256):
             part = slice(start, start + width)
             h_part[slot, :, part] = dot_nt(two_back[slot], gate_up_ref[part, :]).astype(BF)
+        for item in range(items - 1):
+
+            @pl.when(slot == 3 + item)
+            def _(item=item):
+                give_back(item)
+
+        for start, width in strips(model, 256):
+            part = slice(start, start + width)
             y_part[slot, :, part] = dot(hidden[slot], down_ref[:, part]).astype(BF)
         return carry
 
-    lax.fori_loop(0, 4, token_block, 0)
-    d_pass.start()
-    y_pass.start()
-    d_pass.wait_recv()
-    h_part[2] = (h_part[2].astype(F32) + h_in[1].astype(F32)).astype(BF)
-    d_far.start()
-    count = 4 * tokens
+    lax.fori_loop(0, 2 + items, token_block, 0)
+    d_pass[-1].start()
+    y_pass[-1].start()
+    count = (2 + items) * tokens
+    stores = []
+
+    def store(value, strip, hbm, start, width):
+        number = len(stores)
+        if number >= 2:
+            stores[number - 2].wait()
+        strip[number % 2, :width, :] = value
+        stores.append(
+            pltpu.make_async_copy(
+                strip.at[number % 2, pl.ds(0, width)],
+                hbm.at[pl.ds(start, width)],
+                store_sem.at[number],
+            )
+        )
+        stores[-1].start()
+
     for start, width in strips(model, 256):
         part = slice(start, start + width)
-        grad_gu_ref[part, :] = dot_tn(
+        value = dot_tn(
             h_all[:, :, part].reshape(count, width), two_back[...].reshape(count, 2 * units)
-        ).astype(BF)
+        )
+        store(value.astype(BF), gu_strip, grad_gu_hbm, start, width)
+        if start == 0:
+            give_back(items - 1)
     for start, width in strips(units, 256):
         part = slice(start, start + width)
-        grad_down_ref[part, :] = dot_tn(
+        value = dot_tn(
             hidden[:, :, part].reshape(count, width), u_all[...].reshape(count, model)
+        )
+        store(value.astype(BF), down_strip, grad_down_hbm, start, width)
+    for item in range(items):
+        mine = pl.ds(item * rows, rows)
+        y_pass[item].wait_recv()
+        far_ref[mine, :] = (
+            y_part[2 + item, first, :].astype(F32) + y_in[1, mine, :].astype(F32)
         ).astype(BF)
-    y_pass.wait_recv()
-    far_ref[...] = (y_part[2].astype(F32) + y_in[1].astype(F32)).astype(BF)
     y_near.wait_recv()
     near_ref[...] = (y_part[0].astype(F32) + y_in[0].astype(F32)).astype(BF)
     d_near.wait_recv()
-    d_far.wait_recv()
+    for copy in d_far:
+        copy.wait_recv()
     h_back_ref[...] = (
         h_part[0].astype(F32) + h_in[0].astype(F32) + h_in[2].astype(F32)
     )
-    for copy in (h_to_core, h_to_far, h_relay, d_near, d_pass, d_far, y_near, y_pass):
+    for copy in stores[-2:]:
+        copy.wait()
+    for copy in (h_to_core, d_near, y_near, *h_to_far, *h_relay, *d_pass, *y_pass, *d_far):
         copy.wait_send()
 
 
-def ffn(h3, upstreams, gate_up, down):
+def ffn(h3, upstreams, gate_up, down, items):
     tokens, model = h3.shape
     units = down.shape[0]
-    every = (4, tokens, model)
-    flops = 4 * tokens * model * units * 18
+    every = (2 + items, tokens, model)
+    flops = (2 + items) * tokens * model * units * 18
+    grads = len(strips(model, 256)) + len(strips(units, 256))
     return pl.pallas_call(
-        ffn_kernel,
+        functools.partial(ffn_kernel, items),
         out_shape=(
             jax.ShapeDtypeStruct((tokens, model), F32),
             jax.ShapeDtypeStruct((tokens, model), BF),
@@ -591,23 +681,28 @@
             jax.ShapeDtypeStruct((model, 2 * units), BF),
             jax.ShapeDtypeStruct((units, model), BF),
         ),
-        in_specs=[VMEM_SPEC] * 7,
-        out_specs=(VMEM_SPEC,) * 5,
+        in_specs=[VMEM_SPEC] + [ANY_SPEC] * 6,
+        out_specs=(VMEM_SPEC,) * 3 + (ANY_SPEC,) * 2,
         scratch_shapes=[
+            pltpu.VMEM((model, 2 * units), BF),
+            pltpu.VMEM((units, model), BF),
             pltpu.VMEM(every, BF),
             pltpu.VMEM(every, BF),
-            pltpu.VMEM((4, tokens, units), BF),
-            pltpu.VMEM((4, tokens, 2 * units), BF),
+            pltpu.VMEM((2 + items, tokens, units), BF),
+            pltpu.VMEM((2 + items, tokens, 2 * units), BF),
             pltpu.VMEM(every, BF),
             pltpu.VMEM(every, BF),
             pltpu.VMEM((3, tokens, model), BF),
             pltpu.VMEM((2, tokens, model), BF),
-            pltpu.SemaphoreType.DMA((3,)),
-            pltpu.SemaphoreType.DMA((3,)),
-            pltpu.SemaphoreType.DMA((3,)),
-            pltpu.SemaphoreType.DMA((3,)),
-            pltpu.SemaphoreType.DMA((2,)),
-            pltpu.SemaphoreType.DMA((2,)),
+            pltpu.VMEM((2, 256, 2 * units), BF),
+            pltpu.VMEM((2, 256, model), BF),
+        ]
+        + [pltpu.SemaphoreType.DMA((1 + 2 * items,))] * 4
+        + [pltpu.SemaphoreType.DMA((1 + items,))] * 2
+        + [
+            pltpu.SemaphoreType.DMA((4,)),
+            pltpu.SemaphoreType.DMA((items, 2)),
+            pltpu.SemaphoreType.DMA((grads,)),
         ],
         compiler_params=pltpu.CompilerParams(
             collective_id=3, has_side_effects=True, vmem_limit_bytes=FFN_CAP
@@ -633,7 +728,7 @@
 
 def greet_all(mem, tgt):
     barrier = pltpu.get_barrier_semaphore()
-    for offset in (1, 2):
+    for offset in (1, 2, 3):
         pl.semaphore_signal(
             barrier, inc=1, device_id={"mem": jnp.bitwise_xor(mem, offset)}, device_id_type=MESH
         )
@@ -641,7 +736,7 @@
         pl.semaphore_signal(
             barrier, inc=1, device_id={"tgt": jnp.bitwise_xor(tgt, offset)}, device_id_type=MESH
         )
-    pl.semaphore_wait(barrier, 6)
+    pl.semaphore_wait(barrier, 7)
 
 
 FIRST = (1, 2, 4, 6)
@@ -704,8 +799,14 @@
         @pl.when(mem == index)
         def _(index=index, group=group):
             members = list(enumerate(group))
+            far_members = list(enumerate(groups[index ^ 2]))
+            near_members = list(enumerate(groups[index ^ 1]))
+            last_members = list(enumerate(groups[index ^ 3]))
+            extra = [(2, far_members[0][1])] if index % 2 else []
+            far_sent = members[1:] if index % 2 else members
+            far_got = far_members[1:] if index % 2 else far_members
             for step, offset in steps[:4]:
-                for number, member in members:
+                for number, member in members + extra:
                     over_tgt(member, number, step, offset).start()
             own = []
             for place, (src, dst) in enumerate(member for all_of in groups for member in all_of):
@@ -716,13 +817,16 @@
                     over_tgt(member, number, step, offset).wait_recv()
                     if 0 < step < 4:
                         over_tgt(member, number, step + 3, offset + 1).start()
-                    over_far(member, number, step, offset).start()
+                    if (number, member) in far_sent:
+                        over_far(member, number, step, offset).start()
                     over_near(member, number, step, offset).start()
-            far_members = list(enumerate(groups[index ^ 2]))
-            near_members = list(enumerate(groups[index ^ 1]))
-            last_members = list(enumerate(groups[index ^ 3]))
+                for number, member in extra:
+                    over_tgt(member, number, step, offset).wait_recv()
+                    if 0 < step < 4:
+                        over_tgt(member, number, step + 3, offset + 1).start()
+                    relay(member, 0, step, offset).start()
             for step, offset in steps:
-                for number, member in far_members:
+                for number, member in far_got:
                     over_far(member, number, step, offset).wait_recv()
                     relay(member, number, step, offset).start()
             for step, offset in steps:
@@ -730,9 +834,11 @@
                     over_near(member, number, step, offset).wait_recv()
                 for number, member in last_members:
                     relay(member, number, step, offset).wait_recv()
+                for number, member in members + extra:
+                    over_tgt(member, number, step, offset).wait_send()
+                for number, member in far_sent:
+                    over_far(member, number, step, offset).wait_send()
                 for number, member in members:
-                    over_tgt(member, number, step, offset).wait_send()
-                    over_far(member, number, step, offset).wait_send()
                     over_near(member, number, step, offset).wait_send()
                 for number, member in far_members:
                     relay(member, number, step, offset).wait_send()
@@ -749,7 +855,7 @@
         return jax.ShapeDtypeStruct((tgts, height, columns), BF)
 
     shapes = (out(3 * inner), out(2 * inner), out(inner), out(model, o_rows), out(model, o_rows))
-    sems = [pltpu.SemaphoreType.DMA((7, 2))] * 8
+    sems = [pltpu.SemaphoreType.DMA((7, 3))] * 2 + [pltpu.SemaphoreType.DMA((7, 2))] * 6
     return pl.pallas_call(
         gather_kernel,
         out_shape=shapes,
@@ -768,9 +874,9 @@
 
 
 def reduce_kernel(
-    qkv_ref, kv_ref, cq_ref, so_ref, co_ref, small_ref,
-    q_out, k_out, v_out, cq_out, ck_out, cv_out, so_out, co_out, small_out,
-    small_in, s_send, s_recv,
+    qkv_ref, kv_ref, cq_ref, so_ref, co_ref, small_ref, units_ref,
+    q_out, k_out, v_out, cq_out, ck_out, cv_out, so_out, co_out, small_out, units_out,
+    small_in, s_send, s_recv, u_send, u_recv, u_own,
     wide_in, tall_in, wide_x, tall_x, wide_y, tall_y, wide_z, tall_z, wide_e, tall_e,
     a_send, a_recv, b_send, b_recv, x_send, x_recv, y_send, y_recv, z_send, z_recv,
     e_send, e_recv,
@@ -835,14 +941,29 @@
             e_send.at[lane, number], e_recv.at[lane, number], mem=peer,
         )
 
-    partners = (
-        {"mem": near}, {"mem": far}, {"tgt": jnp.bitwise_xor(tgt, 1)},
-        {"tgt": jnp.bitwise_xor(tgt, 2)}, {"tgt": jnp.bitwise_xor(tgt, 4)},
-    )
-    small_moves = [
-        peer_copy(small_in.at[0, step], small_in.at[1, step], s_send.at[step], s_recv.at[step], **to)
-        for step, to in enumerate(partners)
+    z_place = tgt // 2
+    y_place = tgt % 2
+    small_mem = [
+        peer_copy(small_in.at[mem], small_in.at[mem], s_send.at[offset], s_recv.at[offset],
+                  mem=jnp.bitwise_xor(mem, offset))
+        for offset in (1, 2, 3)
     ]
+    small_y = peer_copy(small_in.at[4 + y_place], small_in.at[4 + y_place], s_send.at[0],
+                        s_recv.at[0], tgt=jnp.bitwise_xor(tgt, 1))
+    small_z = [
+        peer_copy(small_in.at[6 + z_place], small_in.at[6 + z_place], s_send.at[3 + offset],
+                  s_recv.at[3 + offset], tgt=jnp.bitwise_xor(tgt, 2 * offset))
+        for offset in (1, 2, 3)
+    ]
+    small_in[mem] = small_ref[...]
+    for move in small_mem:
+        move.start()
+
+    share_far = peer_copy(units_ref, units_out.at[mem], u_send.at[0], u_recv.at[0], mem=far)
+    share_near = peer_copy(units_ref, units_out.at[mem], u_send.at[1], u_recv.at[1], mem=near)
+    share_on = peer_copy(units_out.at[far], units_out.at[far], u_send.at[2], u_recv.at[2], mem=near)
+    share_own = pltpu.make_async_copy(units_ref, units_out.at[mem], u_own)
+    share_own.start()
 
     for index, group in enumerate(groups):
 
@@ -867,43 +988,53 @@
                         + member[2][0][1, step, number].astype(F32)
                     ).astype(BF)
                     to_far(member, number, step).start()
-            small_in[0, 0] = small_ref[...]
-            for step, move in enumerate(small_moves):
+            share_far.start()
+            share_near.start()
+            for move in small_mem:
+                move.wait_recv()
+            small_in[4 + y_place] = (small_in[0] + small_in[1]) + (small_in[2] + small_in[3])
+            small_y.start()
+            def mem_sum(member, number, step):
+                to_near(member, number, step, 0).wait_recv()
+                to_far(member, number, step).wait_recv()
+                return (
+                    member[0](jnp.bitwise_xor(tgt, TURNS[step]))[...].astype(F32)
+                    + member[2][0][0, step, number].astype(F32)
+                    + member[2][1][1, step, number].astype(F32)
+                )
+
+            def for_side(turn):
+                for number, member in mine:
+                    member[2][2][0, turn, number] = mem_sum(member, number, 2 * turn).astype(BF)
+                    to_side(member, number, turn).start()
+
+            for_side(0)
+            small_y.wait_recv()
+            small_in[6 + z_place] = small_in[4] + small_in[5]
+            for move in small_z:
                 move.start()
-                move.wait_recv()
-                total = small_in[0, step] + small_in[1, step]
-                if step + 1 < len(small_moves):
-                    small_in[0, step + 1] = total
-                else:
-                    small_out[...] = total
-            for step in steps:
-                place = jnp.bitwise_xor(tgt, TURNS[step])
-                turn = step // 2
+            for_side(1)
+            for_side(2)
+            for_side(3)
+            for turn in range(4):
                 for number, member in mine:
-                    to_near(member, number, step, 0).wait_recv()
-                    to_far(member, number, step).wait_recv()
-                    total = (
-                        member[0](place)[...].astype(F32)
-                        + member[2][0][0, step, number].astype(F32)
-                        + member[2][1][1, step, number].astype(F32)
-                    )
-                    if step % 2 == 0:
-                        member[2][2][0, turn, number] = total.astype(BF)
-                        to_side(member, number, turn).start()
-                        continue
+                    total = mem_sum(member, number, 2 * turn + 1)
                     to_side(member, number, turn).wait_recv()
                     total = total + member[2][2][1, turn, number].astype(F32)
                     if turn < 3:
                         member[2][3][0, turn, number] = total.astype(BF)
                         to_owner(member, number, turn).start()
                         continue
-                    for other in range(3):
-                        to_owner(member, number, other).wait_recv()
-                        total = total + member[2][3][1, other, number].astype(F32)
                     member[2][4][0, number] = total.astype(BF)
-                    to_all(member, number, 1, far).start()
-                    to_all(member, number, 0, near).start()
-                    member[1][...] = member[2][4][0, number]
+            for number, member in mine:
+                total = member[2][4][0, number].astype(F32)
+                for other in range(3):
+                    to_owner(member, number, other).wait_recv()
+                    total = total + member[2][3][1, other, number].astype(F32)
+                member[2][4][0, number] = total.astype(BF)
+                to_all(member, number, 1, far).start()
+                to_all(member, number, 0, near).start()
+                member[1][...] = member[2][4][0, number]
             for number, member in far_group:
                 to_all(member, number, 1, far).wait_recv()
                 to_all(member, number, 2, near).start()
@@ -914,7 +1045,15 @@
             for number, member in last_group:
                 to_all(member, number, 2, near).wait_recv()
                 member[1][...] = member[2][4][3, number]
-            for move in small_moves:
+            for move in small_z:
+                move.wait_recv()
+            small_out[...] = (small_in[6] + small_in[7]) + (small_in[8] + small_in[9])
+            share_far.wait_recv()
+            share_on.start()
+            share_near.wait_recv()
+            share_on.wait_recv()
+            share_own.wait()
+            for move in (*small_mem, small_y, *small_z, share_far, share_near, share_on):
                 move.wait_send()
             for step in steps:
                 for number, member in last_group:
@@ -934,7 +1073,7 @@
                 to_all(member, number, 2, near).wait_send()
 
 
-def reduce_weights(d_qkv, d_kv, d_cq, d_so, d_co, small):
+def reduce_weights(d_qkv, d_kv, d_cq, d_so, d_co, small, units):
     rows, inner = d_cq.shape[1:]
     o_rows, model = d_so.shape[1:]
     wide, tall = (rows, inner), (o_rows, model)
@@ -948,11 +1087,16 @@
         reduce_kernel,
         out_shape=tuple(jax.ShapeDtypeStruct(wide, BF) for _ in range(6))
         + tuple(jax.ShapeDtypeStruct(tall, BF) for _ in range(2))
-        + (jax.ShapeDtypeStruct(small.shape, F32),),
-        in_specs=[VMEM_SPEC] * 6,
-        out_specs=(VMEM_SPEC,) * 9,
-        scratch_shapes=[pltpu.VMEM((2, 5) + small.shape, F32)]
-        + [pltpu.SemaphoreType.DMA((5,))] * 2
+        + (
+            jax.ShapeDtypeStruct(small.shape, F32),
+            jax.ShapeDtypeStruct((4,) + units.shape, BF),
+        ),
+        in_specs=[VMEM_SPEC] * 6 + [ANY_SPEC],
+        out_specs=(VMEM_SPEC,) * 9 + (ANY_SPEC,),
+        scratch_shapes=[pltpu.VMEM((10,) + small.shape, F32)]
+        + [pltpu.SemaphoreType.DMA((7,))] * 2
+        + [pltpu.SemaphoreType.DMA((3,))] * 2
+        + [pltpu.SemaphoreType.DMA]
         + scratch
         + sems,
         compiler_params=pltpu.CompilerParams(
@@ -962,7 +1106,7 @@
             flops=0, bytes_accessed=150 * 1024 * 1024, transcendentals=0
         ),
         name="reduce_weights",
-    )(d_qkv, d_kv, d_cq, d_so, d_co, small)
+    )(d_qkv, d_kv, d_cq, d_so, d_co, small, units)
 
 
 def pick_kernel(tgts, groups, gate_ref, up_ref, out_ref):
@@ -998,7 +1142,14 @@
     )(gate, up)
 
 
-def place_kernel(tgts, groups, parts_ref, gate_ref, up_ref):
+def place_kernel(tgts, groups, parts_ref, down_parts_ref, *refs):
+    count = (len(refs) - 3) // 2
+    gate_ref, up_ref, down_ref = refs[count : count + 3]
+    for src, dst in zip(refs[:count], refs[count + 3 :]):
+        dst[...] = src[...].astype(F32)
+    height = down_parts_ref.shape[1]
+    for group in range(groups):
+        down_ref[group * height : (group + 1) * height, :] = down_parts_ref[group].astype(F32)
     units = gate_ref.shape[1]
     piece = units // tgts // groups
     for number, ref in enumerate((gate_ref, up_ref)):
@@ -1019,71 +1170,57 @@
         )
 
 
-def place_units(parts):
+def place_units(parts, down_parts, sums):
     groups, tgts = lax.axis_size("mem"), lax.axis_size("tgt")
     rows, columns = parts.shape[1:]
-    shape = jax.ShapeDtypeStruct((rows, groups * columns // 2), F32)
+    wide = jax.ShapeDtypeStruct((rows, groups * columns // 2), F32)
+    down = jax.ShapeDtypeStruct((groups * down_parts.shape[1], down_parts.shape[2]), F32)
+    shapes = (wide, wide, down) + tuple(jax.ShapeDtypeStruct(part.shape, F32) for part in sums)
     return pl.pallas_call(
         functools.partial(place_kernel, tgts, groups),
-        out_shape=(shape, shape),
-        in_specs=[VMEM_SPEC],
-        out_specs=(VMEM_SPEC, VMEM_SPEC),
+        out_shape=shapes,
+        in_specs=[VMEM_SPEC] * (2 + len(sums)),
+        out_specs=(VMEM_SPEC,) * len(shapes),
         compiler_params=pltpu.CompilerParams(vmem_limit_bytes=VMEM_CAP),
         name="place_units",
-    )(parts)
-
-
-def share_kernel(wide_ref, tall_ref, wide_out, tall_out, wide_send, wide_recv, tall_send, tall_recv, own):
+    )(parts, down_parts, *sums)
+
+
+def share_kernel(src, out, sends, recvs, own_sem):
     mem = lax.axis_index("mem")
     greet("mem", (1, 2))
     near = jnp.bitwise_xor(mem, 1)
     far = jnp.bitwise_xor(mem, 2)
-    moves = []
-    for src, out, sends, recvs in (
-        (wide_ref, wide_out, wide_send, wide_recv),
-        (tall_ref, tall_out, tall_send, tall_recv),
-    ):
-        to_far = peer_copy(src, out.at[mem], sends.at[0], recvs.at[0], mem=far)
-        to_near = peer_copy(src, out.at[mem], sends.at[1], recvs.at[1], mem=near)
-        relay = peer_copy(out.at[far], out.at[far], sends.at[2], recvs.at[2], mem=near)
-        to_far.start()
-        to_near.start()
-        moves.append((to_far, to_near, relay))
-    copies = [
-        pltpu.make_async_copy(wide_ref, wide_out.at[mem], own.at[0]),
-        pltpu.make_async_copy(tall_ref, tall_out.at[mem], own.at[1]),
-    ]
-    for copy in copies:
-        copy.start()
-    for to_far, _, relay in moves:
-        to_far.wait_recv()
-        relay.start()
-    for to_far, to_near, relay in moves:
-        to_near.wait_recv()
-        relay.wait_recv()
-        to_far.wait_send()
-        to_near.wait_send()
-        relay.wait_send()
-    for copy in copies:
-        copy.wait()
-
-
-def share(wide, tall):
+    to_far = peer_copy(src, out.at[mem], sends.at[0], recvs.at[0], mem=far)
+    to_near = peer_copy(src, out.at[mem], sends.at[1], recvs.at[1], mem=near)
+    pass_on = peer_copy(out.at[far], out.at[far], sends.at[2], recvs.at[2], mem=near)
+    to_far.start()
+    to_near.start()
+    own = pltpu.make_async_copy(src, out.at[mem], own_sem)
+    own.start()
+    to_far.wait_recv()
+    pass_on.start()
+    to_near.wait_recv()
+    pass_on.wait_recv()
+    for copy in (to_far, to_near, pass_on):
+        copy.wait_send()
+    own.wait()
+
+
+def share(value):
     groups = lax.axis_size("mem")
     return pl.pallas_call(
         share_kernel,
-        out_shape=tuple(
-            jax.ShapeDtypeStruct((groups,) + value.shape, BF) for value in (wide, tall)
-        ),
-        in_specs=[ANY_SPEC] * 2,
-        out_specs=(ANY_SPEC,) * 2,
-        scratch_shapes=[pltpu.SemaphoreType.DMA((3,))] * 4 + [pltpu.SemaphoreType.DMA((2,))],
+        out_shape=jax.ShapeDtypeStruct((groups,) + value.shape, BF),
+        in_specs=[ANY_SPEC],
+        out_specs=ANY_SPEC,
+        scratch_shapes=[pltpu.SemaphoreType.DMA((3,))] * 2 + [pltpu.SemaphoreType.DMA],
         compiler_params=pltpu.CompilerParams(collective_id=6, has_side_effects=True),
         cost_estimate=pl.CostEstimate(
-            flops=0, bytes_accessed=60 * 1024 * 1024, transcendentals=0
+            flops=0, bytes_accessed=30 * 1024 * 1024, transcendentals=0
         ),
         name="share_sums",
-    )(wide, tall)
+    )(value)
 
 
 def over_mem(value, offset):
@@ -1102,6 +1239,29 @@
 
 def scatter_tgt(partial):
     return lax.psum_scatter(partial, "tgt", scatter_dimension=0, tiled=True)
+
+
+def in_tiles(value):
+    rows, columns = value.shape
+    value = jnp.pad(value, ((0, 0), (0, -columns % 128)))
+    return value.reshape(rows // 8, 8, -1, 128).swapaxes(1, 2).reshape(-1, 8, 128)
+
+
+def from_tiles(tiles, rows, columns):
+    shards = tiles.shape[0]
+    tiles = tiles.reshape(shards * rows // 8, -1, 8, 128).swapaxes(1, 2)
+    return tiles.reshape(shards * rows, -1)[:, :columns]
+
+
+def gather_units(gate_up, down):
+    if gate_up.shape[0] % 8 or down.shape[0] % 8:
+        return gather_tgt(gate_up), gather_tgt(down)
+    tiles = in_tiles(gate_up)
+    both = lax.all_gather(jnp.concatenate([tiles, in_tiles(down)]), "tgt", axis=0)
+    return (
+        from_tiles(both[:, : tiles.shape[0]], *gate_up.shape),
+        from_tiles(both[:, tiles.shape[0] :], *down.shape),
+    )
 
 
 def attention_weights(weights):
@@ -1117,9 +1277,9 @@
     )
 
 
-def attention_sums(partials, small):
+def weight_sums(partials, small, units):
     if lax.axis_size("tgt") == 8:
-        return reduce_weights(*partials, small)
+        return reduce_weights(*partials, small, units)
     inner = HEADS * HEAD
     totals = [
         lax.psum_scatter(partial, "tgt", scatter_dimension=0, tiled=False) for partial in partials
@@ -1128,6 +1288,7 @@
     return (
         qkv[:, :inner], qkv[:, inner : 2 * inner], qkv[:, 2 * inner :], cq,
         kv[:, :inner], kv[:, inner:], so, co, lax.psum(small, ("tgt", "mem")),
+        lax.all_gather(units, "mem", axis=0),
     )
 
 
@@ -1169,16 +1330,14 @@
             (self_q, self_k, self_v, cross_q, cross_k, cross_v, self_o, cross_o)
         )
     )
-    gate_up = gather_tgt(pick_units(ffn_gate, ffn_up))
-    down = gather_tgt(
-        lax.dynamic_slice_in_dim(ffn_down, mem_index * piece, piece, axis=0)
-    )
+    gate_up = pick_units(ffn_gate, ffn_up)
+    down = lax.dynamic_slice_in_dim(ffn_down, mem_index * piece, piece, axis=0)
+    gate_up, down = gather_units(gate_up, down)
 
     inputs = padded(target).astype(F32)
     upstream_low = padded(out_grad)
     late, self_w = lax.optimization_barrier((upstream_low, self_w))
     upstreams = gather_mem(late)
-    mem_flat = memory.reshape(all_items * positions_dev, model)
 
     h1 = (inputs * rms_scale(inputs) * norm_self).astype(BF)
     qkv = dot(h1, self_w).astype(BF).reshape(items, ROWS, 3 * inner)
@@ -1186,18 +1345,17 @@
     y1 = inputs + dot(att, self_o_w)
     h2 = (y1 * rms_scale(y1) * norm_cross).astype(BF)
     cq = dot(h2, cross_q_w).astype(BF).reshape(items, ROWS, inner)
-    ckv = dot(mem_flat, cross_kv_w).astype(BF)
-    ck = ckv[:, :inner].reshape(all_items, positions_dev, inner)
-    cv = ckv[:, inner:].reshape(all_items, positions_dev, inner)
-    all_queries, catt, lse = cross_fwd(cq, ck, cv, bias)
+    ckv = jnp.einsum(
+        "npd,dc->npc", memory, cross_kv_w, preferred_element_type=F32
+    ).astype(BF)
+    all_queries, catt, lse = cross_fwd(cq, ckv, bias)
     catt = catt.reshape(tokens, inner)
     y2 = y1 + dot(catt, cross_o_w)
     h3 = (y2 * rms_scale(y2) * norm_ffn).astype(BF)
 
-    h3_back, out_near, out_far, grad_gate_up, grad_down = ffn(h3, upstreams, gate_up, down)
+    h3_back, out_near, out_far, grad_gate_up, grad_down = ffn(h3, upstreams, gate_up, down, items)
     out_sum = over_mem(out_far, 2)
     grad_gate_up = scatter_tgt(grad_gate_up)
-    grad_down = scatter_tgt(grad_down)
     dx, grad_norm_ffn = rms_back(y2, norm_ffn, h3_back)
     dy2 = upstream_low.astype(F32) + dx
     e2 = dy2.astype(BF)
@@ -1209,17 +1367,19 @@
     stats = jnp.concatenate(
         [lse[:, :, :8], delta, jnp.zeros((items, ROWS, STATS - 8 - HEADS), F32)], axis=-1
     )
-    dck, dcv, dcq = cross_bwd(
-        all_queries, dcatt.reshape(items, ROWS, inner), stats, ck, cv, bias
-    )
-    y2_late, dcq = lax.optimization_barrier((y2, dcq))
+    dckv, dcq = cross_bwd(
+        all_queries, dcatt.reshape(items, ROWS, inner), stats, ckv, bias
+    )
+    y2_late, grad_down, dcq = lax.optimization_barrier((y2, grad_down, dcq))
+    grad_down = scatter_tgt(grad_down)
     layer_out = trimmed(
         (y2_late + out_near.astype(F32) + out_sum.astype(F32)).astype(BF)
     )
-    dckv = jnp.concatenate([dck, dcv], axis=-1).reshape(all_items * positions_dev, 2 * inner)
     dcq = dcq.reshape(tokens, inner)
-    grad_cross_kv = dot_tn(mem_flat, dckv)
-    memory_grad = dot_nt(dckv, cross_kv_w).astype(BF).reshape(memory.shape)
+    grad_cross_kv = jnp.einsum("npd,npc->dc", memory, dckv, preferred_element_type=F32)
+    memory_grad = jnp.einsum(
+        "npc,dc->npd", dckv, cross_kv_w, preferred_element_type=F32
+    ).astype(BF)
     grad_cross_q = dot_tn(h2, dcq)
     dx, grad_norm_cross = rms_back(y1, norm_cross, dot_nt(dcq, cross_q_w))
     dy1 = dy2 + dx
@@ -1238,18 +1398,17 @@
     small = jnp.concatenate(
         [grad_norm_self, grad_norm_cross, grad_norm_ffn, table.reshape(-1)]
     )
-    *sums, small = attention_sums(
+    *sums, small, grad_gate_up = weight_sums(
         tuple(
             partial.astype(BF).reshape(tgts, -1, partial.shape[-1])
             for partial in (grad_self, grad_cross_kv, grad_cross_q, grad_self_o, grad_cross_o)
         ),
         jnp.pad(small, (0, -small.size % 1024)).reshape(-1, 128),
-    )
-    columns = [partial.astype(F32) for partial in sums]
-    grad_gate_up, grad_down, small = lax.optimization_barrier((grad_gate_up, grad_down, small))
-    grad_gate_up, grad_down = share(grad_gate_up, grad_down)
-    grad_gate, grad_up = place_units(grad_gate_up)
-    grad_down = grad_down.reshape(-1, model).astype(F32)
+        grad_gate_up,
+    )
+    grad_down, small = lax.optimization_barrier((grad_down, small))
+    grad_down = share(grad_down)
+    grad_gate, grad_up, grad_down, *columns = place_units(grad_gate_up, grad_down, sums)
     small = small.reshape(-1)
     norms = [small[start : start + model] for start in range(0, 3 * model, model)]
     table = small[3 * model : 3 * model + table.size].reshape(table.shape)

time: 550 us -> 501 us (0.911)
  Pallas kernels: 392 us -> 348 us
  local copies, waits for them, and re-layouts: 60.2 us -> 45.4 us
  matrix products: 45 us -> 54.1 us
  waiting for transfers between devices: 3.33 us -> 11.5 us
  other arithmetic: 27.8 us -> 20.7 us
    pallas_call x3, Pallas kernels: 122 us -> 94.9 us  [the longest x1 75.6 us: ffn(): pl.pallas_call(functools.partial(ffn_kernel, items), out_shape=(jax.Shape...]
    dot_general x0 -> x3, matrix products: none -> 19.9 us  [the longest x1 7.18 us: on_device(): jnp.einsum('npd,dc->npc', memory, cross_kv_w, preferred_element_type=F32)]
    convert_element_type x9 -> x0, other arithmetic: 13.3 us -> none  [the longest x8 11.3 us: on_device(): columns = [partial.astype(F32) for partial in sums]]
    reshape x2 -> x0, local copies, waits for them, and re-layouts: 12.9 us -> none  [the longest x1 7.05 us: on_device(): mem_flat = memory.reshape(all_items * positions_dev, model)]
    pallas_call x1, Pallas kernels: 114 us -> 101 us  [reduce_weights(): pl.pallas_call(reduce_kernel, out_shape=tuple((jax.ShapeDtypeStruct(wide,...]
    dot_general x5 -> x4, matrix products: 13.3 us -> 7.87 us  [dot(): return jnp.dot(left, right, preferred_element_type=F32)]
    dot_general x5 -> x4, matrix products: 15.1 us -> 12.2 us  [dot_tn(): return lax.dot_general(left, right, TN, preferred_element_type=F32)]
    unnamed x138 -> x109, local copies, waits for them, and re-layouts: 15.7 us -> 13 us
  transfers between devices with their start and end apart: 8 -> 7, of which waited for: 1 -> 2; matrix products, arithmetic and copies ran while one was open for 22% -> 20% of each run, Pallas kernels for 49% -> 50%
where the time goes in v3:
time: 501 us; the launch traced here: 497 us
  Pallas kernels  348 us (69%)
  matrix products  54.1 us (11%)
  local copies, waits for them, and re-layouts  45.4 us (9%)
  other arithmetic  20.7 us (4%)
  between operations  14.8 us (3%)
  waiting for transfers between devices  11.5 us (2%)
    pallas_call x1, Pallas kernels, reduce_weights(): pl.pallas_call(reduce_kernel, out_shape=tuple((jax.ShapeDtypeStruct(wide,...  101 us
    pallas_call x1, Pallas kernels, ffn(): pl.pallas_call(functools.partial(ffn_kernel, items), out_shape=(jax.Shape...  75.6 us
    pallas_call x1, Pallas kernels, gather_weights(): pl.pallas_call(gather_kernel, out_shape=shapes, in_specs=[ANY_SPEC] * 8,...  60.9 us
    pallas_call x1, Pallas kernels, cross_fwd(): pl.pallas_call(functools.partial(cross_fwd_kernel, items), out_shape=(jax...  38.3 us
    pallas_call x1, Pallas kernels, cross_bwd(): pl.pallas_call(functools.partial(cross_bwd_kernel, items), out_shape=(jax...  36 us
    dot_general x4, matrix products, dot_nt(): return lax.dot_general(left, right, NT, preferred_element_type=F32)  13.1 us
    unnamed x109, local copies, waits for them, and re-layouts  13 us
    dot_general x4, matrix products, dot_tn(): return lax.dot_general(left, right, TN, preferred_element_type=F32)  12.2 us
  transfers between devices with their start and end apart: 7, of which 2 were waited for; matrix products, arithmetic and copies ran while one was open for 20% of the time, Pallas kernels for 50%

profile of v3, /device:TPU:0, one launch (start us, length us, event | category | flops | bytes accessed | tf_op | source)
XLA Modules:
  0.0 497.2 jit_solution(9279372789051683301)
XLA Ops:
  8.6 3.0 pick_units.1
  14.1 60.9 %gather_weights.1 = (bf16[8,184,1152]{2,1,0:T(8,128)(2,1)}, bf16[8,184,768]{2,1,0:T(8,128)(2,1)}, bf16[8,184,384]{2,1,0:T(8,128)(2,1)}, bf16[8,48,1472]{2,1,0:T(8,128)(2,1)}, bf16[8,48,1472]{2,1,0:T(8,128)(2,1)}) custom-call(bf16[184,384]{1,0:T(8,128)(2,1)} %self_q.1, bf16[184,384]{1,0:T(8,128)(2,1)} %self_k.1, bf16[184,384]{1,0:T(8,128)(2,1)} %self_v.1, ...), custom_call_target="tpu_custom_call" | custom-call | bytes 157286400 | tf_op jit(solution)/shard_map/gather_weights/pallas_call | solution.py:859
  81.0 2.3 copy-done.43
  83.3 2.6 convolution_convert_fusion.4
  86.0 7.2 %convert_bitcast_fusion.kv_ref = bf16[8,256,768]{2,1,0:T(8,128)(2,1)} fusion(bf16[1472,768,1]{1,0,2:T(8,128)(2,1)S(1)} %bitcast.158, bf16[8,256,1472]{1,2,0:T(8,128)(2,1)S(1)} %bitcast.153), kind=kOutput, calls=%fused_computation.4 | convolution fusion | flops 4632084480 | bytes 11436032 | tf_op jit(solution)/shard_map/npd,dc->npc/dot_general | solution.py:1348
  94.5 4.5 self_fwd.1
  102.5 38.3 %cross_fwd.1 = (bf16[4,2,192,384]{3,2,1,0:T(8,128)(2,1)}, bf16[2,192,384]{2,1,0:T(8,128)(2,1)}, f32[2,192,128]{2,1,0:T(8,128)}) custom-call(bf16[2,192,384]{2,1,0:T(8,128)(2,1)} %bitcast.147, bf16[8,256,768]{2,1,0:T(8,128)(2,1)} %convert_bitcast_fusion.kv_ref, f32[8,1,256]{2,1,0:T(1,128)} %broadcast_in_dim.9.bias_ref), custom_call_target="tpu_custom_call" | custom-call | flops 1207959552 | bytes 8388608 | tf_op jit(solution)/shard_map/cross_fwd/pallas_call | solution.py:327
  146.6 2.4 copy.106.up2_ref
  149.0 2.4 copy.105.up1_ref
  153.4 6.6 %all-gather.3.cloned.1.call-done = bf16[3920,8,128]{2,1,0:T(8,128)(2,1)} async-done(((bf16[490,8,128]{2,1,0:T(8,128)(2,1)}), bf16[3920,8,128]{2,1,0:T(8,128)(2,1)}) %all-gather.3.cloned.1.call-update) | async-done | bytes 8028176 | tf_op jit(solution)/shard_map/all_gather | solution.py:1260
  160.0 5.2 %slice.44 = bf16[8,322,8,128]{3,2,1,0:T(8,128)(2,1)} slice(bf16[8,490,8,128]{3,2,1,0:T(8,128)(2,1)} %bitcast.117), slice={[0:8], [0:322], [0:8], [0:128]} | slice | bytes 10551296 | tf_op jit(solution)/shard_map/slice | solution.py:1262
  165.3 3.5 slice.45
  168.8 75.6 %feed_forward.1 = (f32[384,1472]{1,0:T(8,128)}, bf16[384,1472]{1,0:T(8,128)(2,1)}, bf16[384,1472]{1,0:T(8,128)(2,1)}, bf16[1472,1792]{1,0:T(8,128)(2,1)}, bf16[896,1472]{1,0:T(8,128)(2,1)}) custom-call(bf16[384,1472]{1,0:T(8,128)(2,1)} %multiply_convert_fusion.1.h_ref, bf16[384,1472]{1,0:T(8,128)(2,1)} %bitcast.116, bf16[384,1472]{1,0:T(8,128)(2,1)} %copy.105.up1_ref, ...), custom_call_target="tpu_custom_call" | custom-call | flops 36465278976 | bytes 33554432 | tf_op jit(solution)/shard_map/feed_forward/pallas_call | solution.py:675
  245.7 3.5 multiply_convert_fusion
  249.1 3.0 multiply_reduce_fusion
  257.0 36.0 %cross_bwd.1 = (bf16[8,256,768]{2,1,0:T(8,128)(2,1)}, bf16[2,192,384]{2,1,0:T(8,128)(2,1)}) custom-call(bf16[4,2,192,384]{3,2,1,0:T(8,128)(2,1)} %get-tuple-element.72.all_ref, bf16[2,192,384]{2,1,0:T(8,128)(2,1)} %bitcast.146, f32[2,192,128]{2,1,0:T(8,128)} %maximum_maximum_fusion.stat_ref, bf16[8,256,768]{2,1,0:T(8,128)(2,1)} %convert_bitcast_fusion.kv_ref, ...), custom_call_target="tpu_custom_call" | custom-call | flops 3019898880 | bytes 12582912 | tf_op jit(solution)/shard_map/cross_bwd/pallas_call | solution.py:444
  293.0 2.7 multiply_reduce_fusion.1
  297.7 3.2 convolution_convert_fusion.5
  300.9 9.4 %self_bwd.1 = (bf16[2,192,1152]{2,1,0:T(8,128)(2,1)}, f32[8,256]{1,0:T(8,128)}) custom-call(bf16[2,192,1152]{2,1,0:T(8,128)(2,1)} %bitcast.144, bf16[2,192,384]{2,1,0:T(8,128)(2,1)} %bitcast.148, f32[8,256]{1,0:T(8,128)} %pad.21.base_ref), custom_call_target="tpu_custom_call" | custom-call | flops 754974720 | bytes 2064384 | tf_op jit(solution)/shard_map/self_bwd/pallas_call | solution.py:196
  311.3 2.7 convolution_convert_fusion.2
  316.3 2.7 convolution_convert_fusion.1
  321.1 5.7 %fusion.8 = (f32[1472]{0:T(1024)}, f32[384]{0:T(512)S(1)}, f32[384,1472]{1,0:T(8,128)S(1)}) fusion(f32[2,192,1472]{2,1,0:T(8,128)} %copy-done.7, f32[384]{0:T(512)S(1)} %copy-done.31, f32[1472]{0:T(1024)S(1)} %convert_element_type.108, bf16[384,1152]{1,0:T(8,128)(2,1)} %bitcast.160, bf16[1472,1152]{1,0:T(8,128)(2,1)} %bitcast.156), kind=kOutput, calls=%fused_computation.22 | convolution fusion | flops 1305720960 | bytes 8813056 | tf_op jit(solution)/shard_map/dot_general | solution.py:53
  326.8 2.6 fusion.6
  329.4 2.2 copy.131
  336.5 3.0 convolution_convert_fusion.3
  339.5 3.9 fusion
  343.4 6.7 %convolution_convert_fusion = bf16[8,256,1472]{1,2,0:T(8,128)(2,1)} fusion(bf16[8,256,768]{2,1,0:T(8,128)(2,1)S(1)} %copy-done.47, bf16[1472,768,1]{1,0,2:T(8,128)(2,1)S(1)} %bitcast.159), kind=kOutput, calls=%fused_computation.2 | convolution fusion | flops 4633526272 | bytes 11436032 | tf_op jit(solution)/shard_map/npc,dc->npd/dot_general | solution.py:1380
  350.1 6.0 %bitcast_convert_fusion = bf16[768,1472]{0,1:T(8,128)(2,1)} fusion(bf16[8,256,1472]{1,2,0:T(8,128)(2,1)S(1)} %bitcast.155, bf16[8,256,768]{2,1,0:T(8,128)(2,1)S(1)} %copy-done.47), kind=kOutput, calls=%fused_computation.3 | convolution fusion | flops 4631642112 | bytes 11436032 | tf_op jit(solution)/shard_map/npd,npc->dc/dot_general | solution.py:1379
  356.1 4.8 collective-permute-done.3
  366.8 101.3 %reduce_weights.1 = (bf16[184,384]{1,0:T(8,128)(2,1)}, bf16[184,384]{1,0:T(8,128)(2,1)}, bf16[184,384]{1,0:T(8,128)(2,1)}, bf16[184,384]{1,0:T(8,128)(2,1)}, bf1...) custom-call(bf16[8,184,1152]{2,1,0:T(8,128)(2,1)} %bitcast.131, ...), custom_call_target="tpu_custom_call" | custom-call | bytes 157286400 | tf_op jit(solution)/shard_map/reduce_weights/pallas_call | solution.py:1086
  470.4 12.1 %share_sums.1.down_parts_ref = bf16[4,112,1472]{2,1,0:T(8,128)(2,1)} custom-call(bf16[112,1472]{1,0:T(8,128)(2,1)} %reduce-scatter.3.cloned.1.call-done.src), custom_call_target="tpu_custom_call" | custom-call | bytes 31457280 | tf_op jit(solution)/shard_map/share_sums/pallas_call | solution.py:1212
  483.2 7.2 %place_units.1 = (f32[184,3584]{1,0:T(8,128)}, f32[184,3584]{1,0:T(8,128)}, f32[448,1472]{1,0:T(8,128)}, f32[184,384]{1,0:T(8,128)}, f32[184,384]{1,0:T(8,128)},...) custom-call(bf16[4,184,1792]{2,1,0:T(8,128)(2,1)} %get-tuple-element, ...), custom_call_target="tpu_custom_call" | custom-call | tf_op jit(solution)/shard_map/place_units/pallas_call | solution.py:1179
  (174 shorter events, 49.3 us)
Async XLA Ops:
  7.2 152.8 %all-gather.3.cloned.1.call-start = ((), (), s32[]{:S(2)}) async-start(), calls=%async_computation.4 | async-start | bytes 9031680 | tf_op jit(solution)/shard_map/all_gather | solution.py:1260
  8.6 5.2 %copy-start.25 = (bf16[2,189,1472]{2,0,1:T(2,128)(2,1)S(1)}, bf16[2,189,1472]{2,0,1:T(2,128)(2,1)}, u32[]{:S(2)}) copy-start(bf16[2,189,1472]{2,0,1:T(2,128)(2,1)} %param.25) | copy-start | bytes 3338500
  13.8 353.1 %reduce-scatter.5.cloned.1.call-start = ((), (), s32[]{:S(2)}) async-start(), calls=%async_computation.3 | async-start | bytes 5935104 | tf_op jit(solution)/shard_map/reduce_scatter | solution.py:1241
  14.0 62.5 %copy-start.13 = (bf16[2,189,1472]{2,0,1:T(2,128)(2,1)S(1)}, bf16[2,189,1472]{2,0,1:T(2,128)(2,1)}, u32[]{:S(2)}) copy-start(bf16[2,189,1472]{2,0,1:T(2,128)(2,1)} %param.21) | copy-start | bytes 3338500
  14.1 64.0 %copy-start.11 = (bf16[2,192,1472]{2,1,0:T(8,128)(2,1)}, bf16[2,192,1472]{2,1,0:T(8,128)(2,1)S(1)}, u32[]{:S(2)}) copy-start(bf16[2,192,1472]{2,1,0:T(8,128)(2,1)S(1)} %pad.20.clone) | copy-start | bytes 3391492
  76.4 64.4 %collective-permute-start.1 = (bf16[384,1472]{0,1:T(8,128)(2,1)}, bf16[384,1472]{0,1:T(8,128)(2,1)}, u32[]{:S(2)}, u32[]{:S(2)}) collective-permute-start(bf16[384,1472]{0,1:T(8,128)(2,1)} %copy.103), channel_id=1, source_target_pairs={{0,2},{1,3},{2,0},{3,1},{4,6},{5,7},{6,4},{7,5},{8,10},{9,11},{10,... | collective-permute-start | bytes 3391496 | tf_op jit(solution)/shard_map/ppermute | solution.py:1227
  76.4 72.6 %collective-permute-start = (bf16[384,1472]{0,1:T(8,128)(2,1)}, bf16[384,1472]{0,1:T(8,128)(2,1)}, u32[]{:S(2)}, u32[]{:S(2)}) collective-permute-start(bf16[384,1472]{0,1:T(8,128)(2,1)} %copy.103), channel_id=1, source_target_pairs={{0,1},{1,0},{2,3},{3,2},{4,5},{5,4},{6,7},{7,6},{8,9},{9,8},{10,11... | collective-permute-start | bytes 3391496 | tf_op jit(solution)/shard_map/ppermute | solution.py:1227
  80.5 18.5 %copy-start.7 = (f32[2,192,1472]{2,1,0:T(8,128)}, f32[2,192,1472]{2,1,0:T(8,128)S(1)}, u32[]{:S(2)}) copy-start(f32[2,192,1472]{2,1,0:T(8,128)S(1)} %copy.97) | copy-start | bytes 6782980
  80.7 5.2 %slice-start = ((s8[6029312]{0:T(1024)(128)(4,1)}), s8[4194304]{0:T(1024)(128)(4,1)S(1)}, s32[]{:S(2)}) async-start(s8[6029312]{0:T(1024)(128)(4,1)} %bitcast.152), calls=%async_computation.5 | async-start | bytes 8388608
  86.0 7.2 %copy-start.36 = (f32[8,256]{1,0:T(8,128)S(1)}, f32[8,256]{1,0:T(8,128)}, u32[]{:S(2)}) copy-start(f32[8,256]{1,0:T(8,128)} %param.24) | copy-start | bytes 24580
  86.0 7.2 %copy-start.41 = (s32[8]{0:T(128)S(1)}, s32[8]{0:T(128)}, u32[]{:S(2)}) copy-start(s32[8]{0:T(128)} %param.23) | copy-start | bytes 100
  86.0 7.3 %copy-start.38 = (bf16[1472]{0:T(1024)(128)(2,1)S(1)}, bf16[1472]{0:T(1024)(128)(2,1)}, u32[]{:S(2)}) copy-start(bf16[1472]{0:T(1024)(128)(2,1)} %param.27) | copy-start | bytes 8836
  86.0 7.9 %copy-start.39 = (bf16[1472]{0:T(1024)(128)(2,1)S(1)}, bf16[1472]{0:T(1024)(128)(2,1)}, u32[]{:S(2)}) copy-start(bf16[1472]{0:T(1024)(128)(2,1)} %param.28) | copy-start | bytes 8836
  86.0 13.0 %copy-start.16 = (bf16[8,48,1472]{2,1,0:T(8,128)(2,1)S(1)}, bf16[8,48,1472]{2,1,0:T(8,128)(2,1)}, u32[]{:S(2)}) copy-start(bf16[8,48,1472]{2,1,0:T(8,128)(2,1)} %get-tuple-element.65) | copy-start | bytes 3391492
  100.9 39.9 %copy-start.32 = (f32[384]{0:T(512)}, f32[384]{0:T(512)S(1)}, u32[]{:S(2)}) copy-start(f32[384]{0:T(512)S(1)} %get-tuple-element.171) | copy-start | bytes 4612
  100.9 41.2 %copy-start.2 = (f32[384,1472]{1,0:T(8,128)}, f32[384,1472]{1,0:T(8,128)S(1)}, u32[]{:S(2)}) copy-start(f32[384,1472]{1,0:T(8,128)S(1)} %get-tuple-element.172) | copy-start | bytes 6782980
  102.5 39.6 %copy-start.18 = (bf16[8,48,1472]{2,1,0:T(8,128)(2,1)S(1)}, bf16[8,48,1472]{2,1,0:T(8,128)(2,1)}, u32[]{:S(2)}) copy-start(bf16[8,48,1472]{2,1,0:T(8,128)(2,1)} %get-tuple-element.69) | copy-start | bytes 3391492
  140.8 10.6 %collective-permute-start.2 = (bf16[384,1472]{0,1:T(8,128)(2,1)}, bf16[384,1472]{0,1:T(8,128)(2,1)S(1)}, u32[]{:S(2)}, u32[]{:S(2)}) collective-permute-start(bf16[384,1472]{0,1:T(8,128)(2,1)} %collective-permute-done.1), channel_id=1, source_target_pairs={{0,1},{1,0},{2,3},{3,2},{4,5},{5,4},{6,7},{7,6},{8,9},{9,8},{10,11... | collective-permute-start | bytes 3391496 | tf_op jit(solution)/shard_map/ppermute | solution.py:1227
  244.4 4.7 copy-start.5
  244.4 223.7 %reduce-scatter.3.cloned.1.call-start = ((), (), s32[]{:S(2)}) async-start(), calls=%async_computation.2 | async-start | bytes 3096576 | tf_op jit(solution)/shard_map/reduce_scatter | solution.py:1241
  257.0 36.0 %copy-start.3 = (f32[384,1472]{1,0:T(8,128)S(1)}, f32[384,1472]{1,0:T(8,128)}, u32[]{:S(2)}) copy-start(f32[384,1472]{1,0:T(8,128)} %copy-done.2) | copy-start | bytes 6782980
  257.0 36.0 %copy-start.21 = (bf16[8,184,384]{2,1,0:T(8,128)(2,1)S(1)}, bf16[8,184,384]{2,1,0:T(8,128)(2,1)}, u32[]{:S(2)}) copy-start(bf16[8,184,384]{2,1,0:T(8,128)(2,1)} %get-tuple-element.66) | copy-start | bytes 3391492
  297.7 12.6 %copy-start.29 = (f32[32,256]{1,0:T(8,128)S(1)}, f32[32,256]{1,0:T(8,128)}, u32[]{:S(2)}) copy-start(f32[32,256]{1,0:T(8,128)} %constant.32.clone) | copy-start | bytes 98308
  316.3 4.8 copy-start.31
  321.1 5.7 %copy-start.8 = (f32[2,192,1472]{2,1,0:T(8,128)S(1)}, f32[2,192,1472]{2,1,0:T(8,128)}, u32[]{:S(2)}) copy-start(f32[2,192,1472]{2,1,0:T(8,128)} %copy-done.7) | copy-start | bytes 6782980
  333.0 6.5 %copy-start.24 = (bf16[2,192,1472]{2,0,1:T(2,128)(2,1)S(1)}, bf16[2,192,1472]{2,0,1:T(2,128)(2,1)}, u32[]{:S(2)}) copy-start(bf16[2,192,1472]{2,0,1:T(2,128)(2,1)} %multiply_convert_fusion) | copy-start | bytes 3391492
  333.0 28.0 %collective-permute-start.3 = (bf16[384,1472]{0,1:T(8,128)(2,1)}, bf16[384,1472]{0,1:T(8,128)(2,1)}, u32[]{:S(2)}, u32[]{:S(2)}) collective-permute-start(bf16[384,1472]{0,1:T(8,128)(2,1)} %copy.110), channel_id=1, source_target_pairs={{0,2},{1,3},{2,0},{3,1},{4,6},{5,7},{6,4},{7,5},{8,10},{9,11},{10,... | collective-permute-start | bytes 3391496 | tf_op jit(solution)/shard_map/ppermute | solution.py:1227
  335.1 4.4 copy-start.46
  339.5 10.6 %slice-start.2 = ((s8[6029312]{0:T(1024)(128)(4,1)}), s8[4194304]{0:T(1024)(128)(4,1)S(1)}, s32[]{:S(2)}) async-start(s8[6029312]{0:T(1024)(128)(4,1)} %bitcast.154), calls=%async_computation.7 | async-start | bytes 8388608
  343.4 6.7 %slice-start.3 = ((s8[6029312]{0:T(1024)(128)(4,1)}), s8[1835008]{0:T(1024)(128)(4,1)S(1)}, s32[]{:S(2)}) async-start(s8[6029312]{0:T(1024)(128)(4,1)} %bitcast.154), calls=%async_computation.8 | async-start | bytes 3670016
  350.1 12.6 %copy-start.6 = (f32[384,1472]{1,0:T(8,128)S(1)}, f32[384,1472]{1,0:T(8,128)}, u32[]{:S(2)}) copy-start(f32[384,1472]{1,0:T(8,128)} %copy-done.4) | copy-start | bytes 6782980
  483.2 7.2 %copy-start.1 = (bf16[448,1472]{1,0:T(8,128)(2,1)S(1)}, bf16[448,1472]{1,0:T(8,128)(2,1)}, u32[]{:S(2)}) copy-start(bf16[448,1472]{1,0:T(8,128)(2,1)} %param.40) | copy-start | bytes 3956740
  (27 other events, 55.3 us)
Sparse Core Ops, SparseCore 0:
  13.9 146.0 all-gather.2
  244.5 109.0 reduce-scatter.4
  357.6 90.0 reduce-scatter.2

commit v4 on v3

--- a/solution.py
+++ b/solution.py
@@ -75,6 +75,16 @@
     return low, 1 - low
 
 
+def stacked(value, masks):
+    return jnp.concatenate([value * masks[0], value * masks[1]], axis=0)
+
+
+def joined_heads(value):
+    rows = value.shape[0] // 2
+    is_low = lax.broadcasted_iota(jnp.int32, (1, 2 * HEAD), 1) < HEAD
+    return jnp.where(is_low, value[:rows], value[rows:])
+
+
 def pair(index):
     return slice(index * 2 * HEAD, (index + 1) * 2 * HEAD)
 
@@ -82,6 +92,12 @@
 def head_bias(base_ref, head):
     row = jnp.broadcast_to(base_ref[head : head + 1, :], (ROWS, SPAN))
     return pltpu.roll(row, 0, 1, stride=1, stride_axis=0)
+
+
+def two_biases(base_ref, index, causal):
+    return jnp.concatenate(
+        [jnp.where(causal, head_bias(base_ref, 2 * index + half), NEG) for half in range(2)], axis=0
+    )
 
 
 def causal_mask():
@@ -100,20 +116,15 @@
     causal = causal_mask()
     masks = half_masks()
     for index in range(HEADS // 2):
-        sums = [None] * items
-        for half in range(2):
-            bias = head_bias(base_ref, 2 * index + half)
-            for item in range(items):
-                query = qkv_ref[item, :, pair(index)] * masks[half]
-                scores = dot_nt(query, k_pad[item, :, pair(index)]) + bias
-                scores = jnp.where(causal, scores, NEG)
-                top = jnp.max(scores, axis=-1, keepdims=True)
-                probs = jnp.exp(scores - top)
-                probs = probs * (1.0 / jnp.sum(probs, axis=-1, keepdims=True))
-                part = dot(probs.astype(BF), v_pad[item, :, pair(index)] * masks[half])
-                sums[item] = part if half == 0 else sums[item] + part
+        bias = two_biases(base_ref, index, causal)
         for item in range(items):
-            att_ref[item, :, pair(index)] = sums[item].astype(BF)
+            query = stacked(qkv_ref[item, :, pair(index)], masks)
+            scores = dot_nt(query, k_pad[item, :, pair(index)]) + bias
+            top = jnp.max(scores, axis=-1, keepdims=True)
+            probs = jnp.exp(scores - top)
+            probs = probs * (1.0 / jnp.sum(probs, axis=-1, keepdims=True))
+            part = dot(probs.astype(BF), v_pad[item, :, pair(index)])
+            att_ref[item, :, pair(index)] = joined_heads(part).astype(BF)
 
 
 def self_fwd(qkv, base):
@@ -156,38 +167,31 @@
     causal = causal_mask()
     masks = half_masks()
     for index in range(HEADS // 2):
-        dq = [None] * items
-        dk = [None] * items
-        dv = [None] * items
+        bias = two_biases(base_ref, index, causal)
+        ds_sum = None
+        for item in range(items):
+            query = stacked(qkv_ref[item, :, pair(index)], masks)
+            upstream = stacked(datt_ref[item, :, pair(index)], masks)
+            keys = k_pad[item, :, pair(index)]
+            scores = dot_nt(query, keys) + bias
+            top = jnp.max(scores, axis=-1, keepdims=True)
+            probs = jnp.exp(scores - top)
+            probs = probs * (1.0 / jnp.sum(probs, axis=-1, keepdims=True))
+            dprobs = dot_nt(upstream, v_pad[item, :, pair(index)])
+            delta = jnp.sum(probs * dprobs, axis=-1, keepdims=True)
+            ds = probs * (dprobs - delta)
+            ds_sum = ds if item == 0 else ds_sum + ds
+            ds_low = ds.astype(BF)
+            dqkv_ref[item, :, pair(index)] = joined_heads(dot(ds_low, keys)).astype(BF)
+            dqkv_ref[item, :, pair(index + 3)] = dot_tn(ds_low, query)[:ROWS].astype(BF)
+            dqkv_ref[item, :, pair(index + 6)] = dot_tn(probs.astype(BF), upstream)[
+                :ROWS
+            ].astype(BF)
         for half in range(2):
             head = 2 * index + half
-            bias = head_bias(base_ref, head)
-            ds_sum = None
-            for item in range(items):
-                query = qkv_ref[item, :, pair(index)] * masks[half]
-                upstream = datt_ref[item, :, pair(index)] * masks[half]
-                keys = k_pad[item, :, pair(index)]
-                scores = dot_nt(query, keys) + bias
-                scores = jnp.where(causal, scores, NEG)
-                top = jnp.max(scores, axis=-1, keepdims=True)
-                probs = jnp.exp(scores - top)
-                probs = probs * (1.0 / jnp.sum(probs, axis=-1, keepdims=True))
-                dprobs = dot_nt(upstream, v_pad[item, :, pair(index)])
-                delta = jnp.sum(probs * dprobs, axis=-1, keepdims=True)
-                ds = probs * (dprobs - delta)
-                ds_sum = ds if item == 0 else ds_sum + ds
-                ds_low = ds.astype(BF)
-                q_part = dot(ds_low, keys * masks[half])
-                k_part = dot_tn(ds_low, query)[:ROWS]
-                v_part = dot_tn(probs.astype(BF), upstream)[:ROWS]
-                dq[item] = q_part if half == 0 else dq[item] + q_part
-                dk[item] = k_part if half == 0 else dk[item] + k_part
-                dv[item] = v_part if half == 0 else dv[item] + v_part
-            diag_ref[head : head + 1, :] = diagonal_sums(ds_sum)
-        for item in range(items):
-            dqkv_ref[item, :, pair(index)] = dq[item].astype(BF)
-            dqkv_ref[item, :, pair(index + 3)] = dk[item].astype(BF)
-            dqkv_ref[item, :, pair(index + 6)] = dv[item].astype(BF)
+            diag_ref[head : head + 1, :] = diagonal_sums(
+                ds_sum[half * ROWS : (half + 1) * ROWS]
+            )
 
 
 def self_bwd(qkv, datt, base):
@@ -275,22 +279,18 @@
                 both = all_ref[slot, item, :, pair(index)]
                 keys = kv_ref[place, :, pair(index)]
                 values = kv_ref[place, :, pair(index + HEADS // 2)]
-                total = None
-                scales = []
-                for half, mask in ((0, low), (1, high)):
-                    scores = dot_nt(both * mask, keys) + bias
-                    top = jnp.max(scores, axis=-1, keepdims=True)
-                    probs = jnp.exp(scores - top)
-                    amount = jnp.sum(probs, axis=-1, keepdims=True)
-                    part = dot(probs.astype(BF), values * mask)
-                    total = part if half == 0 else total + part
-                    scales.append(1.0 / amount)
+                scores = dot_nt(stacked(both, (low, high)), keys) + bias
+                top = jnp.max(scores, axis=-1, keepdims=True)
+                probs = jnp.exp(scores - top)
+                amount = jnp.sum(probs, axis=-1, keepdims=True)
+                total = joined_heads(dot(probs.astype(BF), values) * (1.0 / amount))
+                level = top + jnp.log(amount)
+                for half in range(2):
                     stats = jnp.where(
-                        lane == 2 * index + half, top + jnp.log(amount), stats
+                        lane == 2 * index + half, level[half * ROWS : (half + 1) * ROWS], stats
                     )
-                total = total * jnp.where(is_low, scales[0], scales[1])
                 out_o[slot, item, :, pair(index)] = total.astype(BF)
-            out_s[slot, item] = stats
+            out_s[slot, item] = stats.T[:8]
         if slot:
             copies.append(send(out_o.at[slot], in_o.at[slot], o_send.at[slot], o_recv.at[slot], slot))
             copies.append(send(out_s.at[slot], in_s.at[slot], s_send.at[slot], s_recv.at[slot], slot))
@@ -302,7 +302,10 @@
     for copy in copies:
         copy.wait()
     for item in range(items):
-        stats = [out_s[0, item]] + [in_s[slot, item] for slot in (1, 2, 3)]
+        stats = [
+            jnp.concatenate([part, jnp.zeros((STATS - 8, ROWS), F32)], axis=0).T
+            for part in [out_s[0, item]] + [in_s[slot, item] for slot in (1, 2, 3)]
+        ]
         top = jnp.maximum(jnp.maximum(stats[0], stats[1]), jnp.maximum(stats[2], stats[3]))
         shares = [jnp.exp(part - top) for part in stats]
         amount = shares[0] + shares[1] + shares[2] + shares[3]
@@ -322,7 +325,7 @@
     items = queries.shape[0]
     inner = HEADS * HEAD
     block = (4, items, ROWS, inner)
-    stat_block = (4, items, ROWS, STATS)
+    stat_block = (4, items, 8, ROWS)
     flops = 4 * items * HEADS * ROWS * SPAN * 128 * 4
     return pl.pallas_call(
         functools.partial(cross_fwd_kernel, items),
@@ -394,6 +397,7 @@
             place = owner * items + item
             bias = bias_ref[place]
             stats = stat_ref[item] if slot == 0 else all_s[slot, item]
+            stats = jnp.concatenate([stats, jnp.zeros((STATS - 16, ROWS), F32)], axis=0).T
             for index in range(HEADS // 2):
                 both = all_ref[slot, item, :, pair(index)]
                 if slot == 0:
@@ -402,21 +406,21 @@
                     upstream = all_b[slot, item, :, pair(index)]
                 keys = kv_ref[place, :, pair(index)]
                 values = kv_ref[place, :, pair(index + HEADS // 2)]
-                dq = dk = dv = None
-                for half, mask in ((0, low), (1, high)):
-                    head = 2 * index + half
-                    query = both * mask
-                    back = upstream * mask
-                    scores = dot_nt(query, keys) + bias
-                    probs = jnp.exp(scores - column(stats, head))
-                    dprobs = dot_nt(back, values)
-                    ds = (probs * (dprobs - column(stats, 8 + head))).astype(BF)
-                    q_part = dot(ds, keys * mask)
-                    k_part = dot_tn(ds, query)
-                    v_part = dot_tn(probs.astype(BF), back)
-                    dq = q_part if half == 0 else dq + q_part
-                    dk = k_part if half == 0 else dk + k_part
-                    dv = v_part if half == 0 else dv + v_part
+                query = stacked(both, (low, high))
+                back = stacked(upstream, (low, high))
+
+                def both_columns(start, index=index, stats=stats):
+                    return jnp.concatenate(
+                        [column(stats, start + 2 * index + half) for half in range(2)], axis=0
+                    )
+
+                scores = dot_nt(query, keys) + bias
+                probs = jnp.exp(scores - both_columns(0))
+                dprobs = dot_nt(back, values)
+                ds = (probs * (dprobs - both_columns(8))).astype(BF)
+                dq = joined_heads(dot(ds, keys))
+                dk = dot_tn(ds, query)
+                dv = dot_tn(probs.astype(BF), back)
                 out_q[slot, item, :, pair(index)] = dq.astype(BF)
                 dkv_ref[place, :, pair(index)] = dk.astype(BF)
                 dkv_ref[place, :, pair(index + HEADS // 2)] = dv.astype(BF)
@@ -451,7 +455,7 @@
         out_specs=(VMEM_SPEC,) * 2,
         scratch_shapes=[
             pltpu.VMEM(block, BF),
-            pltpu.VMEM((4, items, ROWS, STATS), F32),
+            pltpu.VMEM((4, items, 16, ROWS), F32),
             pltpu.VMEM(block, BF),
             pltpu.VMEM(block, BF),
             pltpu.SemaphoreType.DMA((3,)),
@@ -486,13 +490,14 @@
     h_send, h_recv, d_send, d_recv, y_send, y_recv, load_sem, up_sem, store_sem,
 ):
     tokens, model = h_ref.shape
+    last = 1 + items
     rows = tokens // items
     units = down_ref.shape[0]
     loads = [
         pltpu.make_async_copy(gate_up_hbm, gate_up_ref, load_sem.at[0]),
         pltpu.make_async_copy(down_hbm, down_ref, load_sem.at[1]),
         pltpu.make_async_copy(up0_ref, u_all.at[0], load_sem.at[2]),
-        pltpu.make_async_copy(up1_ref, u_all.at[1], load_sem.at[3]),
+        pltpu.make_async_copy(up1_ref, u_all.at[last], load_sem.at[3]),
     ]
     for copy in loads:
         copy.start()
@@ -502,17 +507,17 @@
         for place, ref in enumerate((up2_ref, up3_ref)):
             ups.append(
                 pltpu.make_async_copy(
-                    ref.at[mine], u_all.at[2 + item, pl.ds(place * rows, rows)],
+                    ref.at[mine], u_all.at[1 + item, pl.ds(place * rows, rows)],
                     up_sem.at[item, place],
                 )
             )
             ups[-1].start()
     greet("mem", (1, 2))
-    h_to_core = send(h_ref, h_all.at[1], h_send.at[0], h_recv.at[0], 1)
+    h_to_core = send(h_ref, h_all.at[last], h_send.at[0], h_recv.at[0], 1)
     h_to_far, h_relay, d_pass, d_far, y_pass = [], [], [], [], []
     first, second = pl.ds(0, rows), pl.ds(rows, rows)
     for item in range(items):
-        block, at = 2 + item, 1 + item
+        block = at = 1 + item
         h_to_far.append(
             send(h_ref.at[pl.ds(item * rows, rows)], h_all.at[block, first],
                  h_send.at[at], h_recv.at[at], 2)
@@ -533,11 +538,10 @@
             send(h_part.at[block, first], h_in.at[2, pl.ds(item * rows, rows)],
                  d_send.at[at + items], d_recv.at[at + items], 2)
         )
-    d_near = send(h_part.at[1], h_in.at[0], d_send.at[0], d_recv.at[0], 1)
-    y_near = send(y_part.at[1], y_in.at[0], y_send.at[0], y_recv.at[0], 1)
-    for copy in h_to_far:
-        copy.start()
+    d_near = send(h_part.at[last], h_in.at[0], d_send.at[0], d_recv.at[0], 1)
+    y_near = send(y_part.at[last], y_in.at[0], y_send.at[0], y_recv.at[0], 1)
     h_to_core.start()
+    h_to_far[0].start()
     h_all[0] = h_ref[...]
     for copy in loads:
         copy.wait()
@@ -547,36 +551,26 @@
     def give_back(item):
         mine = pl.ds(item * rows, rows)
         d_pass[item].wait_recv()
-        h_part[2 + item, first, :] = (
-            h_part[2 + item, first, :].astype(F32) + h_in[1, mine, :].astype(F32)
+        h_part[1 + item, first, :] = (
+            h_part[1 + item, first, :].astype(F32) + h_in[1, mine, :].astype(F32)
         ).astype(BF)
         d_far[item].start()
 
     def token_block(slot, carry):
-        @pl.when(slot == 1)
+        @pl.when(slot == last)
         def _():
             h_to_core.wait_recv()
 
-        @pl.when(slot == 2)
-        def _():
-            d_near.start()
-            y_near.start()
-
         for item in range(items):
+
+            @pl.when(slot == 1 + item)
+            def _(item=item):
+                h_relay[item].wait_recv()
 
             @pl.when(slot == 2 + item)
             def _(item=item):
-                if item:
-                    d_pass[item - 1].start()
-                    y_pass[item - 1].start()
-                h_relay[item].wait_recv()
-
-        for item in range(items):
-
-            @pl.when(slot == 1 + item)
-            def _(item=item):
-                h_to_far[item].wait_recv()
-                h_relay[item].start()
+                d_pass[item].start()
+                y_pass[item].start()
 
         def units_block(block, inside):
             pairs = pl.ds(pl.multiple_of(block * 256, 256), 256)
@@ -598,12 +592,23 @@
             return inside
 
         lax.fori_loop(0, units // 128, units_block, 0)
+        for item in range(1, items):
+
+            @pl.when(slot == item - 1)
+            def _(item=item):
+                h_to_far[item].start()
+
         for start, width in strips(model, 256):
             part = slice(start, start + width)
             h_part[slot, :, part] = dot_nt(two_back[slot], gate_up_ref[part, :]).astype(BF)
-        for item in range(items - 1):
-
-            @pl.when(slot == 3 + item)
+        for item in range(items):
+
+            @pl.when(slot == item)
+            def _(item=item):
+                h_to_far[item].wait_recv()
+                h_relay[item].start()
+
+            @pl.when(slot == 2 + item)
             def _(item=item):
                 give_back(item)
 
@@ -613,8 +618,8 @@
         return carry
 
     lax.fori_loop(0, 2 + items, token_block, 0)
-    d_pass[-1].start()
-    y_pass[-1].start()
+    d_near.start()
+    y_near.start()
     count = (2 + items) * tokens
     stores = []
 
@@ -638,8 +643,6 @@
             h_all[:, :, part].reshape(count, width), two_back[...].reshape(count, 2 * units)
         )
         store(value.astype(BF), gu_strip, grad_gu_hbm, start, width)
-        if start == 0:
-            give_back(items - 1)
     for start, width in strips(units, 256):
         part = slice(start, start + width)
         value = dot_tn(
@@ -650,7 +653,7 @@
         mine = pl.ds(item * rows, rows)
         y_pass[item].wait_recv()
         far_ref[mine, :] = (
-            y_part[2 + item, first, :].astype(F32) + y_in[1, mine, :].astype(F32)
+            y_part[1 + item, first, :].astype(F32) + y_in[1, mine, :].astype(F32)
         ).astype(BF)
     y_near.wait_recv()
     near_ref[...] = (y_part[0].astype(F32) + y_in[0].astype(F32)).astype(BF)
@@ -802,9 +805,9 @@
             far_members = list(enumerate(groups[index ^ 2]))
             near_members = list(enumerate(groups[index ^ 1]))
             last_members = list(enumerate(groups[index ^ 3]))
-            extra = [(2, far_members[0][1])] if index % 2 else []
-            far_sent = members[1:] if index % 2 else members
-            far_got = far_members[1:] if index % 2 else far_members
+            extra = []
+            far_sent = members
+            far_got = far_members
             for step, offset in steps[:4]:
                 for number, member in members + extra:
                     over_tgt(member, number, step, offset).start()
@@ -1359,14 +1362,14 @@
     dx, grad_norm_ffn = rms_back(y2, norm_ffn, h3_back)
     dy2 = upstream_low.astype(F32) + dx
     e2 = dy2.astype(BF)
-    grad_cross_o = dot_tn(catt, e2)
+    grad_cross_o = dot_tn(catt, e2).astype(BF)
     dcatt = dot_nt(e2, cross_o_w).astype(BF)
     delta = jnp.sum(
         (dcatt.astype(F32) * catt.astype(F32)).reshape(tokens, HEADS, HEAD), axis=-1
     ).reshape(items, ROWS, HEADS)
     stats = jnp.concatenate(
-        [lse[:, :, :8], delta, jnp.zeros((items, ROWS, STATS - 8 - HEADS), F32)], axis=-1
-    )
+        [lse[:, :, :8], delta, jnp.zeros((items, ROWS, 8 - HEADS), F32)], axis=-1
+    ).swapaxes(1, 2)
     dckv, dcq = cross_bwd(
         all_queries, dcatt.reshape(items, ROWS, inner), stats, ckv, bias
     )
@@ -1384,7 +1387,7 @@
     dx, grad_norm_cross = rms_back(y1, norm_cross, dot_nt(dcq, cross_q_w))
     dy1 = dy2 + dx
     e1 = dy1.astype(BF)
-    grad_self_o = dot_tn(att, e1)
+    grad_self_o = dot_tn(att, e1).astype(BF)
     datt = dot_nt(e1, self_o_w).astype(BF).reshape(items, ROWS, inner)
     dqkv, diag = self_bwd(qkv, datt, base)
     dqkv = dqkv.reshape(tokens, 3 * inner)

time: 501 us -> 491 us (0.980)
  Pallas kernels: 348 us -> 337 us
    pallas_call x1, Pallas kernels: 38.3 us -> 30 us  [cross_fwd(): pl.pallas_call(functools.partial(cross_fwd_kernel, items), out_shape=(jax...]
    pallas_call x1, Pallas kernels: 36 us -> 30.9 us  [cross_bwd(): pl.pallas_call(functools.partial(cross_bwd_kernel, items), out_shape=(jax...]
    unnamed x109 -> x107, local copies, waits for them, and re-layouts: 13 us -> 12.7 us
  transfers between devices with their start and end apart: 7 -> 7, of which waited for: 2 -> 2; matrix products, arithmetic and copies ran while one was open for 20% -> 21% of each run, Pallas kernels for 50% -> 49%
where the time goes in v4:
time: 491 us; the launch traced here: 487 us
  Pallas kernels  337 us (69%)
  matrix products  54.1 us (11%)
  local copies, waits for them, and re-layouts  47.6 us (10%)
  other arithmetic  20.8 us (4%)
  between operations  14.5 us (3%)
  waiting for transfers between devices  10.8 us (2%)
    pallas_call x1, Pallas kernels, reduce_weights(): pl.pallas_call(reduce_kernel, out_shape=tuple((jax.ShapeDtypeStruct(wide,...  102 us
    pallas_call x1, Pallas kernels, ffn(): pl.pallas_call(functools.partial(ffn_kernel, items), out_shape=(jax.Shape...  76.4 us
    pallas_call x1, Pallas kernels, gather_weights(): pl.pallas_call(gather_kernel, out_shape=shapes, in_specs=[ANY_SPEC] * 8,...  63.9 us
    pallas_call x1, Pallas kernels, cross_bwd(): pl.pallas_call(functools.partial(cross_bwd_kernel, items), out_shape=(jax...  30.9 us
    pallas_call x1, Pallas kernels, cross_fwd(): pl.pallas_call(functools.partial(cross_fwd_kernel, items), out_shape=(jax...  30 us
    dot_general x4, matrix products, dot_nt(): return lax.dot_general(left, right, NT, preferred_element_type=F32)  13.1 us
    unnamed x107, local copies, waits for them, and re-layouts  12.7 us
    dot_general x4, matrix products, dot_tn(): return lax.dot_general(left, right, TN, preferred_element_type=F32)  12.2 us
  transfers between devices with their start and end apart: 7, of which 2 were waited for; matrix products, arithmetic and copies ran while one was open for 21% of the time, Pallas kernels for 49%

profile of v4, /device:TPU:0, one launch (start us, length us, event | category | flops | bytes accessed | tf_op | source)
XLA Modules:
  0.0 487.2 jit_solution(11530658140273387059)
XLA Ops:
  8.6 3.0 pick_units.1
  14.1 63.9 %gather_weights.1 = (bf16[8,184,1152]{2,1,0:T(8,128)(2,1)}, bf16[8,184,768]{2,1,0:T(8,128)(2,1)}, bf16[8,184,384]{2,1,0:T(8,128)(2,1)}, bf16[8,48,1472]{2,1,0:T(8,128)(2,1)}, bf16[8,48,1472]{2,1,0:T(8,128)(2,1)}) custom-call(bf16[184,384]{1,0:T(8,128)(2,1)} %self_q.1, bf16[184,384]{1,0:T(8,128)(2,1)} %self_k.1, bf16[184,384]{1,0:T(8,128)(2,1)} %self_v.1, ...), custom_call_target="tpu_custom_call" | custom-call | bytes 157286400 | tf_op jit(solution)/shard_map/gather_weights/pallas_call | solution.py:862
  84.4 2.4 copy-done.42
  86.7 2.6 convolution_convert_fusion.4
  89.4 7.1 %convert_bitcast_fusion.kv_ref = bf16[8,256,768]{2,1,0:T(8,128)(2,1)} fusion(bf16[1472,768,1]{1,0,2:T(8,128)(2,1)S(1)} %bitcast.158, bf16[8,256,1472]{1,2,0:T(8,128)(2,1)S(1)} %bitcast.153), kind=kOutput, calls=%fused_computation.4 | convolution fusion | flops 4632084480 | bytes 11436032 | tf_op jit(solution)/shard_map/npd,dc->npc/dot_general | solution.py:1351
  97.8 4.3 self_fwd.1
  105.7 30.0 %cross_fwd.1 = (bf16[4,2,192,384]{3,2,1,0:T(8,128)(2,1)}, bf16[2,192,384]{2,1,0:T(8,128)(2,1)}, f32[2,192,128]{2,1,0:T(8,128)}) custom-call(bf16[2,192,384]{2,1,0:T(8,128)(2,1)} %bitcast.148, bf16[8,256,768]{2,1,0:T(8,128)(2,1)} %convert_bitcast_fusion.kv_ref, f32[8,1,256]{2,1,0:T(1,128)} %broadcast_in_dim.9.bias_ref), custom_call_target="tpu_custom_call" | custom-call | flops 1207959552 | bytes 8388608 | tf_op jit(solution)/shard_map/cross_fwd/pallas_call | solution.py:330
  141.4 2.5 copy.110.up2_ref
  143.9 2.5 copy.109.up1_ref
  148.4 5.6 %all-gather.3.cloned.1.call-done = bf16[3920,8,128]{2,1,0:T(8,128)(2,1)} async-done(((bf16[490,8,128]{2,1,0:T(8,128)(2,1)}), bf16[3920,8,128]{2,1,0:T(8,128)(2,1)}) %all-gather.3.cloned.1.call-update) | async-done | bytes 8028176 | tf_op jit(solution)/shard_map/all_gather | solution.py:1263
  154.0 5.2 %slice.44 = bf16[8,322,8,128]{3,2,1,0:T(8,128)(2,1)} slice(bf16[8,490,8,128]{3,2,1,0:T(8,128)(2,1)} %bitcast.119), slice={[0:8], [0:322], [0:8], [0:128]} | slice | bytes 10551296 | tf_op jit(solution)/shard_map/slice | solution.py:1265
  159.2 3.5 slice.45
  162.7 76.4 %feed_forward.1 = (f32[384,1472]{1,0:T(8,128)}, bf16[384,1472]{1,0:T(8,128)(2,1)}, bf16[384,1472]{1,0:T(8,128)(2,1)}, bf16[1472,1792]{1,0:T(8,128)(2,1)}, bf16[896,1472]{1,0:T(8,128)(2,1)}) custom-call(bf16[384,1472]{1,0:T(8,128)(2,1)} %multiply_convert_fusion.1.h_ref, bf16[384,1472]{1,0:T(8,128)(2,1)} %bitcast.118, bf16[384,1472]{1,0:T(8,128)(2,1)} %copy.109.up1_ref, ...), custom_call_target="tpu_custom_call" | custom-call | flops 36465278976 | bytes 33554432 | tf_op jit(solution)/shard_map/feed_forward/pallas_call | solution.py:678
  242.3 3.5 multiply_convert_fusion
  245.7 3.4 multiply_reduce_fusion
  253.8 30.9 %cross_bwd.1 = (bf16[8,256,768]{2,1,0:T(8,128)(2,1)}, bf16[2,192,384]{2,1,0:T(8,128)(2,1)}) custom-call(bf16[4,2,192,384]{3,2,1,0:T(8,128)(2,1)} %get-tuple-element.72.all_ref, bf16[2,192,384]{2,1,0:T(8,128)(2,1)} %bitcast.147, f32[2,16,192]{2,1,0:T(8,128)} %maximum_bitcast_fusion.stat_ref, bf16[8,256,768]{2,1,0:T(8,128)(2,1)} %convert_bitcast_fusion.kv_ref, ...), custom_call_target="tpu_custom_call" | custom-call | flops 3019898880 | bytes 12582912 | tf_op jit(solution)/shard_map/cross_bwd/pallas_call | solution.py:448
  284.7 2.7 multiply_reduce_fusion.1
  289.4 3.2 convolution_convert_fusion.5
  292.6 6.7 %self_bwd.1 = (bf16[2,192,1152]{2,1,0:T(8,128)(2,1)}, f32[8,256]{1,0:T(8,128)}) custom-call(bf16[2,192,1152]{2,1,0:T(8,128)(2,1)} %bitcast.146, bf16[2,192,384]{2,1,0:T(8,128)(2,1)} %bitcast.149, f32[8,256]{1,0:T(8,128)} %pad.21.base_ref), custom_call_target="tpu_custom_call" | custom-call | flops 754974720 | bytes 2064384 | tf_op jit(solution)/shard_map/self_bwd/pallas_call | solution.py:200
  300.3 2.8 convolution_convert_fusion.2
  303.1 2.3 copy.123
  305.4 2.7 convolution_convert_fusion.1
  310.2 5.7 %fusion.8 = (f32[1472]{0:T(1024)}, f32[384]{0:T(512)S(1)}, f32[384,1472]{1,0:T(8,128)S(1)}) fusion(f32[2,192,1472]{2,1,0:T(8,128)} %copy-done.7, f32[384]{0:T(512)S(1)} %copy-done.30, f32[1472]{0:T(1024)S(1)} %convert_element_type.108, bf16[384,1152]{1,0:T(8,128)(2,1)} %bitcast.160, bf16[1472,1152]{1,0:T(8,128)(2,1)} %bitcast.156), kind=kOutput, calls=%fused_computation.22 | convolution fusion | flops 1305720960 | bytes 8813056 | tf_op jit(solution)/shard_map/dot_general | solution.py:53
  315.9 2.5 fusion.6
  325.3 3.0 convolution_convert_fusion.3
  328.3 3.9 fusion
  332.1 6.7 %convolution_convert_fusion = bf16[8,256,1472]{1,2,0:T(8,128)(2,1)} fusion(bf16[8,256,768]{2,1,0:T(8,128)(2,1)S(1)} %copy-done.46, bf16[1472,768,1]{1,0,2:T(8,128)(2,1)S(1)} %bitcast.159), kind=kOutput, calls=%fused_computation.2 | convolution fusion | flops 4633526272 | bytes 11436032 | tf_op jit(solution)/shard_map/npc,dc->npd/dot_general | solution.py:1383
  338.9 6.0 %bitcast_convert_fusion = bf16[768,1472]{0,1:T(8,128)(2,1)} fusion(bf16[8,256,1472]{1,2,0:T(8,128)(2,1)S(1)} %bitcast.155, bf16[8,256,768]{2,1,0:T(8,128)(2,1)S(1)} %copy-done.46), kind=kOutput, calls=%fused_computation.3 | convolution fusion | flops 4631642112 | bytes 11436032 | tf_op jit(solution)/shard_map/npd,npc->dc/dot_general | solution.py:1382
  344.9 5.1 %collective-permute-done.3 = bf16[384,1472]{0,1:T(8,128)(2,1)} collective-permute-done((bf16[384,1472]{0,1:T(8,128)(2,1)}, bf16[384,1472]{0,1:T(8,128)(2,1)}, u32[]{:S(2)}, u32[]{:S(2)}) %collective-permute-start.3) | collective-permute-done | bytes 1130528 | tf_op jit(solution)/shard_map/ppermute | solution.py:1230
  356.0 102.3 %reduce_weights.1 = (bf16[184,384]{1,0:T(8,128)(2,1)}, bf16[184,384]{1,0:T(8,128)(2,1)}, bf16[184,384]{1,0:T(8,128)(2,1)}, bf16[184,384]{1,0:T(8,128)(2,1)}, bf1...) custom-call(bf16[8,184,1152]{2,1,0:T(8,128)(2,1)} %bitcast.133, ...), custom_call_target="tpu_custom_call" | custom-call | bytes 157286400 | tf_op jit(solution)/shard_map/reduce_weights/pallas_call | solution.py:1089
  460.5 12.1 %share_sums.1.down_parts_ref = bf16[4,112,1472]{2,1,0:T(8,128)(2,1)} custom-call(bf16[112,1472]{1,0:T(8,128)(2,1)} %reduce-scatter.3.cloned.1.call-done.src), custom_call_target="tpu_custom_call" | custom-call | bytes 31457280 | tf_op jit(solution)/shard_map/share_sums/pallas_call | solution.py:1215
  473.3 7.2 %place_units.1 = (f32[184,3584]{1,0:T(8,128)}, f32[184,3584]{1,0:T(8,128)}, f32[448,1472]{1,0:T(8,128)}, f32[184,384]{1,0:T(8,128)}, f32[184,384]{1,0:T(8,128)},...) custom-call(bf16[4,184,1792]{2,1,0:T(8,128)(2,1)} %get-tuple-element, ...), custom_call_target="tpu_custom_call" | custom-call | tf_op jit(solution)/shard_map/place_units/pallas_call | solution.py:1182
  (176 shorter events, 51.2 us)
Async XLA Ops:
  7.2 146.8 %all-gather.3.cloned.1.call-start = ((), (), s32[]{:S(2)}) async-start(), calls=%async_computation.4 | async-start | bytes 9031680 | tf_op jit(solution)/shard_map/all_gather | solution.py:1263
  8.6 5.2 %copy-start.25 = (bf16[2,189,1472]{2,0,1:T(2,128)(2,1)S(1)}, bf16[2,189,1472]{2,0,1:T(2,128)(2,1)}, u32[]{:S(2)}) copy-start(bf16[2,189,1472]{2,0,1:T(2,128)(2,1)} %param.25) | copy-start | bytes 3338500
  13.8 342.2 %reduce-scatter.5.cloned.1.call-start = ((), (), s32[]{:S(2)}) async-start(), calls=%async_computation.3 | async-start | bytes 5935104 | tf_op jit(solution)/shard_map/reduce_scatter | solution.py:1244
  14.0 65.8 %copy-start.13 = (bf16[2,189,1472]{2,0,1:T(2,128)(2,1)S(1)}, bf16[2,189,1472]{2,0,1:T(2,128)(2,1)}, u32[]{:S(2)}) copy-start(bf16[2,189,1472]{2,0,1:T(2,128)(2,1)} %param.21) | copy-start | bytes 3338500
  14.1 67.4 %copy-start.11 = (bf16[2,192,1472]{2,1,0:T(8,128)(2,1)}, bf16[2,192,1472]{2,1,0:T(8,128)(2,1)S(1)}, u32[]{:S(2)}) copy-start(bf16[2,192,1472]{2,1,0:T(8,128)(2,1)S(1)} %pad.20.clone) | copy-start | bytes 3391492
  79.4 56.3 %collective-permute-start.1 = (bf16[384,1472]{0,1:T(8,128)(2,1)}, bf16[384,1472]{0,1:T(8,128)(2,1)}, u32[]{:S(2)}, u32[]{:S(2)}) collective-permute-start(bf16[384,1472]{0,1:T(8,128)(2,1)} %copy.107), channel_id=1, source_target_pairs={{0,2},{1,3},{2,0},{3,1},{4,6},{5,7},{6,4},{7,5},{8,10},{9,11},{10,... | collective-permute-start | bytes 3391496 | tf_op jit(solution)/shard_map/ppermute | solution.py:1230
  79.4 64.5 %collective-permute-start = (bf16[384,1472]{0,1:T(8,128)(2,1)}, bf16[384,1472]{0,1:T(8,128)(2,1)}, u32[]{:S(2)}, u32[]{:S(2)}) collective-permute-start(bf16[384,1472]{0,1:T(8,128)(2,1)} %copy.107), channel_id=1, source_target_pairs={{0,1},{1,0},{2,3},{3,2},{4,5},{5,4},{6,7},{7,6},{8,9},{9,8},{10,11... | collective-permute-start | bytes 3391496 | tf_op jit(solution)/shard_map/ppermute | solution.py:1230
  83.8 18.3 %copy-start.7 = (f32[2,192,1472]{2,1,0:T(8,128)}, f32[2,192,1472]{2,1,0:T(8,128)S(1)}, u32[]{:S(2)}) copy-start(f32[2,192,1472]{2,1,0:T(8,128)S(1)} %copy.101) | copy-start | bytes 6782980
  84.1 5.3 %slice-start.1 = ((s8[6029312]{0:T(1024)(128)(4,1)}), s8[4194304]{0:T(1024)(128)(4,1)S(1)}, s32[]{:S(2)}) async-start(s8[6029312]{0:T(1024)(128)(4,1)} %bitcast.152), calls=%async_computation.6 | async-start | bytes 8388608
  89.4 7.2 %copy-start.35 = (f32[8,256]{1,0:T(8,128)S(1)}, f32[8,256]{1,0:T(8,128)}, u32[]{:S(2)}) copy-start(f32[8,256]{1,0:T(8,128)} %param.24) | copy-start | bytes 24580
  89.4 7.2 %copy-start.41 = (s32[8]{0:T(128)S(1)}, s32[8]{0:T(128)}, u32[]{:S(2)}) copy-start(s32[8]{0:T(128)} %param.23) | copy-start | bytes 100
  89.4 7.2 %copy-start.37 = (bf16[1472]{0:T(1024)(128)(2,1)S(1)}, bf16[1472]{0:T(1024)(128)(2,1)}, u32[]{:S(2)}) copy-start(bf16[1472]{0:T(1024)(128)(2,1)} %param.27) | copy-start | bytes 8836
  89.4 7.8 %copy-start.38 = (bf16[1472]{0:T(1024)(128)(2,1)S(1)}, bf16[1472]{0:T(1024)(128)(2,1)}, u32[]{:S(2)}) copy-start(bf16[1472]{0:T(1024)(128)(2,1)} %param.28) | copy-start | bytes 8836
  89.4 12.8 %copy-start.16 = (bf16[8,48,1472]{2,1,0:T(8,128)(2,1)S(1)}, bf16[8,48,1472]{2,1,0:T(8,128)(2,1)}, u32[]{:S(2)}) copy-start(bf16[8,48,1472]{2,1,0:T(8,128)(2,1)} %get-tuple-element.65) | copy-start | bytes 3391492
  104.1 31.6 %copy-start.31 = (f32[384]{0:T(512)}, f32[384]{0:T(512)S(1)}, u32[]{:S(2)}) copy-start(f32[384]{0:T(512)S(1)} %get-tuple-element.171) | copy-start | bytes 4612
  104.1 32.8 %copy-start.2 = (f32[384,1472]{1,0:T(8,128)}, f32[384,1472]{1,0:T(8,128)S(1)}, u32[]{:S(2)}) copy-start(f32[384,1472]{1,0:T(8,128)S(1)} %get-tuple-element.172) | copy-start | bytes 6782980
  105.7 31.2 %copy-start.18 = (bf16[8,48,1472]{2,1,0:T(8,128)(2,1)S(1)}, bf16[8,48,1472]{2,1,0:T(8,128)(2,1)}, u32[]{:S(2)}) copy-start(bf16[8,48,1472]{2,1,0:T(8,128)(2,1)} %get-tuple-element.69) | copy-start | bytes 3391492
  135.7 10.7 %collective-permute-start.2 = (bf16[384,1472]{0,1:T(8,128)(2,1)}, bf16[384,1472]{0,1:T(8,128)(2,1)S(1)}, u32[]{:S(2)}, u32[]{:S(2)}) collective-permute-start(bf16[384,1472]{0,1:T(8,128)(2,1)} %collective-permute-done.1), channel_id=1, source_target_pairs={{0,1},{1,0},{2,3},{3,2},{4,5},{5,4},{6,7},{7,6},{8,9},{9,8},{10,11... | collective-permute-start | bytes 3391496 | tf_op jit(solution)/shard_map/ppermute | solution.py:1230
  239.2 6.5 %copy-start.5 = (f32[384,1472]{1,0:T(8,128)S(1)}, f32[384,1472]{1,0:T(8,128)}, u32[]{:S(2)}) copy-start(f32[384,1472]{1,0:T(8,128)} %copy-done.4) | copy-start | bytes 6782980
  239.2 219.1 %reduce-scatter.3.cloned.1.call-start = ((), (), s32[]{:S(2)}) async-start(), calls=%async_computation.2 | async-start | bytes 3096576 | tf_op jit(solution)/shard_map/reduce_scatter | solution.py:1244
  253.8 30.9 %copy-start.3 = (f32[384,1472]{1,0:T(8,128)S(1)}, f32[384,1472]{1,0:T(8,128)}, u32[]{:S(2)}) copy-start(f32[384,1472]{1,0:T(8,128)} %copy-done.2) | copy-start | bytes 6782980
  253.8 30.9 %copy-start.21 = (bf16[8,184,384]{2,1,0:T(8,128)(2,1)S(1)}, bf16[8,184,384]{2,1,0:T(8,128)(2,1)}, u32[]{:S(2)}) copy-start(bf16[8,184,384]{2,1,0:T(8,128)(2,1)} %get-tuple-element.66) | copy-start | bytes 3391492
  289.4 9.9 %copy-start.28 = (f32[32,256]{1,0:T(8,128)S(1)}, f32[32,256]{1,0:T(8,128)}, u32[]{:S(2)}) copy-start(f32[32,256]{1,0:T(8,128)} %constant.32.clone) | copy-start | bytes 98308
  305.4 4.8 copy-start.30
  310.2 5.7 %copy-start.8 = (f32[2,192,1472]{2,1,0:T(8,128)S(1)}, f32[2,192,1472]{2,1,0:T(8,128)}, u32[]{:S(2)}) copy-start(f32[2,192,1472]{2,1,0:T(8,128)} %copy-done.7) | copy-start | bytes 6782980
  322.0 6.3 %copy-start.24 = (bf16[2,192,1472]{2,0,1:T(2,128)(2,1)S(1)}, bf16[2,192,1472]{2,0,1:T(2,128)(2,1)}, u32[]{:S(2)}) copy-start(bf16[2,192,1472]{2,0,1:T(2,128)(2,1)} %multiply_convert_fusion) | copy-start | bytes 3391492
  322.0 28.0 %collective-permute-start.3 = (bf16[384,1472]{0,1:T(8,128)(2,1)}, bf16[384,1472]{0,1:T(8,128)(2,1)}, u32[]{:S(2)}, u32[]{:S(2)}) collective-permute-start(bf16[384,1472]{0,1:T(8,128)(2,1)} %copy.115), channel_id=1, source_target_pairs={{0,2},{1,3},{2,0},{3,1},{4,6},{5,7},{6,4},{7,5},{8,10},{9,11},{10,... | collective-permute-start | bytes 3391496 | tf_op jit(solution)/shard_map/ppermute | solution.py:1230
  323.9 4.4 copy-start.45
  328.3 10.6 %slice-start.3 = ((s8[6029312]{0:T(1024)(128)(4,1)}), s8[4194304]{0:T(1024)(128)(4,1)S(1)}, s32[]{:S(2)}) async-start(s8[6029312]{0:T(1024)(128)(4,1)} %bitcast.154), calls=%async_computation.8 | async-start | bytes 8388608
  332.1 6.7 %slice-start.4 = ((s8[6029312]{0:T(1024)(128)(4,1)}), s8[1835008]{0:T(1024)(128)(4,1)S(1)}, s32[]{:S(2)}) async-start(s8[6029312]{0:T(1024)(128)(4,1)} %bitcast.154), calls=%async_computation.9 | async-start | bytes 3670016
  338.9 13.1 %copy-start.6 = (f32[384,1472]{1,0:T(8,128)S(1)}, f32[384,1472]{1,0:T(8,128)}, u32[]{:S(2)}) copy-start(f32[384,1472]{1,0:T(8,128)} %copy-done.4) | copy-start | bytes 6782980
  473.3 7.2 %copy-start.1 = (bf16[448,1472]{1,0:T(8,128)(2,1)S(1)}, bf16[448,1472]{1,0:T(8,128)(2,1)}, u32[]{:S(2)}) copy-start(bf16[448,1472]{1,0:T(8,128)(2,1)} %param.40) | copy-start | bytes 3956740
  (27 other events, 58.4 us)
Sparse Core Ops, SparseCore 0:
  13.9 140.0 all-gather.2
  239.3 103.6 reduce-scatter.4
  347.0 92.7 reduce-scatter.2

commit v5 on v4

--- a/solution.py
+++ b/solution.py
@@ -991,8 +991,6 @@
                         + member[2][0][1, step, number].astype(F32)
                     ).astype(BF)
                     to_far(member, number, step).start()
-            share_far.start()
-            share_near.start()
             for move in small_mem:
                 move.wait_recv()
             small_in[4 + y_place] = (small_in[0] + small_in[1]) + (small_in[2] + small_in[3])
@@ -1019,6 +1017,8 @@
             for_side(1)
             for_side(2)
             for_side(3)
+            share_far.start()
+            share_near.start()
             for turn in range(4):
                 for number, member in mine:
                     total = mem_sum(member, number, 2 * turn + 1)

time: 491 us -> 491 us (level)
  no operation moved by 1% of the time
where the time goes in v5:
time: 491 us; the launch traced here: 487 us
  Pallas kernels  337 us (69%)
  matrix products  54.1 us (11%)
  local copies, waits for them, and re-layouts  47.6 us (10%)
  other arithmetic  20.8 us (4%)
  between operations  14.5 us (3%)
  waiting for transfers between devices  10.8 us (2%)
    pallas_call x1, Pallas kernels, reduce_weights(): pl.pallas_call(reduce_kernel, out_shape=tuple((jax.ShapeDtypeStruct(wide,...  102 us
    pallas_call x1, Pallas kernels, ffn(): pl.pallas_call(functools.partial(ffn_kernel, items), out_shape=(jax.Shape...  76.4 us
    pallas_call x1, Pallas kernels, gather_weights(): pl.pallas_call(gather_kernel, out_shape=shapes, in_specs=[ANY_SPEC] * 8,...  63.9 us
    pallas_call x1, Pallas kernels, cross_bwd(): pl.pallas_call(functools.partial(cross_bwd_kernel, items), out_shape=(jax...  30.9 us
    pallas_call x1, Pallas kernels, cross_fwd(): pl.pallas_call(functools.partial(cross_fwd_kernel, items), out_shape=(jax...  30 us
    dot_general x4, matrix products, dot_nt(): return lax.dot_general(left, right, NT, preferred_element_type=F32)  13.1 us
    unnamed x107, local copies, waits for them, and re-layouts  12.7 us
    dot_general x4, matrix products, dot_tn(): return lax.dot_general(left, right, TN, preferred_element_type=F32)  12.2 us
  transfers between devices with their start and end apart: 7, of which 2 were waited for; matrix products, arithmetic and copies ran while one was open for 21% of the time, Pallas kernels for 49%

profile of v5, /device:TPU:0, one launch (start us, length us, event | category | flops | bytes accessed | tf_op | source)
XLA Modules:
  0.0 487.2 jit_solution(14569958038948210002)
XLA Ops:
  8.6 3.0 pick_units.1
  14.1 63.9 %gather_weights.1 = (bf16[8,184,1152]{2,1,0:T(8,128)(2,1)}, bf16[8,184,768]{2,1,0:T(8,128)(2,1)}, bf16[8,184,384]{2,1,0:T(8,128)(2,1)}, bf16[8,48,1472]{2,1,0:T(8,128)(2,1)}, bf16[8,48,1472]{2,1,0:T(8,128)(2,1)}) custom-call(bf16[184,384]{1,0:T(8,128)(2,1)} %self_q.1, bf16[184,384]{1,0:T(8,128)(2,1)} %self_k.1, bf16[184,384]{1,0:T(8,128)(2,1)} %self_v.1, ...), custom_call_target="tpu_custom_call" | custom-call | bytes 157286400 | tf_op jit(solution)/shard_map/gather_weights/pallas_call | solution.py:862
  84.4 2.4 copy-done.42
  86.7 2.6 convolution_convert_fusion.4
  89.4 7.1 %convert_bitcast_fusion.kv_ref = bf16[8,256,768]{2,1,0:T(8,128)(2,1)} fusion(bf16[1472,768,1]{1,0,2:T(8,128)(2,1)S(1)} %bitcast.158, bf16[8,256,1472]{1,2,0:T(8,128)(2,1)S(1)} %bitcast.153), kind=kOutput, calls=%fused_computation.4 | convolution fusion | flops 4632084480 | bytes 11436032 | tf_op jit(solution)/shard_map/npd,dc->npc/dot_general | solution.py:1351
  97.8 4.3 self_fwd.1
  105.7 30.0 %cross_fwd.1 = (bf16[4,2,192,384]{3,2,1,0:T(8,128)(2,1)}, bf16[2,192,384]{2,1,0:T(8,128)(2,1)}, f32[2,192,128]{2,1,0:T(8,128)}) custom-call(bf16[2,192,384]{2,1,0:T(8,128)(2,1)} %bitcast.148, bf16[8,256,768]{2,1,0:T(8,128)(2,1)} %convert_bitcast_fusion.kv_ref, f32[8,1,256]{2,1,0:T(1,128)} %broadcast_in_dim.9.bias_ref), custom_call_target="tpu_custom_call" | custom-call | flops 1207959552 | bytes 8388608 | tf_op jit(solution)/shard_map/cross_fwd/pallas_call | solution.py:330
  141.4 2.5 copy.110.up2_ref
  143.9 2.5 copy.109.up1_ref
  148.4 5.6 %all-gather.3.cloned.1.call-done = bf16[3920,8,128]{2,1,0:T(8,128)(2,1)} async-done(((bf16[490,8,128]{2,1,0:T(8,128)(2,1)}), bf16[3920,8,128]{2,1,0:T(8,128)(2,1)}) %all-gather.3.cloned.1.call-update) | async-done | bytes 8028176 | tf_op jit(solution)/shard_map/all_gather | solution.py:1263
  154.0 5.2 %slice.44 = bf16[8,322,8,128]{3,2,1,0:T(8,128)(2,1)} slice(bf16[8,490,8,128]{3,2,1,0:T(8,128)(2,1)} %bitcast.119), slice={[0:8], [0:322], [0:8], [0:128]} | slice | bytes 10551296 | tf_op jit(solution)/shard_map/slice | solution.py:1265
  159.2 3.5 slice.45
  162.7 76.4 %feed_forward.1 = (f32[384,1472]{1,0:T(8,128)}, bf16[384,1472]{1,0:T(8,128)(2,1)}, bf16[384,1472]{1,0:T(8,128)(2,1)}, bf16[1472,1792]{1,0:T(8,128)(2,1)}, bf16[896,1472]{1,0:T(8,128)(2,1)}) custom-call(bf16[384,1472]{1,0:T(8,128)(2,1)} %multiply_convert_fusion.1.h_ref, bf16[384,1472]{1,0:T(8,128)(2,1)} %bitcast.118, bf16[384,1472]{1,0:T(8,128)(2,1)} %copy.109.up1_ref, ...), custom_call_target="tpu_custom_call" | custom-call | flops 36465278976 | bytes 33554432 | tf_op jit(solution)/shard_map/feed_forward/pallas_call | solution.py:678
  242.3 3.5 multiply_convert_fusion
  245.7 3.4 multiply_reduce_fusion
  253.8 30.9 %cross_bwd.1 = (bf16[8,256,768]{2,1,0:T(8,128)(2,1)}, bf16[2,192,384]{2,1,0:T(8,128)(2,1)}) custom-call(bf16[4,2,192,384]{3,2,1,0:T(8,128)(2,1)} %get-tuple-element.72.all_ref, bf16[2,192,384]{2,1,0:T(8,128)(2,1)} %bitcast.147, f32[2,16,192]{2,1,0:T(8,128)} %maximum_bitcast_fusion.stat_ref, bf16[8,256,768]{2,1,0:T(8,128)(2,1)} %convert_bitcast_fusion.kv_ref, ...), custom_call_target="tpu_custom_call" | custom-call | flops 3019898880 | bytes 12582912 | tf_op jit(solution)/shard_map/cross_bwd/pallas_call | solution.py:448
  284.7 2.7 multiply_reduce_fusion.1
  289.4 3.2 convolution_convert_fusion.5
  292.6 6.7 %self_bwd.1 = (bf16[2,192,1152]{2,1,0:T(8,128)(2,1)}, f32[8,256]{1,0:T(8,128)}) custom-call(bf16[2,192,1152]{2,1,0:T(8,128)(2,1)} %bitcast.146, bf16[2,192,384]{2,1,0:T(8,128)(2,1)} %bitcast.149, f32[8,256]{1,0:T(8,128)} %pad.21.base_ref), custom_call_target="tpu_custom_call" | custom-call | flops 754974720 | bytes 2064384 | tf_op jit(solution)/shard_map/self_bwd/pallas_call | solution.py:200
  300.3 2.8 convolution_convert_fusion.2
  303.1 2.3 copy.123
  305.4 2.7 convolution_convert_fusion.1
  310.2 5.7 %fusion.8 = (f32[1472]{0:T(1024)}, f32[384]{0:T(512)S(1)}, f32[384,1472]{1,0:T(8,128)S(1)}) fusion(f32[2,192,1472]{2,1,0:T(8,128)} %copy-done.7, f32[384]{0:T(512)S(1)} %copy-done.30, f32[1472]{0:T(1024)S(1)} %convert_element_type.108, bf16[384,1152]{1,0:T(8,128)(2,1)} %bitcast.160, bf16[1472,1152]{1,0:T(8,128)(2,1)} %bitcast.156), kind=kOutput, calls=%fused_computation.22 | convolution fusion | flops 1305720960 | bytes 8813056 | tf_op jit(solution)/shard_map/dot_general | solution.py:53
  315.9 2.5 fusion.6
  325.3 3.0 convolution_convert_fusion.3
  328.3 3.9 fusion
  332.1 6.7 %convolution_convert_fusion = bf16[8,256,1472]{1,2,0:T(8,128)(2,1)} fusion(bf16[8,256,768]{2,1,0:T(8,128)(2,1)S(1)} %copy-done.46, bf16[1472,768,1]{1,0,2:T(8,128)(2,1)S(1)} %bitcast.159), kind=kOutput, calls=%fused_computation.2 | convolution fusion | flops 4633526272 | bytes 11436032 | tf_op jit(solution)/shard_map/npc,dc->npd/dot_general | solution.py:1383
  338.9 6.0 %bitcast_convert_fusion = bf16[768,1472]{0,1:T(8,128)(2,1)} fusion(bf16[8,256,1472]{1,2,0:T(8,128)(2,1)S(1)} %bitcast.155, bf16[8,256,768]{2,1,0:T(8,128)(2,1)S(1)} %copy-done.46), kind=kOutput, calls=%fused_computation.3 | convolution fusion | flops 4631642112 | bytes 11436032 | tf_op jit(solution)/shard_map/npd,npc->dc/dot_general | solution.py:1382
  344.9 5.1 %collective-permute-done.3 = bf16[384,1472]{0,1:T(8,128)(2,1)} collective-permute-done((bf16[384,1472]{0,1:T(8,128)(2,1)}, bf16[384,1472]{0,1:T(8,128)(2,1)}, u32[]{:S(2)}, u32[]{:S(2)}) %collective-permute-start.3) | collective-permute-done | bytes 1130528 | tf_op jit(solution)/shard_map/ppermute | solution.py:1230
  356.0 102.3 %reduce_weights.1 = (bf16[184,384]{1,0:T(8,128)(2,1)}, bf16[184,384]{1,0:T(8,128)(2,1)}, bf16[184,384]{1,0:T(8,128)(2,1)}, bf16[184,384]{1,0:T(8,128)(2,1)}, bf1...) custom-call(bf16[8,184,1152]{2,1,0:T(8,128)(2,1)} %bitcast.133, ...), custom_call_target="tpu_custom_call" | custom-call | bytes 157286400 | tf_op jit(solution)/shard_map/reduce_weights/pallas_call | solution.py:1089
  460.5 12.1 %share_sums.1.down_parts_ref = bf16[4,112,1472]{2,1,0:T(8,128)(2,1)} custom-call(bf16[112,1472]{1,0:T(8,128)(2,1)} %reduce-scatter.3.cloned.1.call-done.src), custom_call_target="tpu_custom_call" | custom-call | bytes 31457280 | tf_op jit(solution)/shard_map/share_sums/pallas_call | solution.py:1215
  473.3 7.2 %place_units.1 = (f32[184,3584]{1,0:T(8,128)}, f32[184,3584]{1,0:T(8,128)}, f32[448,1472]{1,0:T(8,128)}, f32[184,384]{1,0:T(8,128)}, f32[184,384]{1,0:T(8,128)},...) custom-call(bf16[4,184,1792]{2,1,0:T(8,128)(2,1)} %get-tuple-element, ...), custom_call_target="tpu_custom_call" | custom-call | tf_op jit(solution)/shard_map/place_units/pallas_call | solution.py:1182
  (176 shorter events, 51.2 us)
Async XLA Ops:
  7.2 146.8 %all-gather.3.cloned.1.call-start = ((), (), s32[]{:S(2)}) async-start(), calls=%async_computation.4 | async-start | bytes 9031680 | tf_op jit(solution)/shard_map/all_gather | solution.py:1263
  8.6 5.2 %copy-start.25 = (bf16[2,189,1472]{2,0,1:T(2,128)(2,1)S(1)}, bf16[2,189,1472]{2,0,1:T(2,128)(2,1)}, u32[]{:S(2)}) copy-start(bf16[2,189,1472]{2,0,1:T(2,128)(2,1)} %param.25) | copy-start | bytes 3338500
  13.8 342.2 %reduce-scatter.5.cloned.1.call-start = ((), (), s32[]{:S(2)}) async-start(), calls=%async_computation.3 | async-start | bytes 5935104 | tf_op jit(solution)/shard_map/reduce_scatter | solution.py:1244
  14.0 65.8 %copy-start.13 = (bf16[2,189,1472]{2,0,1:T(2,128)(2,1)S(1)}, bf16[2,189,1472]{2,0,1:T(2,128)(2,1)}, u32[]{:S(2)}) copy-start(bf16[2,189,1472]{2,0,1:T(2,128)(2,1)} %param.21) | copy-start | bytes 3338500
  14.1 67.4 %copy-start.11 = (bf16[2,192,1472]{2,1,0:T(8,128)(2,1)}, bf16[2,192,1472]{2,1,0:T(8,128)(2,1)S(1)}, u32[]{:S(2)}) copy-start(bf16[2,192,1472]{2,1,0:T(8,128)(2,1)S(1)} %pad.20.clone) | copy-start | bytes 3391492
  79.4 56.3 %collective-permute-start.1 = (bf16[384,1472]{0,1:T(8,128)(2,1)}, bf16[384,1472]{0,1:T(8,128)(2,1)}, u32[]{:S(2)}, u32[]{:S(2)}) collective-permute-start(bf16[384,1472]{0,1:T(8,128)(2,1)} %copy.107), channel_id=1, source_target_pairs={{0,2},{1,3},{2,0},{3,1},{4,6},{5,7},{6,4},{7,5},{8,10},{9,11},{10,... | collective-permute-start | bytes 3391496 | tf_op jit(solution)/shard_map/ppermute | solution.py:1230
  79.4 64.5 %collective-permute-start = (bf16[384,1472]{0,1:T(8,128)(2,1)}, bf16[384,1472]{0,1:T(8,128)(2,1)}, u32[]{:S(2)}, u32[]{:S(2)}) collective-permute-start(bf16[384,1472]{0,1:T(8,128)(2,1)} %copy.107), channel_id=1, source_target_pairs={{0,1},{1,0},{2,3},{3,2},{4,5},{5,4},{6,7},{7,6},{8,9},{9,8},{10,11... | collective-permute-start | bytes 3391496 | tf_op jit(solution)/shard_map/ppermute | solution.py:1230
  83.8 18.3 %copy-start.7 = (f32[2,192,1472]{2,1,0:T(8,128)}, f32[2,192,1472]{2,1,0:T(8,128)S(1)}, u32[]{:S(2)}) copy-start(f32[2,192,1472]{2,1,0:T(8,128)S(1)} %copy.101) | copy-start | bytes 6782980
  84.1 5.3 %slice-start.1 = ((s8[6029312]{0:T(1024)(128)(4,1)}), s8[4194304]{0:T(1024)(128)(4,1)S(1)}, s32[]{:S(2)}) async-start(s8[6029312]{0:T(1024)(128)(4,1)} %bitcast.152), calls=%async_computation.6 | async-start | bytes 8388608
  89.4 7.2 %copy-start.35 = (f32[8,256]{1,0:T(8,128)S(1)}, f32[8,256]{1,0:T(8,128)}, u32[]{:S(2)}) copy-start(f32[8,256]{1,0:T(8,128)} %param.24) | copy-start | bytes 24580
  89.4 7.2 %copy-start.41 = (s32[8]{0:T(128)S(1)}, s32[8]{0:T(128)}, u32[]{:S(2)}) copy-start(s32[8]{0:T(128)} %param.23) | copy-start | bytes 100
  89.4 7.2 %copy-start.37 = (bf16[1472]{0:T(1024)(128)(2,1)S(1)}, bf16[1472]{0:T(1024)(128)(2,1)}, u32[]{:S(2)}) copy-start(bf16[1472]{0:T(1024)(128)(2,1)} %param.27) | copy-start | bytes 8836
  89.4 7.8 %copy-start.38 = (bf16[1472]{0:T(1024)(128)(2,1)S(1)}, bf16[1472]{0:T(1024)(128)(2,1)}, u32[]{:S(2)}) copy-start(bf16[1472]{0:T(1024)(128)(2,1)} %param.28) | copy-start | bytes 8836
  89.4 12.8 %copy-start.16 = (bf16[8,48,1472]{2,1,0:T(8,128)(2,1)S(1)}, bf16[8,48,1472]{2,1,0:T(8,128)(2,1)}, u32[]{:S(2)}) copy-start(bf16[8,48,1472]{2,1,0:T(8,128)(2,1)} %get-tuple-element.65) | copy-start | bytes 3391492
  104.1 31.6 %copy-start.31 = (f32[384]{0:T(512)}, f32[384]{0:T(512)S(1)}, u32[]{:S(2)}) copy-start(f32[384]{0:T(512)S(1)} %get-tuple-element.171) | copy-start | bytes 4612
  104.1 32.8 %copy-start.2 = (f32[384,1472]{1,0:T(8,128)}, f32[384,1472]{1,0:T(8,128)S(1)}, u32[]{:S(2)}) copy-start(f32[384,1472]{1,0:T(8,128)S(1)} %get-tuple-element.172) | copy-start | bytes 6782980
  105.7 31.2 %copy-start.18 = (bf16[8,48,1472]{2,1,0:T(8,128)(2,1)S(1)}, bf16[8,48,1472]{2,1,0:T(8,128)(2,1)}, u32[]{:S(2)}) copy-start(bf16[8,48,1472]{2,1,0:T(8,128)(2,1)} %get-tuple-element.69) | copy-start | bytes 3391492
  135.7 10.7 %collective-permute-start.2 = (bf16[384,1472]{0,1:T(8,128)(2,1)}, bf16[384,1472]{0,1:T(8,128)(2,1)S(1)}, u32[]{:S(2)}, u32[]{:S(2)}) collective-permute-start(bf16[384,1472]{0,1:T(8,128)(2,1)} %collective-permute-done.1), channel_id=1, source_target_pairs={{0,1},{1,0},{2,3},{3,2},{4,5},{5,4},{6,7},{7,6},{8,9},{9,8},{10,11... | collective-permute-start | bytes 3391496 | tf_op jit(solution)/shard_map/ppermute | solution.py:1230
  239.2 6.5 %copy-start.5 = (f32[384,1472]{1,0:T(8,128)S(1)}, f32[384,1472]{1,0:T(8,128)}, u32[]{:S(2)}) copy-start(f32[384,1472]{1,0:T(8,128)} %copy-done.4) | copy-start | bytes 6782980
  239.2 219.1 %reduce-scatter.3.cloned.1.call-start = ((), (), s32[]{:S(2)}) async-start(), calls=%async_computation.2 | async-start | bytes 3096576 | tf_op jit(solution)/shard_map/reduce_scatter | solution.py:1244
  253.8 30.9 %copy-start.3 = (f32[384,1472]{1,0:T(8,128)S(1)}, f32[384,1472]{1,0:T(8,128)}, u32[]{:S(2)}) copy-start(f32[384,1472]{1,0:T(8,128)} %copy-done.2) | copy-start | bytes 6782980
  253.8 30.9 %copy-start.21 = (bf16[8,184,384]{2,1,0:T(8,128)(2,1)S(1)}, bf16[8,184,384]{2,1,0:T(8,128)(2,1)}, u32[]{:S(2)}) copy-start(bf16[8,184,384]{2,1,0:T(8,128)(2,1)} %get-tuple-element.66) | copy-start | bytes 3391492
  289.4 9.9 %copy-start.28 = (f32[32,256]{1,0:T(8,128)S(1)}, f32[32,256]{1,0:T(8,128)}, u32[]{:S(2)}) copy-start(f32[32,256]{1,0:T(8,128)} %constant.32.clone) | copy-start | bytes 98308
  305.4 4.8 copy-start.30
  310.2 5.7 %copy-start.8 = (f32[2,192,1472]{2,1,0:T(8,128)S(1)}, f32[2,192,1472]{2,1,0:T(8,128)}, u32[]{:S(2)}) copy-start(f32[2,192,1472]{2,1,0:T(8,128)} %copy-done.7) | copy-start | bytes 6782980
  322.0 6.3 %copy-start.24 = (bf16[2,192,1472]{2,0,1:T(2,128)(2,1)S(1)}, bf16[2,192,1472]{2,0,1:T(2,128)(2,1)}, u32[]{:S(2)}) copy-start(bf16[2,192,1472]{2,0,1:T(2,128)(2,1)} %multiply_convert_fusion) | copy-start | bytes 3391492
  322.0 28.0 %collective-permute-start.3 = (bf16[384,1472]{0,1:T(8,128)(2,1)}, bf16[384,1472]{0,1:T(8,128)(2,1)}, u32[]{:S(2)}, u32[]{:S(2)}) collective-permute-start(bf16[384,1472]{0,1:T(8,128)(2,1)} %copy.115), channel_id=1, source_target_pairs={{0,2},{1,3},{2,0},{3,1},{4,6},{5,7},{6,4},{7,5},{8,10},{9,11},{10,... | collective-permute-start | bytes 3391496 | tf_op jit(solution)/shard_map/ppermute | solution.py:1230
  323.9 4.4 copy-start.45
  328.3 10.6 %slice-start.3 = ((s8[6029312]{0:T(1024)(128)(4,1)}), s8[4194304]{0:T(1024)(128)(4,1)S(1)}, s32[]{:S(2)}) async-start(s8[6029312]{0:T(1024)(128)(4,1)} %bitcast.154), calls=%async_computation.8 | async-start | bytes 8388608
  332.1 6.7 %slice-start.4 = ((s8[6029312]{0:T(1024)(128)(4,1)}), s8[1835008]{0:T(1024)(128)(4,1)S(1)}, s32[]{:S(2)}) async-start(s8[6029312]{0:T(1024)(128)(4,1)} %bitcast.154), calls=%async_computation.9 | async-start | bytes 3670016
  338.9 13.1 %copy-start.6 = (f32[384,1472]{1,0:T(8,128)S(1)}, f32[384,1472]{1,0:T(8,128)}, u32[]{:S(2)}) copy-start(f32[384,1472]{1,0:T(8,128)} %copy-done.4) | copy-start | bytes 6782980
  473.3 7.2 %copy-start.1 = (bf16[448,1472]{1,0:T(8,128)(2,1)S(1)}, bf16[448,1472]{1,0:T(8,128)(2,1)}, u32[]{:S(2)}) copy-start(bf16[448,1472]{1,0:T(8,128)(2,1)} %param.40) | copy-start | bytes 3956740
  (27 other events, 58.4 us)
Sparse Core Ops, SparseCore 0:
  13.9 140.0 all-gather.2
  239.3 103.6 reduce-scatter.4
  347.0 92.7 reduce-scatter.2
